TPU v7x, 256 devices: a whole 4x4x8 slice. The times are simulated.
256 devices in a mesh: seq: 32 (over x, z), head: 8 (over y, core).
Axes of the slice: x: 4, y: 4, z: 8, core: 2. Of those that a mesh axis runs over, the one named last changes fastest.
Arguments:
- values: bfloat16 [24, 64, 131072], P('head', None, 'seq'), may hold values from -6 to 6
- b_rows: bfloat16 [128, 131072], P(None, ('seq', 'head')), may hold values from -0.59765625 to 0.59765625
- c_rows: bfloat16 [128, 131072], P(None, ('seq', 'head')), may hold values from -0.59765625 to 0.59765625
- log_decay: float32 [24, 131072], P('head', 'seq'), may hold values from -0.6 to 0
- level_weight: float32 [12, 24, 131072], P(None, 'head', 'seq'), may hold values from 0 to 2
Outputs:
- layer_out: bfloat16 [24, 64, 131072], P('head', None, 'seq')
All inputs are finite; a program needn't handle non-finite values.
Results may differ from a plain program's by a relative error of at most 0.0034.
Values may be sent and summed in bfloat16 or wider, within the bound.
No kernel may reach another device: no remote copies, remote signals or barrier semaphores. Data moves between devices by JAX's collectives and lax.ppermute only.
A program may use at most 128 MiB of HBM per device.

v0:
```python
import jax
import jax.numpy as jnp
from jax import lax
from jax.sharding import PartitionSpec as P

STRETCH = 64


def on_device(values, b_rows, c_rows, log_decay, level_weight):
    b_all, c_all = (
        lax.all_gather(b_rows, "head", axis=1, tiled=True),
        lax.all_gather(c_rows, "head", axis=1, tiled=True),
    )
    head_count, head_width, row_count = values.shape
    state_size = b_all.shape[0]
    stretch_count = row_count // STRETCH
    local_bits = stretch_count.bit_length() - 1
    val_blk = values.reshape(head_count, head_width, stretch_count, STRETCH)
    b_blk = b_all.reshape(state_size, stretch_count, STRETCH)
    c_blk = c_all.reshape(state_size, stretch_count, STRETCH)
    cum_log = jnp.cumsum(log_decay.reshape(head_count, stretch_count, STRETCH), axis=2)
    stretch_tot = cum_log[:, :, -1]
    scores = jnp.einsum("nkt,nks->kts", c_blk, b_blk, preferred_element_type=jnp.float32)
    causal = jnp.arange(STRETCH)[:, None] >= jnp.arange(STRETCH)[None, :]
    diff_log = cum_log[:, :, :, None] - cum_log[:, :, None, :]
    decay = jnp.exp(jnp.where(causal[None, None], diff_log, -jnp.inf))
    weight_zero = level_weight[0].reshape(head_count, stretch_count, STRETCH)
    mix = (weight_zero[..., None] * decay * scores[None]).astype(jnp.bfloat16)
    result = jnp.einsum("hkts,hpks->hpkt", mix, val_blk, preferred_element_type=jnp.float32)
    keys_decayed = (jnp.exp(stretch_tot[:, :, None] - cum_log)[:, None] * b_blk[None]).astype(
        jnp.bfloat16
    )
    state = jnp.einsum("hnks,hpks->hknp", keys_decayed, val_blk, preferred_element_type=jnp.float32)
    c_exp = jnp.exp(cum_log)[:, None] * c_blk[None]
    agg, tot_blk = (state, stretch_tot)
    for level in range(local_bits):
        span = 2**level
        groups = stretch_count // (2 * span)
        paired = agg.reshape(head_count, groups, 2, state_size, head_width)
        left_part = paired[:, :, 0]
        right_part = paired[:, :, 1]
        tot_pair = tot_blk.reshape(head_count, groups, 2)
        src_tot = stretch_tot.reshape(head_count, groups, 2, span)[:, :, 1]
        pre_tot = jnp.concatenate(
            [
                jnp.zeros((head_count, groups, 1), jnp.float32),
                jnp.cumsum(src_tot[..., :-1], axis=2),
            ],
            axis=2,
        )
        carried = jnp.exp(pre_tot)[..., None, None] * left_part[:, :, None]
        c_right = c_exp.reshape(head_count, state_size, groups, 2, span, STRETCH)[:, :, :, 1]
        w_right = level_weight[level + 1].reshape(head_count, groups, 2, span, STRETCH)[:, :, 1]
        contrib = (
            jnp.einsum("hngwq,hgwnp->hpgwq", c_right, carried, precision=lax.Precision.HIGHEST)
            * w_right[:, None]
        )
        result = (
            result.reshape(head_count, head_width, groups, 2, span, STRETCH)
            .at[:, :, :, 1]
            .add(contrib)
            .reshape(head_count, head_width, stretch_count, STRETCH)
        )
        agg = jnp.exp(tot_pair[:, :, 1])[..., None, None] * left_part + right_part
        tot_blk = tot_pair[:, :, 0] + tot_pair[:, :, 1]
    dev_state = agg[:, 0]
    dev_total = tot_blk[:, 0]
    seq_count = lax.axis_size("seq")
    seq_bits = seq_count.bit_length() - 1
    index = lax.axis_index("seq")
    all_states, all_totals = (
        lax.all_gather(dev_state[None], "seq", axis=0, tiled=True),
        lax.all_gather(dev_total[None], "seq", axis=0, tiled=True),
    )
    peers = jnp.arange(seq_count, dtype=jnp.int32)
    between = (peers[None, :] > peers[:, None]) & (peers[None, :] < index)
    log_weight = jnp.einsum(
        "ji,ih->jh", between.astype(jnp.float32), all_totals, precision=lax.Precision.HIGHEST
    )
    bit_ids = jnp.arange(seq_bits, dtype=jnp.int32)
    same_high = peers[None, :] >> bit_ids[:, None] + 1 == index >> bit_ids[:, None] + 1
    own_set = (index >> bit_ids & 1)[:, None] == 1
    peer_clear = peers[None, :] >> bit_ids[:, None] & 1 == 0
    member = same_high & own_set & peer_clear
    coefs = jnp.where(member[:, :, None], jnp.exp(log_weight)[None], 0.0)
    level_states = jnp.einsum("rjh,jhnp->rhnp", coefs, all_states, precision=lax.Precision.HIGHEST)
    pre_dev = jnp.concatenate(
        [jnp.zeros((head_count, 1), jnp.float32), jnp.cumsum(stretch_tot[:, :-1], axis=1)], axis=1
    )
    c_dev = (c_exp * jnp.exp(pre_dev)[:, None, :, None]).reshape(head_count, state_size, row_count)
    reads = jnp.einsum("hnt,rhnp->rhpt", c_dev, level_states, precision=lax.Precision.HIGHEST)
    weights_dev = level_weight[1 + local_bits :]
    total_out = result.reshape(head_count, head_width, row_count) + jnp.sum(
        weights_dev[:, :, None, :] * reads, axis=0
    )
    return total_out.astype(jnp.bfloat16)


def solution(mesh):
    return jax.shard_map(
        on_device,
        mesh=mesh,
        in_specs=(
            P("head", None, "seq"),
            P(None, ("seq", "head")),
            P(None, ("seq", "head")),
            P("head", "seq"),
            P(None, "head", "seq"),
        ),
        out_specs=P("head", None, "seq"),
        check_vma=False,
    )
```

profile of v0, /device:TPU:8, one launch (start us, length us, event | category | flops | bytes accessed | tf_op | source)
XLA Modules:
  0.0 294.2 jit_solution(10901174084038737325)
XLA Ops:
  6.5 1.7 copy.98
  8.3 1.6 copy.97
  16.1 1.8 fusion.128
  17.9 4.3 %reshape.685 = bf16[3,64,64,64]{3,2,1,0:T(8,128)(2,1)S(1)} reshape(bf16[3,64,4096]{2,1,0:T(8,128)(2,1)} %param.17) | data formatting | bytes 3145728 | tf_op jit(solution)/shard_map/reshape | solution.py:18
  36.7 78.2 %all-reduce.6 = f32[96]{0:T(128)S(1)} all-reduce(f32[96]{0:T(128)S(1)} %bitcast_dynamic-update-slice_fusion), channel_id=2, replica_groups=mesh['seq'=32,'head'=8] {'seq'}, use_global_device_ids=true, to_apply=%add.6 | all-reduce | flops 96 | bytes 768
  119.3 7.9 %fusion.5 = f32[3,64,128,64]{2,3,1,0:T(8,128)S(1)} fusion(f32[128,64,64]{0,2,1:T(8,128)S(1)} %convert_element_type.63, f32[3,64,64]{2,1,0:T(8,128)S(1)} %get-tuple-element.99, bf16[3,64,64,64]{3,2,1,0:T(8,128)(2,1)S(1)} %reshape.685), kind=kOutput, calls=%fused_computation.8 | convolution fusion | flops 204472320 | bytes 10010624 | tf_op jit(solution)/shard_map/hnks,hpks->hknp/dot_general | solution.py:33
  128.3 1.9 copy-done.1
  137.7 1.7 slice.452
  150.8 1.6 reshape_squeeze.43
  152.4 1.6 reshape_squeeze.45
  156.9 1.9 copy.144
  160.2 1.6 mul.434
  168.9 2.2 fusion.130
  171.2 9.0 %fusion.4 = f32[3,64,64,64]{3,2,1,0:T(8,128)} fusion(f32[64,64,64]{2,1,0:T(8,128)S(1)} %fusion.130, f32[3,64,64]{2,1,0:T(8,128)S(1)} %reduce_window_sum.72, f32[3,64,64]{2,1,0:T(8,128)S(1)} %copy-done.9, pred[64,64]{1,0:T(8,128)(4,1)S(1)} %iota_compare_fusion, bf16[3,64,64,64]{3,2,1,0:T(8,128)(2,1)S(1)} %reshape.685), kind=kOutput, calls=%fused_computation.7 | convolution fusion | flops 104595456 | bytes 5869568 | tf_op jit(solution)/shard_map/hkts,hpks->hpkt/dot_general | solution.py:29
  180.1 6.6 %copy.106 = f32[3,64,32,2,1,64]{5,1,3,2,0,4:T(8,128)} copy(f32[3,64,32,2,1,64]{1,5,3,2,0,4:T(8,128)} %bitcast.283) | data formatting | bytes 6291456 | tf_op jit(solution)/shard_map/reshape | solution.py:59
  186.7 2.4 slice.458
  189.1 2.4 copy.152
  193.7 8.3 %fusion.20 = f32[3,64,32,2,1,64]{5,1,3,2,0,4:T(8,128)} fusion(f32[3,64,32,2,1,64]{5,1,3,2,0,4:T(8,128)} %copy.106, f32[3,64,32,1,1,64]{5,1,2,0,4,3:T(8,128)S(1)} %copy-done.2, f32[3,32,1,64]{3,1,0,2:T(8,128)S(1)} %copy-done.12, f32[3,32,64]{2,1,0:T(8,128)S(1)} %bitcast.308, f32[3,32,2,128,64]{3,4,2,1,0:T(8,128)} %bitcast.282, ...), kind=kOutput, calls=%fused_computation.30 | convolution fusion | flops 605552640 | bytes 10584064 | tf_op jit(solution)/shard_map/hngwq,hgwnp->hpgwq/dot_general | solution.py:55
  202.0 8.7 %fusion.15 = f32[3,64,16,2,2,64]{5,1,4,3,2,0:T(8,128)} fusion(f32[3,64,16,2,2,64]{5,1,4,3,2,0:T(8,128)} %bitcast.277, f32[3,16,2,64]{3,2,1,0:T(2,128)S(1)} %copy-done.17, f32[3,16,128,64]{2,3,1,0:T(8,128)S(1)} %copy-done.3, f32[3,16,2]{2,1,0:T(8,128)S(1)} %copy-done.18, f32[128,16,2,2,64]{0,4,3,2,1:T(8,128)S(1)} %bitcast.286, ...), kind=kOutput, calls=%fused_computation.22 | convolution fusion | flops 606339072 | bytes 9035776 | tf_op jit(solution)/shard_map/hngwq,hgwnp->hpgwq/dot_general | solution.py:55
  210.7 8.5 %fusion.12 = f32[3,64,8,2,4,64]{5,1,4,3,2,0:T(8,128)} fusion(f32[3,64,8,2,4,64]{5,1,4,3,2,0:T(8,128)} %bitcast.278, f32[3,8,4,64]{3,2,1,0:T(4,128)S(1)} %copy-done.16, f32[3,8,128,64]{2,3,1,0:T(8,128)S(1)} %copy-done.4, f32[3,8,4]{2,1,0:T(8,128)S(1)} %copy-done.21, f32[128,8,2,4,64]{0,4,3,2,1:T(8,128)S(1)} %bitcast.287, f32[3,8,2,4,64]{4,3,2,1,0:T(4,128)S(1)} %bitcast.302), kind=kOutput, calls=%fused_computation.18 | convolution fusion | flops 606339072 | bytes 8237056 | tf_op jit(solution)/shard_map/hngwq,hgwnp->hpgwq/dot_general | solution.py:55
  219.3 8.6 %fusion.9 = f32[3,64,4,2,8,64]{5,1,4,3,2,0:T(8,128)} fusion(f32[3,64,4,2,8,64]{5,1,4,3,2,0:T(8,128)} %bitcast.279, f32[3,4,8,64]{3,2,1,0:T(8,128)S(1)} %copy-done.15, f32[3,4,128,64]{2,3,1,0:T(8,128)S(1)} %copy-done.8, f32[3,4,8]{2,1,0:T(4,128)S(1)} %pad_exponential_fusion, f32[128,4,2,8,64]{0,4,3,2,1:T(8,128)S(1)} %bitcast.288, ...), kind=kOutput, calls=%fused_computation.14 | convolution fusion | flops 606339072 | bytes 7837696 | tf_op jit(solution)/shard_map/hngwq,hgwnp->hpgwq/dot_general | solution.py:55
  227.9 9.2 %copy.129 = f32[3,64,4,2,8,64]{5,4,3,2,1,0:T(8,128)} copy(f32[3,64,4,2,8,64]{5,1,4,3,2,0:T(8,128)} %fusion.9) | data formatting | bytes 6291456 | tf_op jit(solution)/shard_map/scatter-add | solution.py:61
  237.2 5.5 %fusion.6 = f32[3,64,2,1,16,64]{5,1,4,2,0,3:T(8,128)S(1)} fusion(f32[3,64,2,2,16,64]{5,1,4,3,2,0:T(8,128)S(1)} %bitcast.280, f32[3,2,16,64]{3,2,1,0:T(8,128)S(1)} %copy-done.14, f32[3,2,128,64]{2,3,1,0:T(8,128)S(1)} %slice_bitcast_fusion.5, f32[3,2,16]{2,1,0:T(2,128)S(1)} %copy-done.23, f32[128,2,2,16,64]{0,4,3,2,1:T(8,128)S(1)} %bitcast.289, ...), kind=kOutput, calls=%fused_computation.10 | convolution fusion | flops 606339072 | bytes 6065152 | tf_op jit(solution)/shard_map/hngwq,hgwnp->hpgwq/dot_general | solution.py:55
  242.7 3.6 %copy_dynamic-update-slice_fusion.1 = f32[3,64,2,2,16,64]{5,4,3,2,1,0:T(8,128)} fusion(f32[3,64,2,2,16,64]{5,4,3,2,1,0:T(8,128)} %bitcast.52, f32[3,64,2,1,16,64]{5,1,4,2,0,3:T(8,128)S(1)} %fusion.6), kind=kLoop, calls=%fused_computation.47 | loop fusion | bytes 4718592 | tf_op jit(solution)/shard_map/scatter-add | solution.py:61
  246.2 2.2 slice.503
  248.6 7.2 %copy_add_fusion = f32[3,64,1,1,32,64]{5,1,4,0,3,2:T(8,128)S(1)} fusion(f32[3,64,1,1,32,64]{5,4,3,1,0,2:T(8,128)S(1)} %slice.503, f32[128,1,32,64]{0,3,2,1:T(8,128)S(1)} %slice.511, f32[3,32,64]{2,1,0:T(8,128)S(1)} %copy-done.11, f32[3,128,64]{1,2,0:T(8,128)S(1)} %slice_bitcast_fusion.7, f32[3,32]{1,0:T(4,128)S(1)} %bitcast.317, ...), kind=kOutput, calls=%fused_computation.27 | convolution fusion | flops 606339072 | bytes 5965824 | tf_op jit(solution)/shard_map/hngwq,hgwnp->hpgwq/dot_general | solution.py:55
  255.8 3.6 %copy_dynamic-update-slice_fusion = f32[3,64,1,2,32,64]{5,4,3,1,0,2:T(8,128)} fusion(f32[3,64,1,2,32,64]{5,4,3,1,0,2:T(8,128)} %bitcast.66, f32[3,64,1,1,32,64]{5,1,4,0,3,2:T(8,128)S(1)} %copy_add_fusion), kind=kLoop, calls=%fused_computation.46 | loop fusion | bytes 4718592 | tf_op jit(solution)/shard_map/scatter-add | solution.py:61
  259.4 4.5 %reshape_reshape.23 = f32[3,64,4096]{2,1,0:T(8,128)S(1)} reshape(f32[3,64,1,2,32,64]{5,4,3,1,0,2:T(8,128)} %copy_dynamic-update-slice_fusion) | data formatting | bytes 6291456 | tf_op jit(solution)/shard_map/reshape;reshape | solution.py:93
  263.8 2.8 copy.146
  266.7 5.4 %fusion.104 = f32[5,3,128,64]{2,0,3,1:T(8,128)S(1)} fusion(f32[32,3,128,64]{2,3,1,0:T(8,128)} %all-gather.9.cloned.1.call-done, f32[32,3]{0,1:T(4,128)S(1)} %copy-done.24, pred[5,32]{1,0:T(8,128)(4,1)S(1)} %copy-done.27), kind=kOutput, calls=%fused_computation.97 | convolution fusion | flops 47186400 | bytes 3637792 | tf_op jit(solution)/shard_map/rjh,jhnp->rhnp/dot_general | solution.py:86
  272.1 13.7 %fusion = f32[3,64,4096]{2,1,0:T(8,128)S(1)} fusion(f32[5,3,4096]{2,0,1:T(8,128)S(1)} %copy-done.10, f32[3,4096]{1,0:T(4,128)S(1)} %copy-done.20, f32[128,4096]{1,0:T(8,128)S(1)} %copy-done.7, f32[3,4096]{1,0:T(4,128)S(1)} %copy-done.19, f32[5,3,128,64]{2,0,3,1:T(8,128)S(1)} %fusion.104), kind=kOutput, calls=%fused_computation.1 | convolution fusion | flops 6050021376 | bytes 6078464 | tf_op jit(solution)/shard_map/hnt,rhnp->rhpt/dot_general | solution.py:91
  285.8 1.7 add_convert_fusion
  (153 shorter events, 57.9 us)
Async XLA Ops:
  6.5 111.3 %all-gather.7.cloned.1.call-start = ((), (), s32[]{:S(2)}) async-start(), calls=%async_computation.1 | async-start | bytes 1179648 | tf_op jit(solution)/shard_map/all_gather | solution.py:11
  8.2 160.7 %all-gather.5.cloned.1.call-start = ((), (), s32[]{:S(2)}) async-start(), calls=%async_computation | async-start | bytes 1179648 | tf_op jit(solution)/shard_map/all_gather | solution.py:12
  9.9 256.7 %all-gather.9.cloned.1.call-start = ((), (), s32[]{:S(2)}) async-start(), calls=%async_computation.2 | async-start | bytes 3244032 | tf_op jit(solution)/shard_map/all_gather | solution.py:72
  127.2 3.0 %copy-start.1 = (f32[3,64,128,64]{2,3,1,0:T(8,128)}, f32[3,64,128,64]{2,3,1,0:T(8,128)S(1)}, u32[]{:S(2)}) copy-start(f32[3,64,128,64]{2,3,1,0:T(8,128)S(1)} %fusion.5) | copy-start | bytes 18874372
  133.6 1.9 copy-start.25
  133.6 2.0 copy-start.28
  133.7 16.4 %copy-start.22 = (f32[3,8,4]{1,2,0:T(4,128)S(1)}, f32[3,8,4]{1,2,0:T(4,128)}, u32[]{:S(2)}) copy-start(f32[3,8,4]{1,2,0:T(4,128)} %pad_exponential_fusion.1) | copy-start | bytes 1156
  134.7 0.8 copy-start.5
  168.9 2.2 copy-start.9
  189.1 3.9 %copy-start.12 = (f32[3,32,1,64]{3,1,0,2:T(8,128)S(1)}, f32[3,32,1,64]{3,1,0,2:T(8,128)}, u32[]{:S(2)}) copy-start(f32[3,32,1,64]{3,1,0,2:T(8,128)} %copy.182) | copy-start | bytes 73732
  189.1 3.9 %copy-start.13 = (f32[3,32,1,1,64]{4,2,1,0,3:T(1,128)S(1)}, f32[3,32,1,1,64]{4,2,1,0,3:T(1,128)}, u32[]{:S(2)}) copy-start(f32[3,32,1,1,64]{4,2,1,0,3:T(1,128)} %slice.463) | copy-start | bytes 73732
  191.5 2.2 copy-start.2
  193.7 8.3 %copy-start.3 = (f32[3,16,128,64]{2,3,1,0:T(8,128)S(1)}, f32[3,16,128,64]{2,3,1,0:T(8,128)}, u32[]{:S(2)}) copy-start(f32[3,16,128,64]{2,3,1,0:T(8,128)} %get-tuple-element.84) | copy-start | bytes 4718596
  193.7 8.3 %copy-start.17 = (f32[3,16,2,64]{3,2,1,0:T(2,128)S(1)}, f32[3,16,2,64]{3,2,1,0:T(2,128)}, u32[]{:S(2)}) copy-start(f32[3,16,2,64]{3,2,1,0:T(2,128)} %slice_bitcast_fusion.12) | copy-start | bytes 73732
  193.7 8.3 %copy-start.18 = (f32[3,16,2]{2,1,0:T(8,128)S(1)}, f32[3,16,2]{2,1,0:T(8,128)}, u32[]{:S(2)}) copy-start(f32[3,16,2]{2,1,0:T(8,128)} %copy.110) | copy-start | bytes 1156
  202.0 8.7 %copy-start.4 = (f32[3,8,128,64]{2,3,1,0:T(8,128)S(1)}, f32[3,8,128,64]{2,3,1,0:T(8,128)}, u32[]{:S(2)}) copy-start(f32[3,8,128,64]{2,3,1,0:T(8,128)} %get-tuple-element.87) | copy-start | bytes 2359300
  202.0 8.7 %copy-start.16 = (f32[3,8,4,64]{3,2,1,0:T(4,128)S(1)}, f32[3,8,4,64]{3,2,1,0:T(4,128)}, u32[]{:S(2)}) copy-start(f32[3,8,4,64]{3,2,1,0:T(4,128)} %slice_bitcast_fusion.11) | copy-start | bytes 73732
  202.0 8.7 %copy-start.21 = (f32[3,8,4]{2,1,0:T(8,128)S(1)}, f32[3,8,4]{2,1,0:T(8,128)}, u32[]{:S(2)}) copy-start(f32[3,8,4]{2,1,0:T(8,128)} %copy.117) | copy-start | bytes 1156
  210.7 8.5 %copy-start.8 = (f32[3,4,128,64]{2,3,1,0:T(8,128)S(1)}, f32[3,4,128,64]{2,3,1,0:T(8,128)}, u32[]{:S(2)}) copy-start(f32[3,4,128,64]{2,3,1,0:T(8,128)} %get-tuple-element.97) | copy-start | bytes 1179652
  210.7 8.5 %copy-start.15 = (f32[3,4,8,64]{3,2,1,0:T(8,128)S(1)}, f32[3,4,8,64]{3,2,1,0:T(8,128)}, u32[]{:S(2)}) copy-start(f32[3,4,8,64]{3,2,1,0:T(8,128)} %slice_bitcast_fusion.10) | copy-start | bytes 73732
  227.9 9.3 %copy-start.6 = (f32[3,2,2,128,64]{3,4,2,1,0:T(8,128)S(1)}, f32[3,2,2,128,64]{3,4,2,1,0:T(8,128)}, u32[]{:S(2)}) copy-start(f32[3,2,2,128,64]{3,4,2,1,0:T(8,128)} %copy-done.5) | copy-start | bytes 1179652
  227.9 9.3 %copy-start = (f32[3,64,4,2,8,64]{5,1,4,3,2,0:T(8,128)S(1)}, f32[3,64,4,2,8,64]{5,1,4,3,2,0:T(8,128)}, u32[]{:S(2)}) copy-start(f32[3,64,4,2,8,64]{5,1,4,3,2,0:T(8,128)} %fusion.9) | copy-start | bytes 9437188
  227.9 9.3 %copy-start.14 = (f32[3,2,16,64]{3,2,1,0:T(8,128)S(1)}, f32[3,2,16,64]{3,2,1,0:T(8,128)}, u32[]{:S(2)}) copy-start(f32[3,2,16,64]{3,2,1,0:T(8,128)} %slice_bitcast_fusion.9) | copy-start | bytes 73732
  227.9 9.3 %copy-start.23 = (f32[3,2,16]{2,1,0:T(2,128)S(1)}, f32[3,2,16]{2,1,0:T(2,128)}, u32[]{:S(2)}) copy-start(f32[3,2,16]{2,1,0:T(2,128)} %pad_exponential_fusion.2) | copy-start | bytes 1156
  246.2 2.4 copy-start.11
  246.2 2.4 copy-start.26
  263.8 2.8 copy-start.24
  263.8 2.8 copy-start.27
  263.8 8.2 %copy-start.10 = (f32[5,3,4096]{2,0,1:T(8,128)S(1)}, f32[5,3,4096]{2,0,1:T(8,128)}, u32[]{:S(2)}) copy-start(f32[5,3,4096]{2,0,1:T(8,128)} %copy.144) | copy-start | bytes 737284
  266.7 5.4 %copy-start.7 = (f32[128,4096]{1,0:T(8,128)S(1)}, f32[128,4096]{1,0:T(8,128)}, u32[]{:S(2)}) copy-start(f32[128,4096]{1,0:T(8,128)} %copy.146) | copy-start | bytes 6291460
  266.7 5.4 %copy-start.19 = (f32[3,4096]{1,0:T(4,128)S(1)}, f32[3,4096]{1,0:T(4,128)}, u32[]{:S(2)}) copy-start(f32[3,4096]{1,0:T(4,128)} %exp.154) | copy-start | bytes 147460
  266.7 5.4 %copy-start.20 = (f32[3,4096]{1,0:T(4,128)S(1)}, f32[3,4096]{1,0:T(4,128)}, u32[]{:S(2)}) copy-start(f32[3,4096]{1,0:T(4,128)} %mul.434) | copy-start | bytes 147460
Sparse Core Ops, SparseCore 0:
  9.2 27.1 all-gather.6
  38.3 26.0 all-gather.4
  136.5 73.6 all-gather.8
where the time goes:
time: 298 us; the launch traced here: 294 us
  local copies, waits for them, and re-layouts  101 us (34%)
  matrix products  86.4 us (29%)
  blocking collectives  78.2 us (26%)
  between operations  14.6 us (5%)
  other arithmetic  14.2 us (5%)
    unnamed x1, blocking collectives  78.2 us
    dot_general x6, matrix products, on_device(): jnp.einsum('hngwq,hgwnp->hpgwq', c_right, carried, precision=lax.Precisio...  46.7 us
    scatter-add x3, local copies, waits for them, and re-layouts, on_device(): result = result.reshape(head_count, head_width, groups, 2, span, STRETCH)...  16.4 us
    dot_general x1, matrix products, on_device(): jnp.einsum('hnt,rhnp->rhpt', c_dev, level_states, precision=lax.Precision...  13.7 us
    unnamed x65, local copies, waits for them, and re-layouts  12.3 us
    another operation x6, local copies, waits for them, and re-layouts, on_device(): level_weight[level + 1].reshape(head_count, groups, 2, span, STRETCH)  9.6 us
    dot_general x1, matrix products, on_device(): jnp.einsum('hkts,hpks->hpkt', mix, val_blk, preferred_element_type=jnp.fl...  8.96 us
    dot_general x1, matrix products, on_device(): jnp.einsum('hnks,hpks->hknp', keys_decayed, val_blk, preferred_element_ty...  7.93 us
  transfers between devices with their start and end apart: 3, of which 0 were waited for; matrix products, arithmetic and copies ran while one was open for 60% of the time, Pallas kernels for 0%

commit v1 on v0

v1 whole, which is shorter than its diff:
```python
import jax
import jax.numpy as jnp
from jax import lax
from jax.experimental import pallas as pl
from jax.experimental.pallas import tpu as pltpu
from jax.sharding import PartitionSpec as P

STRETCH = 64
HEADS = 3
WIDTH = 64
STATE = 128
ROWS = HEADS * WIDTH
PIECE = 512
PIECES = 8
TOKENS = PIECE * PIECES
LOCAL = 6
CROSS = 5
FIRST = (0, 32, 48, 56, 60, 62, 63)
F32 = jnp.float32
BF16 = jnp.bfloat16

VMEM = pl.BlockSpec(memory_space=pltpu.VMEM)
SMEM = pl.BlockSpec(memory_space=pltpu.SMEM)


def params():
    return pltpu.CompilerParams(vmem_limit_bytes=56 * 1024 * 1024)


def decay_kernel(ld_ref, lw_ref, sc_ref, binv_ref, dec_ref, grp_ref):
    tiles = TOKENS // 128
    lane = lax.broadcasted_iota(jnp.int32, (HEADS, 128), 1)
    local = lane & 63
    runs = []
    for i in range(tiles):
        cols = pl.ds(i * 128, 128)
        ld = ld_ref[:, cols]
        cum = ld
        for k in (1, 2, 4, 8, 16, 32):
            cum = cum + jnp.where(local >= k, pltpu.roll(cum, k, 1), 0.0)
        rest = ld
        for k in (1, 2, 4, 8, 16, 32):
            rest = rest + jnp.where(local < 64 - k, pltpu.roll(rest, 128 - k, 1), 0.0)
        runs.append(cum)
        grow = jnp.exp(cum)
        dec_ref[:, cols] = jnp.exp(rest - ld)
        binv_ref[:, cols] = jnp.exp(-cum)
        sc_ref[0, :, cols] = lw_ref[0, :, cols] * grow
        sc_ref[1, :, cols] = jnp.where(lane >= 64, lw_ref[1, :, cols] * grow, 0.0)
        grp_ref[:, cols] = jnp.broadcast_to(grow[:, 127:128], (HEADS, 128))
        left = jnp.broadcast_to(cum[:, 63:64], (HEADS, 128))
        runs[i] = cum + jnp.where(lane >= 64, left, 0.0)
    for level in range(2, LOCAL + 2):
        span = 2 ** (level - 2)
        ends = [jnp.broadcast_to(runs[i][:, 127:128], (HEADS, 128)) for i in range(span - 1, tiles, span)]
        for i in range(tiles):
            cols = pl.ds(i * 128, 128)
            if level <= LOCAL:
                if (i // span) % 2:
                    sc_ref[level, :, cols] = lw_ref[level, :, cols] * jnp.exp(runs[i])
                else:
                    sc_ref[level, :, cols] = jnp.zeros((HEADS, 128), F32)
            else:
                grow = jnp.exp(runs[i])
                for up in range(CROSS):
                    sc_ref[level + up, :, cols] = lw_ref[level + up, :, cols] * grow
        if level <= LOCAL:
            for i in range(tiles // (2 * span)):
                grp_ref[:, pl.ds((FIRST[level - 1] + i) * 128, 128)] = jnp.exp(ends[2 * i + 1])
            for i in range(tiles):
                if (i // span) % 2:
                    runs[i] = runs[i] + ends[i // span - 1]
        else:
            grp_ref[:, pl.ds(63 * 128, 128)] = ends[0]


def decay_rows(log_decay, level_weight):
    row = jax.ShapeDtypeStruct((HEADS, TOKENS), F32)
    return pl.pallas_call(
        decay_kernel,
        out_shape=[
            jax.ShapeDtypeStruct((1 + LOCAL + CROSS, HEADS, TOKENS), F32),
            row,
            row,
            jax.ShapeDtypeStruct((HEADS, 64 * 128), F32),
        ],
        in_specs=[VMEM] * 2,
        out_specs=[VMEM] * 4,
        compiler_params=params(),
        name="decay_rows",
    )(log_decay, level_weight)


def state_kernel(order_ref, v_ref, dec_ref, grp_ref, *refs):
    b_refs = refs[:PIECES]
    agg_ref, end_ref, b_buf, p_buf = refs[PIECES:]
    for q in range(PIECES):
        b_buf[q] = b_refs[q][...]
    lane = lax.broadcasted_iota(jnp.int32, (WIDTH, 128), 1)
    first = lane < 64

    def factor(h, slot):
        return grp_ref[h : h + 1, pl.ds(pl.multiple_of(slot * 128, 128), 128)]

    def piece(q, carry):
        j = order_ref[q]
        for h in range(HEADS):
            here = slice(h * WIDTH, (h + 1) * WIDTH)
            tops = []
            for a in range(4):
                cols = pl.ds(pl.multiple_of(j * PIECE + a * 128, 128), 128)
                b = b_buf[q, :, a * 128 : (a + 1) * 128].astype(F32)
                v = v_ref[h, :, cols]
                keys = (dec_ref[h : h + 1, cols] * b).astype(BF16)
                zero = jnp.zeros_like(v)
                both = jnp.concatenate([jnp.where(first, v, zero), jnp.where(first, zero, v)], axis=0)
                s = lax.dot_general(both, keys, (((1,), (1,)), ((), ())), preferred_element_type=F32)
                agg_ref[j * 4 + a, here, :] = s[:WIDTH].astype(BF16)
                tops.append(factor(h, j * 4 + a) * s[:WIDTH] + s[WIDTH:])
            agg_ref[FIRST[1] + j * 2, here, :] = tops[0].astype(BF16)
            agg_ref[FIRST[1] + j * 2 + 1, here, :] = tops[2].astype(BF16)
            lo = factor(h, FIRST[1] + j * 2) * tops[0] + tops[1]
            hi = factor(h, FIRST[1] + j * 2 + 1) * tops[2] + tops[3]
            agg_ref[FIRST[2] + j, here, :] = lo.astype(BF16)
            p_buf[j, here, :] = factor(h, FIRST[2] + j) * lo + hi
        return carry

    lax.fori_loop(0, PIECES, piece, 0)
    for h in range(HEADS):
        here = slice(h * WIDTH, (h + 1) * WIDTH)
        tops = [p_buf[j, here, :] for j in range(PIECES)]
        for level in range(4, LOCAL + 1):
            nxt = []
            for i in range(len(tops) // 2):
                slot = FIRST[level - 1] + i
                agg_ref[slot, here, :] = tops[2 * i].astype(BF16)
                nxt.append(factor(h, slot) * tops[2 * i] + tops[2 * i + 1])
            tops = nxt
        end_ref[here, :] = tops[0]
    end_ref[ROWS : ROWS + 8, :] = jnp.concatenate([grp_ref[:, 63 * 128 :], jnp.zeros((5, 128), F32)], axis=0)


def block_states(order, values, dec, grp, b_list):
    return pl.pallas_call(
        state_kernel,
        out_shape=[
            jax.ShapeDtypeStruct((63, ROWS, STATE), BF16),
            jax.ShapeDtypeStruct((ROWS + 8, STATE), F32),
        ],
        in_specs=[SMEM] + [VMEM] * (3 + PIECES),
        out_specs=[VMEM] * 2,
        scratch_shapes=[
            pltpu.VMEM((PIECES, STATE, PIECE), BF16),
            pltpu.VMEM((PIECES, ROWS, STATE), F32),
        ],
        compiler_params=params(),
        name="block_states",
    )(order, values, dec, grp, *b_list)


def local_kernel(order_ref, v_ref, sc_ref, binv_ref, agg_ref, *refs):
    b_refs = refs[:PIECES]
    c_refs = refs[PIECES : 2 * PIECES]
    out_ref, b_buf, c_buf = refs[2 * PIECES :]
    for q in range(PIECES):
        b_buf[q] = b_refs[q][...]
        c_buf[q] = c_refs[q][...]
    s_id = lax.broadcasted_iota(jnp.int32, (128, 128), 0)
    t_id = lax.broadcasted_iota(jnp.int32, (128, 128), 1)
    keep = (s_id <= t_id) & ((s_id >> 6) == (t_id >> 6))

    def piece(q, carry):
        j = order_ref[q]
        base = j * PIECE
        for a in range(4):
            cols = pl.ds(pl.multiple_of(base + a * 128, 128), 128)
            c = c_buf[q, :, a * 128 : (a + 1) * 128]
            b = b_buf[q, :, a * 128 : (a + 1) * 128]
            scores = lax.dot_general(b, c, (((0,), (0,)), ((), ())), preferred_element_type=F32)
            scores = jnp.where(keep, scores, 0.0)
            slots = [(1, j * 4 + a)]
            if a & 1:
                slots.append((2, FIRST[1] + j * 2 + a // 2))
            if a & 2:
                slots.append((3, FIRST[2] + j))
            reads = [(level, jnp.dot(agg_ref[slot], c, preferred_element_type=F32)) for level, slot in slots]
            for h in range(HEADS):
                here = slice(h * WIDTH, (h + 1) * WIDTH)
                col = jnp.transpose(jnp.broadcast_to(binv_ref[h : h + 1, cols], (128, 128)))
                mix = ((sc_ref[0, h : h + 1, cols] * scores) * col).astype(BF16)
                acc = jnp.dot(v_ref[h, :, cols], mix, preferred_element_type=F32)
                for level, r in reads:
                    acc = acc + sc_ref[level, h : h + 1, cols] * r[here, :]
                out_ref[h, :, cols] = acc
        for level in range(4, LOCAL + 1):
            bit = level - 4

            @pl.when(((j >> bit) & 1) == 1)
            def _():
                slot = FIRST[level - 1] + (j >> (bit + 1))
                for a in range(2):
                    cols = pl.ds(pl.multiple_of(base + a * 256, 256), 256)
                    c = c_buf[q, :, a * 256 : (a + 1) * 256]
                    r = jnp.dot(agg_ref[slot], c, preferred_element_type=F32)
                    for h in range(HEADS):
                        here = slice(h * WIDTH, (h + 1) * WIDTH)
                        out_ref[h, :, cols] += sc_ref[level, h : h + 1, cols] * r[here, :]

        return carry

    lax.fori_loop(0, PIECES, piece, 0)


def local_part(order, values, sc, binv, agg, b_list, c_list):
    return pl.pallas_call(
        local_kernel,
        out_shape=jax.ShapeDtypeStruct((HEADS, WIDTH, TOKENS), F32),
        in_specs=[SMEM] + [VMEM] * (4 + 2 * PIECES),
        out_specs=VMEM,
        scratch_shapes=[
            pltpu.VMEM((PIECES, STATE, PIECE), BF16),
            pltpu.VMEM((PIECES, STATE, PIECE), BF16),
        ],
        compiler_params=params(),
        name="local_part",
    )(order, values, sc, binv, agg, *b_list, *c_list)


def cross_kernel(order_ref, loc_ref, sc_ref, fac_ref, *refs):
    s_refs = refs[:CROSS]
    c_refs = refs[CROSS : CROSS + PIECES]
    out_ref, c_buf = refs[CROSS + PIECES :]
    for q in range(PIECES):
        c_buf[q] = c_refs[q][...]

    def piece(q, carry):
        base = order_ref[q] * PIECE
        for a in range(2):
            cols = pl.ds(pl.multiple_of(base + a * 256, 256), 256)
            c = c_buf[q, :, a * 256 : (a + 1) * 256]
            accs = [loc_ref[h, :, cols] for h in range(HEADS)]
            for level in range(CROSS):
                r = jnp.dot(s_refs[level][...], c, preferred_element_type=F32)
                for h in range(HEADS):
                    here = slice(h * WIDTH, (h + 1) * WIDTH)
                    fac = fac_ref[level, h : h + 1, :]
                    row = sc_ref[1 + LOCAL + level, h : h + 1, cols] * jnp.concatenate([fac, fac], axis=1)
                    accs[h] = accs[h] + row * r[here, :]
            for h in range(HEADS):
                out_ref[h, :, cols] = accs[h].astype(BF16)
        return carry

    lax.fori_loop(0, PIECES, piece, 0)


def cross_part(order, loc, sc, fac, states, c_list):
    return pl.pallas_call(
        cross_kernel,
        out_shape=jax.ShapeDtypeStruct((HEADS, WIDTH, TOKENS), BF16),
        in_specs=[SMEM] + [VMEM] * (3 + CROSS + PIECES),
        out_specs=VMEM,
        scratch_shapes=[pltpu.VMEM((PIECES, STATE, PIECE), BF16)],
        compiler_params=params(),
        name="cross_part",
    )(order, loc, sc, fac, *states, *c_list)


def y_shift(x, k):
    return lax.ppermute(x, "head", [(i, ((i // 2 + k) % 4) * 2 + i % 2) for i in range(8)])


def other_core(x):
    return lax.ppermute(x, "head", [(i, i ^ 1) for i in range(8)])


def gather_pieces(x):
    near = [x] + [y_shift(x, k) for k in (1, 3, 2)]
    return near + [other_core(p) for p in near]


def partner(r, i):
    x, z = i // 8, i % 8
    if r == 0:
        z = z ^ 1
    elif r == 1:
        z = z ^ 2
    elif r == 2:
        z = 7 - z
    elif r == 3:
        x = x ^ 1
    else:
        x = 3 - x
    return x * 8 + z


def on_device(values, b_rows, c_rows, log_decay, level_weight):
    me = lax.axis_index("head")
    index = lax.axis_index("seq")
    y, core = me // 2, me % 2
    order = jnp.stack(
        [((y - k) % 4) * 2 + core for k in (0, 1, 3, 2)] + [((y - k) % 4) * 2 + 1 - core for k in (0, 1, 3, 2)]
    ).astype(jnp.int32)
    b_list = gather_pieces(b_rows)
    c_list = gather_pieces(c_rows)
    sc, binv, dec, grp = decay_rows(log_decay, level_weight)
    agg, own = block_states(order, values, dec, grp, b_list)
    loc = local_part(order, values, sc, binv, agg, b_list, c_list)
    states, facs = [], []
    before = jnp.zeros((HEADS, STATE), F32)
    for r in range(CROSS):
        got = lax.ppermute(own, "seq", [(i, partner(r, i)) for i in range(32)])
        right = ((index >> r) & 1) == 1
        states.append(got[:ROWS].astype(BF16))
        facs.append(jnp.where(right, jnp.exp(before), 0.0))
        if r == CROSS - 1:
            break
        own_tot = own[ROWS : ROWS + HEADS]
        got_tot = got[ROWS : ROWS + HEADS]
        scale = jnp.exp(jnp.where(right, own_tot, got_tot))
        scale = jnp.broadcast_to(scale[:, None], (HEADS, WIDTH, STATE)).reshape(ROWS, STATE)
        scale = jnp.concatenate([scale, jnp.ones((8, STATE), F32)], axis=0)
        own = scale * jnp.where(right, got, own) + jnp.where(right, own, got)
        before = before + jnp.where(right, got_tot, 0.0)
    fac = jnp.stack(facs)
    return cross_part(order, loc, sc, fac, states, c_list)


def solution(mesh):
    return jax.shard_map(
        on_device,
        mesh=mesh,
        in_specs=(
            P("head", None, "seq"),
            P(None, ("seq", "head")),
            P(None, ("seq", "head")),
            P("head", "seq"),
            P(None, "head", "seq"),
        ),
        out_specs=P("head", None, "seq"),
        check_vma=False,
    )
```

time: 298 us -> 83 us (0.28)
  the two profiles are of different devices: /device:TPU:8 before, /device:TPU:6 now
where the time goes in v1:
time: 83 us; the launch traced here: 82.9 us
  Pallas kernels  33.6 us (40%)
  starting transfers between devices  23.5 us (28%)
  waiting for transfers between devices  20.2 us (24%)
  local copies, waits for them, and re-layouts  5.24 us (6%)
    ppermute x5, waiting for transfers between devices, on_device(): got = lax.ppermute(own, 'seq', [(i, partner(r, i)) for i in range(32)])  15 us
    pallas_call x1, Pallas kernels, local_part(): pl.pallas_call(local_kernel, out_shape=jax.ShapeDtypeStruct((HEADS, WIDTH...  14.7 us
    ppermute x5, starting transfers between devices, on_device(): got = lax.ppermute(own, 'seq', [(i, partner(r, i)) for i in range(32)])  11.7 us
    ppermute x6, starting transfers between devices, y_shift(): lax.ppermute(x, 'head', [(i, (i // 2 + k) % 4 * 2 + i % 2) for i in range...  10.2 us
    pallas_call x1, Pallas kernels, cross_part(): pl.pallas_call(cross_kernel, out_shape=jax.ShapeDtypeStruct((HEADS, WIDTH...  6.96 us
    pallas_call x1, Pallas kernels, block_states(): pl.pallas_call(state_kernel, out_shape=[jax.ShapeDtypeStruct((63, ROWS, S...  6.83 us
    pallas_call x1, Pallas kernels, decay_rows(): pl.pallas_call(decay_kernel, out_shape=[jax.ShapeDtypeStruct((1 + LOCAL +...  5.14 us
    ppermute x6, waiting for transfers between devices, y_shift(): lax.ppermute(x, 'head', [(i, (i // 2 + k) % 4 * 2 + i % 2) for i in range...  5.11 us
  transfers between devices with their start and end apart: 19, of which 8 were waited for; matrix products, arithmetic and copies ran while one was open for 4% of the time, Pallas kernels for 32%

profile of v1, /device:TPU:6, one launch (start us, length us, event | category | flops | bytes accessed | tf_op | source)
XLA Modules:
  0.0 82.9 jit_solution(16368066284884778346)
XLA Ops:
  0.0 1.6 %collective-permute-start = (bf16[128,512]{1,0:T(8,128)(2,1)}, bf16[128,512]{1,0:T(8,128)(2,1)S(1)}, u32[]{:S(2)}, u32[]{:S(2)}) collective-permute-start(bf16[128,512]{1,0:T(8,128)(2,1)} %refs_0_.3), channel_id=1, source_target_pairs={{0,2},{1,3},{2,4},{3,5},{4,6},{5,7},{6,0},{7,1},{8,10},{9,11},{10,... | collective-permute-start | bytes 393224 | tf_op jit(solution)/shard_map/ppermute | solution.py:269
  1.6 1.7 %collective-permute-start.1 = (bf16[128,512]{1,0:T(8,128)(2,1)}, bf16[128,512]{1,0:T(8,128)(2,1)S(1)}, u32[]{:S(2)}, u32[]{:S(2)}) collective-permute-start(bf16[128,512]{1,0:T(8,128)(2,1)} %refs_0_.3), channel_id=1, source_target_pairs={{0,6},{1,7},{2,0},{3,1},{4,2},{5,3},{6,4},{7,5},{8,14},{9,15},{10,... | collective-permute-start | bytes 393224 | tf_op jit(solution)/shard_map/ppermute | solution.py:269
  3.2 2.0 %collective-permute-start.2 = (bf16[128,512]{1,0:T(8,128)(2,1)}, bf16[128,512]{1,0:T(8,128)(2,1)S(1)}, u32[]{:S(2)}, u32[]{:S(2)}) collective-permute-start(bf16[128,512]{1,0:T(8,128)(2,1)} %refs_0_.3), channel_id=1, source_target_pairs={{0,4},{1,5},{2,6},{3,7},{4,0},{5,1},{6,2},{7,3},{8,12},{9,13},{10,... | collective-permute-start | bytes 393224 | tf_op jit(solution)/shard_map/ppermute | solution.py:269
  5.2 0.7 collective-permute-start.7
  5.9 0.8 collective-permute-done.refs_1_
  6.7 2.8 %collective-permute-start.8 = (bf16[128,512]{1,0:T(8,128)(2,1)}, bf16[128,512]{1,0:T(8,128)(2,1)S(1)}, u32[]{:S(2)}, u32[]{:S(2)}) collective-permute-start(bf16[128,512]{1,0:T(8,128)(2,1)} %refs_5_.1), channel_id=1, source_target_pairs={{0,6},{1,7},{2,0},{3,1},{4,2},{5,3},{6,4},{7,5},{8,14},{9,15},{10,... | collective-permute-start | bytes 393224 | tf_op jit(solution)/shard_map/ppermute | solution.py:269
  9.5 1.5 %collective-permute-start.9 = (bf16[128,512]{1,0:T(8,128)(2,1)}, bf16[128,512]{1,0:T(8,128)(2,1)S(1)}, u32[]{:S(2)}, u32[]{:S(2)}) collective-permute-start(bf16[128,512]{1,0:T(8,128)(2,1)} %refs_5_.1), channel_id=1, source_target_pairs={{0,4},{1,5},{2,6},{3,7},{4,0},{5,1},{6,2},{7,3},{8,12},{9,13},{10,... | collective-permute-start | bytes 393224 | tf_op jit(solution)/shard_map/ppermute | solution.py:269
  11.1 0.7 collective-permute-done.2.refs_3_
  12.3 2.0 %collective-permute-done.7.refs_9_.refs_6_ = bf16[128,512]{1,0:T(8,128)(2,1)S(1)} collective-permute-done((bf16[128,512]{1,0:T(8,128)(2,1)}, bf16[128,512]{1,0:T(8,128)(2,1)S(1)}, u32[]{:S(2)}, u32[]{:S(2)}) %collective-permute-start.7) | collective-permute-done | bytes 131104 | tf_op jit(solution)/shard_map/ppermute | solution.py:269
  14.8 1.6 %collective-permute-done.9.refs_11_.refs_8_ = bf16[128,512]{1,0:T(8,128)(2,1)S(1)} collective-permute-done((bf16[128,512]{1,0:T(8,128)(2,1)}, bf16[128,512]{1,0:T(8,128)(2,1)S(1)}, u32[]{:S(2)}, u32[]{:S(2)}) %collective-permute-start.9) | collective-permute-done | bytes 131104 | tf_op jit(solution)/shard_map/ppermute | solution.py:269
  16.4 0.5 collective-permute-start.12
  17.0 5.1 %decay_rows.1 = (f32[12,3,4096]{2,1,0:T(4,128)}, f32[3,4096]{1,0:T(4,128)}, f32[3,4096]{1,0:T(4,128)}, f32[3,8192]{1,0:T(4,128)}) custom-call(f32[3,4096]{1,0:T(4,128)} %ld_ref.1, f32[12,3,4096]{2,1,0:T(4,128)} %lw_ref.1), custom_call_target="tpu_custom_call" | custom-call | tf_op jit(solution)/shard_map/decay_rows/pallas_call | solution.py:79
  22.2 0.7 stack.53.order_ref
  22.9 0.6 copy-done.13
  23.5 6.8 %block_states.1 = (bf16[63,192,128]{2,1,0:T(8,128)(2,1)}, f32[200,128]{1,0:T(8,128)}) custom-call(s32[8]{0:T(128)} %stack.53.order_ref, bf16[3,64,4096]{2,1,0:T(8,128)(2,1)} %v_ref.3, f32[3,4096]{1,0:T(4,128)} %get-tuple-element.13.dec_ref, f32[3,8192]{1,0:T(4,128)} %get-tuple-element.14.grp_ref, bf16[128,512]{1,0:T(8,128)(2,1)} %refs_0_.3, ...), custom_call_target="tpu_custom_call" | custom-call | tf_op jit(solution)/shard_map/block_states/pallas_call | solution.py:144
  30.3 1.9 %collective-permute-start.14 = (f32[200,128]{1,0:T(8,128)}, f32[200,128]{1,0:T(8,128)S(1)}, u32[]{:S(2)}, u32[]{:S(2)}) collective-permute-start(f32[200,128]{1,0:T(8,128)} %get-tuple-element.16), channel_id=1, source_target_pairs={{0,8},{8,0},{16,24},{24,16},{32,40},{40,32},{48,56},{56,48},{64,72... | collective-permute-start | bytes 307208 | tf_op jit(solution)/shard_map/ppermute | solution.py:311
  32.3 0.6 copy-done.3
  33.1 14.7 %local_part.1.loc_ref = f32[3,64,4096]{2,1,0:T(8,128)} custom-call(s32[8]{0:T(128)} %stack.53.order_ref, bf16[3,64,4096]{2,1,0:T(8,128)(2,1)} %v_ref.3, f32[12,3,4096]{2,1,0:T(4,128)} %get-tuple-element.11.sc_ref, f32[3,4096]{1,0:T(4,128)} %get-tuple-element.12.binv_ref, bf16[63,192,128]{2,1,0:T(8,128)(2,1)} %get-tuple-element.15.agg_ref, ...), custom_call_target="tpu_custom_call" | custom-call | tf_op jit(solution)/shard_map/local_part/pallas_call | solution.py:215
  47.8 3.5 %collective-permute-start.15 = (f32[200,128]{1,0:T(8,128)S(1)}, f32[200,128]{1,0:T(8,128)S(1)}, u32[]{:S(2)}, u32[]{:S(2)}) collective-permute-start(f32[200,128]{1,0:T(8,128)S(1)} %select_add_fusion.3), channel_id=1, source_target_pairs={{0,16},{8,24},{16,0},{24,8},{32,48},{40,56},{48,32},{56,40},{64,80... | collective-permute-start | bytes 307208 | tf_op jit(solution)/shard_map/ppermute | solution.py:311
  51.4 0.6 slice.104.refs_0_
  52.0 4.5 %collective-permute-done.15 = f32[200,128]{1,0:T(8,128)S(1)} collective-permute-done((f32[200,128]{1,0:T(8,128)S(1)}, f32[200,128]{1,0:T(8,128)S(1)}, u32[]{:S(2)}, u32[]{:S(2)}) %collective-permute-start.15) | collective-permute-done | bytes 102432 | tf_op jit(solution)/shard_map/ppermute | solution.py:311
  56.5 4.7 %collective-permute-start.16 = (f32[200,128]{1,0:T(8,128)S(1)}, f32[200,128]{1,0:T(8,128)S(1)}, u32[]{:S(2)}, u32[]{:S(2)}) collective-permute-start(f32[200,128]{1,0:T(8,128)S(1)} %select_add_fusion.2), channel_id=1, source_target_pairs={{0,56},{8,48},{16,40},{24,32},{32,24},{40,16},{48,8},{56,0},{64,12... | collective-permute-start | bytes 307208 | tf_op jit(solution)/shard_map/ppermute | solution.py:311
  61.3 0.6 slice.103.refs_1_
  61.9 3.0 %collective-permute-done.16 = f32[200,128]{1,0:T(8,128)S(1)} collective-permute-done((f32[200,128]{1,0:T(8,128)S(1)}, f32[200,128]{1,0:T(8,128)S(1)}, u32[]{:S(2)}, u32[]{:S(2)}) %collective-permute-start.16) | collective-permute-done | bytes 102432 | tf_op jit(solution)/shard_map/ppermute | solution.py:311
  65.0 0.9 %collective-permute-start.17 = (f32[200,128]{1,0:T(8,128)S(1)}, f32[200,128]{1,0:T(8,128)S(1)}, u32[]{:S(2)}, u32[]{:S(2)}) collective-permute-start(f32[200,128]{1,0:T(8,128)S(1)} %select_add_fusion.1), channel_id=1, source_target_pairs={{0,64},{8,72},{16,80},{24,88},{32,96},{40,104},{48,112},{56,120},{... | collective-permute-start | bytes 307208 | tf_op jit(solution)/shard_map/ppermute | solution.py:311
  65.9 0.6 slice.102.refs_2_
  66.5 3.3 %collective-permute-done.17 = f32[200,128]{1,0:T(8,128)S(1)} collective-permute-done((f32[200,128]{1,0:T(8,128)S(1)}, f32[200,128]{1,0:T(8,128)S(1)}, u32[]{:S(2)}, u32[]{:S(2)}) %collective-permute-start.17) | collective-permute-done | bytes 102432 | tf_op jit(solution)/shard_map/ppermute | solution.py:311
  69.9 0.6 collective-permute-start.18
  70.5 0.6 slice.101.refs_3_
  71.1 4.2 %collective-permute-done.18 = bf16[200,128]{1,0:T(8,128)(2,1)S(1)} collective-permute-done((bf16[200,128]{1,0:T(8,128)(2,1)S(1)}, bf16[200,128]{1,0:T(8,128)(2,1)S(1)}, u32[]{:S(2)}, u32[]{:S(2)}) %collective-permute-start.18) | collective-permute-done | bytes 51232 | tf_op jit(solution)/shard_map/ppermute | solution.py:311
  75.3 0.6 slice.100.refs_4_
  75.9 7.0 %cross_part.1 = bf16[3,64,4096]{2,1,0:T(8,128)(2,1)} custom-call(s32[8]{0:T(128)} %stack.53.order_ref, f32[3,64,4096]{2,1,0:T(8,128)} %local_part.1.loc_ref, f32[12,3,4096]{2,1,0:T(4,128)} %get-tuple-element.11.sc_ref, f32[5,3,128]{2,1,0:T(4,128)} %copy-done.15, bf16[192,128]{1,0:T(8,128)(2,1)} %slice.104.refs_0_, bf16[192,128]{1,0:T(8,128)(2,1)} %slice.103.refs_1_, ...), custom_call_target="tpu_custom_call" | custom-call | tf_op jit(solution)/shard_map/cross_part/pallas_call | solution.py:257
  (65 shorter events, 1.6 us)
Async XLA Ops:
  0.0 6.7 %collective-permute-start = (bf16[128,512]{1,0:T(8,128)(2,1)}, bf16[128,512]{1,0:T(8,128)(2,1)S(1)}, u32[]{:S(2)}, u32[]{:S(2)}) collective-permute-start(bf16[128,512]{1,0:T(8,128)(2,1)} %refs_0_.3), channel_id=1, source_target_pairs={{0,2},{1,3},{2,4},{3,5},{4,6},{5,7},{6,0},{7,1},{8,10},{9,11},{10,... | collective-permute-start | bytes 393224 | tf_op jit(solution)/shard_map/ppermute | solution.py:269
  1.6 8.0 %collective-permute-start.1 = (bf16[128,512]{1,0:T(8,128)(2,1)}, bf16[128,512]{1,0:T(8,128)(2,1)S(1)}, u32[]{:S(2)}, u32[]{:S(2)}) collective-permute-start(bf16[128,512]{1,0:T(8,128)(2,1)} %refs_0_.3), channel_id=1, source_target_pairs={{0,6},{1,7},{2,0},{3,1},{4,2},{5,3},{6,4},{7,5},{8,14},{9,15},{10,... | collective-permute-start | bytes 393224 | tf_op jit(solution)/shard_map/ppermute | solution.py:269
  3.2 8.5 %collective-permute-start.2 = (bf16[128,512]{1,0:T(8,128)(2,1)}, bf16[128,512]{1,0:T(8,128)(2,1)S(1)}, u32[]{:S(2)}, u32[]{:S(2)}) collective-permute-start(bf16[128,512]{1,0:T(8,128)(2,1)} %refs_0_.3), channel_id=1, source_target_pairs={{0,4},{1,5},{2,6},{3,7},{4,0},{5,1},{6,2},{7,3},{8,12},{9,13},{10,... | collective-permute-start | bytes 393224 | tf_op jit(solution)/shard_map/ppermute | solution.py:269
  5.2 6.6 %collective-permute-start.3 = (bf16[128,512]{1,0:T(8,128)(2,1)}, bf16[128,512]{1,0:T(8,128)(2,1)S(1)}, u32[]{:S(2)}, u32[]{:S(2)}) collective-permute-start(bf16[128,512]{1,0:T(8,128)(2,1)} %refs_0_.3), channel_id=1, source_target_pairs={{0,1},{1,0},{2,3},{3,2},{4,5},{5,4},{6,7},{7,6},{8,9},{9,8},{10,11... | collective-permute-start | bytes 393224 | tf_op jit(solution)/shard_map/ppermute | solution.py:273
  5.2 9.1 %collective-permute-start.7 = (bf16[128,512]{1,0:T(8,128)(2,1)}, bf16[128,512]{1,0:T(8,128)(2,1)S(1)}, u32[]{:S(2)}, u32[]{:S(2)}) collective-permute-start(bf16[128,512]{1,0:T(8,128)(2,1)} %refs_5_.1), channel_id=1, source_target_pairs={{0,2},{1,3},{2,4},{3,5},{4,6},{5,7},{6,0},{7,1},{8,10},{9,11},{10,... | collective-permute-start | bytes 393224 | tf_op jit(solution)/shard_map/ppermute | solution.py:269
  6.7 16.1 %copy-start.7 = (bf16[128,512]{1,0:T(8,128)(2,1)}, bf16[128,512]{1,0:T(8,128)(2,1)S(1)}, u32[]{:S(2)}) copy-start(bf16[128,512]{1,0:T(8,128)(2,1)S(1)} %collective-permute-done.refs_1_) | copy-start | bytes 393220
  6.7 7.6 %collective-permute-start.8 = (bf16[128,512]{1,0:T(8,128)(2,1)}, bf16[128,512]{1,0:T(8,128)(2,1)S(1)}, u32[]{:S(2)}, u32[]{:S(2)}) collective-permute-start(bf16[128,512]{1,0:T(8,128)(2,1)} %refs_5_.1), channel_id=1, source_target_pairs={{0,6},{1,7},{2,0},{3,1},{4,2},{5,3},{6,4},{7,5},{8,14},{9,15},{10,... | collective-permute-start | bytes 393224 | tf_op jit(solution)/shard_map/ppermute | solution.py:269
  9.5 13.3 %copy-start.8 = (bf16[128,512]{1,0:T(8,128)(2,1)}, bf16[128,512]{1,0:T(8,128)(2,1)S(1)}, u32[]{:S(2)}) copy-start(bf16[128,512]{1,0:T(8,128)(2,1)S(1)} %collective-permute-done.1.refs_2_) | copy-start | bytes 393220
  9.5 6.8 %collective-permute-start.9 = (bf16[128,512]{1,0:T(8,128)(2,1)}, bf16[128,512]{1,0:T(8,128)(2,1)S(1)}, u32[]{:S(2)}, u32[]{:S(2)}) collective-permute-start(bf16[128,512]{1,0:T(8,128)(2,1)} %refs_5_.1), channel_id=1, source_target_pairs={{0,4},{1,5},{2,6},{3,7},{4,0},{5,1},{6,2},{7,3},{8,12},{9,13},{10,... | collective-permute-start | bytes 393224 | tf_op jit(solution)/shard_map/ppermute | solution.py:269
  11.8 11.0 %copy-start.9 = (bf16[128,512]{1,0:T(8,128)(2,1)}, bf16[128,512]{1,0:T(8,128)(2,1)S(1)}, u32[]{:S(2)}) copy-start(bf16[128,512]{1,0:T(8,128)(2,1)S(1)} %collective-permute-done.2.refs_3_) | copy-start | bytes 393220
  11.8 4.6 %collective-permute-start.4 = (bf16[128,512]{1,0:T(8,128)(2,1)S(1)}, bf16[128,512]{1,0:T(8,128)(2,1)S(1)}, u32[]{:S(2)}, u32[]{:S(2)}) collective-permute-start(bf16[128,512]{1,0:T(8,128)(2,1)S(1)} %collective-permute-done.refs_1_), channel_id=1, source_target_pairs={{0,1},{1,0},{2,3},{3,2},{4,5},{5,4},{6,7},{7,6},{8,9},{9,8},{10,11... | collective-permute-start | bytes 393224 | tf_op jit(solution)/shard_map/ppermute | solution.py:273
  11.8 11.0 %copy-start.10 = (bf16[128,512]{1,0:T(8,128)(2,1)}, bf16[128,512]{1,0:T(8,128)(2,1)S(1)}, u32[]{:S(2)}) copy-start(bf16[128,512]{1,0:T(8,128)(2,1)S(1)} %collective-permute-done.3.refs_4_) | copy-start | bytes 393220
  11.8 5.1 %collective-permute-start.5 = (bf16[128,512]{1,0:T(8,128)(2,1)S(1)}, bf16[128,512]{1,0:T(8,128)(2,1)S(1)}, u32[]{:S(2)}, u32[]{:S(2)}) collective-permute-start(bf16[128,512]{1,0:T(8,128)(2,1)S(1)} %collective-permute-done.1.refs_2_), channel_id=1, source_target_pairs={{0,1},{1,0},{2,3},{3,2},{4,5},{5,4},{6,7},{7,6},{8,9},{9,8},{10,11... | collective-permute-start | bytes 393224 | tf_op jit(solution)/shard_map/ppermute | solution.py:273
  14.3 18.0 %copy-start = (bf16[128,512]{1,0:T(8,128)(2,1)}, bf16[128,512]{1,0:T(8,128)(2,1)S(1)}, u32[]{:S(2)}) copy-start(bf16[128,512]{1,0:T(8,128)(2,1)S(1)} %collective-permute-done.7.refs_9_.refs_6_) | copy-start | bytes 393220
  14.3 8.5 %collective-permute-start.6 = (bf16[128,512]{1,0:T(8,128)(2,1)S(1)}, bf16[128,512]{1,0:T(8,128)(2,1)S(1)}, u32[]{:S(2)}, u32[]{:S(2)}) collective-permute-start(bf16[128,512]{1,0:T(8,128)(2,1)S(1)} %collective-permute-done.2.refs_3_), channel_id=1, source_target_pairs={{0,1},{1,0},{2,3},{3,2},{4,5},{5,4},{6,7},{7,6},{8,9},{9,8},{10,11... | collective-permute-start | bytes 393224 | tf_op jit(solution)/shard_map/ppermute | solution.py:273
  14.3 18.0 %copy-start.1 = (bf16[128,512]{1,0:T(8,128)(2,1)}, bf16[128,512]{1,0:T(8,128)(2,1)S(1)}, u32[]{:S(2)}) copy-start(bf16[128,512]{1,0:T(8,128)(2,1)S(1)} %collective-permute-done.8.refs_10_.refs_7_) | copy-start | bytes 393220
  14.3 17.9 %collective-permute-start.10 = (bf16[128,512]{1,0:T(8,128)(2,1)}, bf16[128,512]{1,0:T(8,128)(2,1)S(1)}, u32[]{:S(2)}, u32[]{:S(2)}) collective-permute-start(bf16[128,512]{1,0:T(8,128)(2,1)} %refs_5_.1), channel_id=1, source_target_pairs={{0,1},{1,0},{2,3},{3,2},{4,5},{5,4},{6,7},{7,6},{8,9},{9,8},{10,11... | collective-permute-start | bytes 393224 | tf_op jit(solution)/shard_map/ppermute | solution.py:273
  16.4 15.9 %copy-start.2 = (bf16[128,512]{1,0:T(8,128)(2,1)}, bf16[128,512]{1,0:T(8,128)(2,1)S(1)}, u32[]{:S(2)}) copy-start(bf16[128,512]{1,0:T(8,128)(2,1)S(1)} %collective-permute-done.9.refs_11_.refs_8_) | copy-start | bytes 393220
  16.4 15.8 %collective-permute-start.11 = (bf16[128,512]{1,0:T(8,128)(2,1)S(1)}, bf16[128,512]{1,0:T(8,128)(2,1)S(1)}, u32[]{:S(2)}, u32[]{:S(2)}) collective-permute-start(bf16[128,512]{1,0:T(8,128)(2,1)S(1)} %collective-permute-done.7.refs_9_.refs_6_), channel_id=1, source_target_pairs={{0,1},{1,0},{2,3},{3,2},{4,5},{5,4},{6,7},{7,6},{8,9},{9,8},{10,11... | collective-permute-start | bytes 393224 | tf_op jit(solution)/shard_map/ppermute | solution.py:273
  16.4 6.5 %copy-start.11 = (bf16[128,512]{1,0:T(8,128)(2,1)}, bf16[128,512]{1,0:T(8,128)(2,1)S(1)}, u32[]{:S(2)}) copy-start(bf16[128,512]{1,0:T(8,128)(2,1)S(1)} %collective-permute-done.4.refs_5_) | copy-start | bytes 393220
  16.4 15.8 %collective-permute-start.12 = (bf16[128,512]{1,0:T(8,128)(2,1)S(1)}, bf16[128,512]{1,0:T(8,128)(2,1)S(1)}, u32[]{:S(2)}, u32[]{:S(2)}) collective-permute-start(bf16[128,512]{1,0:T(8,128)(2,1)S(1)} %collective-permute-done.8.refs_10_.refs_7_), channel_id=1, source_target_pairs={{0,1},{1,0},{2,3},{3,2},{4,5},{5,4},{6,7},{7,6},{8,9},{9,8},{10,11... | collective-permute-start | bytes 393224 | tf_op jit(solution)/shard_map/ppermute | solution.py:273
  16.9 6.0 %copy-start.12 = (bf16[128,512]{1,0:T(8,128)(2,1)}, bf16[128,512]{1,0:T(8,128)(2,1)S(1)}, u32[]{:S(2)}) copy-start(bf16[128,512]{1,0:T(8,128)(2,1)S(1)} %collective-permute-done.5.refs_6_) | copy-start | bytes 393220
  16.9 15.4 %collective-permute-start.13 = (bf16[128,512]{1,0:T(8,128)(2,1)S(1)}, bf16[128,512]{1,0:T(8,128)(2,1)S(1)}, u32[]{:S(2)}, u32[]{:S(2)}) collective-permute-start(bf16[128,512]{1,0:T(8,128)(2,1)S(1)} %collective-permute-done.9.refs_11_.refs_8_), channel_id=1, source_target_pairs={{0,1},{1,0},{2,3},{3,2},{4,5},{5,4},{6,7},{7,6},{8,9},{9,8},{10,11... | collective-permute-start | bytes 393224 | tf_op jit(solution)/shard_map/ppermute | solution.py:273
  30.3 17.5 %collective-permute-start.14 = (f32[200,128]{1,0:T(8,128)}, f32[200,128]{1,0:T(8,128)S(1)}, u32[]{:S(2)}, u32[]{:S(2)}) collective-permute-start(f32[200,128]{1,0:T(8,128)} %get-tuple-element.16), channel_id=1, source_target_pairs={{0,8},{8,0},{16,24},{24,16},{32,40},{40,32},{48,56},{56,48},{64,72... | collective-permute-start | bytes 307208 | tf_op jit(solution)/shard_map/ppermute | solution.py:311
  32.2 0.8 copy-start.5
  32.3 0.8 copy-start.6
  33.1 14.7 %copy-start.14 = (f32[200,128]{1,0:T(8,128)S(1)}, f32[200,128]{1,0:T(8,128)}, u32[]{:S(2)}) copy-start(f32[200,128]{1,0:T(8,128)} %get-tuple-element.16) | copy-start | bytes 307204
  47.8 8.6 %collective-permute-start.15 = (f32[200,128]{1,0:T(8,128)S(1)}, f32[200,128]{1,0:T(8,128)S(1)}, u32[]{:S(2)}, u32[]{:S(2)}) collective-permute-start(f32[200,128]{1,0:T(8,128)S(1)} %select_add_fusion.3), channel_id=1, source_target_pairs={{0,16},{8,24},{16,0},{24,8},{32,48},{40,56},{48,32},{56,40},{64,80... | collective-permute-start | bytes 307208 | tf_op jit(solution)/shard_map/ppermute | solution.py:311
  56.5 8.4 %collective-permute-start.16 = (f32[200,128]{1,0:T(8,128)S(1)}, f32[200,128]{1,0:T(8,128)S(1)}, u32[]{:S(2)}, u32[]{:S(2)}) collective-permute-start(f32[200,128]{1,0:T(8,128)S(1)} %select_add_fusion.2), channel_id=1, source_target_pairs={{0,56},{8,48},{16,40},{24,32},{32,24},{40,16},{48,8},{56,0},{64,12... | collective-permute-start | bytes 307208 | tf_op jit(solution)/shard_map/ppermute | solution.py:311
  65.0 4.9 %collective-permute-start.17 = (f32[200,128]{1,0:T(8,128)S(1)}, f32[200,128]{1,0:T(8,128)S(1)}, u32[]{:S(2)}, u32[]{:S(2)}) collective-permute-start(f32[200,128]{1,0:T(8,128)S(1)} %select_add_fusion.1), channel_id=1, source_target_pairs={{0,64},{8,72},{16,80},{24,88},{32,96},{40,104},{48,112},{56,120},{... | collective-permute-start | bytes 307208 | tf_op jit(solution)/shard_map/ppermute | solution.py:311
  69.9 5.4 %collective-permute-start.18 = (bf16[200,128]{1,0:T(8,128)(2,1)S(1)}, bf16[200,128]{1,0:T(8,128)(2,1)S(1)}, u32[]{:S(2)}, u32[]{:S(2)}) collective-permute-start(bf16[200,128]{1,0:T(8,128)(2,1)S(1)} %select_add_fusion), channel_id=1, source_target_pairs={{0,192},{8,200},{16,208},{24,216},{32,224},{40,232},{48,240},{56,2... | collective-permute-start | bytes 153608 | tf_op jit(solution)/shard_map/ppermute | solution.py:311
  70.5 5.5 %copy-start.15 = (f32[5,3,128]{2,1,0:T(4,128)}, f32[5,3,128]{2,1,0:T(4,128)S(1)}, u32[]{:S(2)}) copy-start(f32[5,3,128]{2,1,0:T(4,128)S(1)} %constant_dynamic-update-slice_fusion.fac_ref) | copy-start | bytes 23044
  (3 other events, 2.0 us)

commit v2 on v1

v2 whole, which is shorter than its diff:
```python
import functools

import jax
import jax.numpy as jnp
from jax import lax
from jax.experimental import pallas as pl
from jax.experimental.pallas import tpu as pltpu
from jax.sharding import PartitionSpec as P

STRETCH = 64
HEADS = 3
WIDTH = 64
STATE = 128
ROWS = HEADS * WIDTH
PIECE = 512
PIECES = 8
TOKENS = PIECE * PIECES
LOCAL = 6
CROSS = 5
FIRST = (0, 32, 48, 56, 60, 62, 63)
HALF = PIECES // 2
U_STATE, U_LOCAL, U_CROSS = True, True, True
VMEM_LIMIT = 20 * 1024 * 1024
BINV, DEC, GRP = 12, 13, 14
F32 = jnp.float32
BF16 = jnp.bfloat16

VMEM = pl.BlockSpec(memory_space=pltpu.VMEM)
SMEM = pl.BlockSpec(memory_space=pltpu.SMEM)
ANY = pl.BlockSpec(memory_space=pl.ANY)


def params():
    return pltpu.CompilerParams(vmem_limit_bytes=VMEM_LIMIT)


def decay_kernel(ld_hbm, lw_hbm, *refs):
    out_ref, ld_ref, lw_ref, ld_sem, lw_sem = refs[-5:]
    ld_copy = pltpu.make_async_copy(ld_hbm, ld_ref, ld_sem)
    lw_copy = pltpu.make_async_copy(lw_hbm, lw_ref, lw_sem)
    ld_copy.start()
    lw_copy.start()
    ld_copy.wait()
    tiles = TOKENS // 128
    lane = lax.broadcasted_iota(jnp.int32, (HEADS, 128), 1)
    local = lane & 63

    def put_factor(slot, value):
        out_ref[GRP + slot // 32, :, pl.ds(slot % 32 * 128, 128)] = value

    runs, grows = [], []
    for i in range(tiles):
        cols = pl.ds(i * 128, 128)
        ld = ld_ref[:, cols]
        cum = ld
        for k in (1, 2, 4, 8, 16, 32):
            cum = cum + jnp.where(local >= k, pltpu.roll(cum, k, 1), 0.0)
        rest = ld
        for k in (1, 2, 4, 8, 16, 32):
            rest = rest + jnp.where(local < 64 - k, pltpu.roll(rest, 128 - k, 1), 0.0)
        grow = jnp.exp(cum)
        grows.append(grow)
        out_ref[DEC, :, cols] = jnp.exp(rest - ld)
        out_ref[BINV, :, cols] = jnp.exp(-cum)
        put_factor(i, jnp.broadcast_to(grow[:, 127:128], (HEADS, 128)))
        left = jnp.broadcast_to(cum[:, 63:64], (HEADS, 128))
        runs.append(cum + jnp.where(lane >= 64, left, 0.0))
    lw_copy.wait()
    for i in range(tiles):
        cols = pl.ds(i * 128, 128)
        out_ref[0, :, cols] = lw_ref[0, :, cols] * grows[i]
        out_ref[1, :, cols] = jnp.where(lane >= 64, lw_ref[1, :, cols] * grows[i], 0.0)
    for level in range(2, LOCAL + 2):
        span = 2 ** (level - 2)
        ends = [jnp.broadcast_to(runs[i][:, 127:128], (HEADS, 128)) for i in range(span - 1, tiles, span)]
        for i in range(tiles):
            cols = pl.ds(i * 128, 128)
            if level <= LOCAL:
                if (i // span) % 2:
                    out_ref[level, :, cols] = lw_ref[level, :, cols] * jnp.exp(runs[i])
                else:
                    out_ref[level, :, cols] = jnp.zeros((HEADS, 128), F32)
            else:
                grow = jnp.exp(runs[i])
                for up in range(CROSS):
                    out_ref[level + up, :, cols] = lw_ref[level + up, :, cols] * grow
        if level <= LOCAL:
            for i in range(tiles // (2 * span)):
                put_factor(FIRST[level - 1] + i, jnp.exp(ends[2 * i + 1]))
            for i in range(tiles):
                if (i // span) % 2:
                    runs[i] = runs[i] + ends[i // span - 1]
        else:
            put_factor(63, ends[0])


def decay_rows(log_decay, level_weight, after):
    return pl.pallas_call(
        decay_kernel,
        out_shape=jax.ShapeDtypeStruct((16, HEADS, TOKENS), F32),
        in_specs=[ANY] * (2 + len(after)),
        out_specs=VMEM,
        scratch_shapes=[
            pltpu.VMEM(log_decay.shape, F32),
            pltpu.VMEM(level_weight.shape, F32),
            pltpu.SemaphoreType.DMA,
            pltpu.SemaphoreType.DMA,
        ],
        compiler_params=params(),
        name="decay_rows",
    )(log_decay, level_weight, *after)


def stack_kernel(own_hbm, p1, p2, p3, *refs):
    out_ref, sem = refs[-2:]
    copy = pltpu.make_async_copy(own_hbm, out_ref.at[0], sem)
    copy.start()
    out_ref[1] = p1[...]
    out_ref[2] = p2[...]
    out_ref[3] = p3[...]
    copy.wait()


def stack(own, parts, after):
    return pl.pallas_call(
        stack_kernel,
        out_shape=jax.ShapeDtypeStruct((HALF, STATE, PIECE), BF16),
        in_specs=[ANY] + [VMEM] * 3 + [ANY] * len(after),
        out_specs=VMEM,
        scratch_shapes=[pltpu.SemaphoreType.DMA],
        compiler_params=params(),
        name="stack_pieces",
    )(own, *parts, *after)


def state_kernel(half, order_ref, v_ref, row_ref, b_ref, *refs):
    if half == 0:
        agg_ref, p_ref = refs
    else:
        p_old, agg_ref, tree_ref, end_ref, p_ref = refs
    lane = lax.broadcasted_iota(jnp.int32, (WIDTH, 128), 1)
    first = lane < 64

    def factor(h, slot):
        if isinstance(slot, int):
            return row_ref[GRP + slot // 32, h : h + 1, pl.ds(slot % 32 * 128, 128)]
        return row_ref[GRP + (slot >> 5), h : h + 1, pl.ds(pl.multiple_of((slot & 31) * 128, 128), 128)]

    def piece(q, carry):
        j = order_ref[half * HALF + q]
        for h in range(HEADS):
            here = slice(h * WIDTH, (h + 1) * WIDTH)
            tops = []
            for a in range(4):
                cols = pl.ds(pl.multiple_of(j * PIECE + a * 128, 128), 128)
                b = b_ref[q, :, a * 128 : (a + 1) * 128].astype(F32)
                v = v_ref[h, :, cols]
                keys = (row_ref[DEC, h : h + 1, cols] * b).astype(BF16)
                zero = jnp.zeros_like(v)
                both = jnp.concatenate([jnp.where(first, v, zero), jnp.where(first, zero, v)], axis=0)
                s = lax.dot_general(both, keys, (((1,), (1,)), ((), ())), preferred_element_type=F32)
                agg_ref[q, a, here, :] = s[:WIDTH].astype(BF16)
                tops.append(factor(h, j * 4 + a) * s[:WIDTH] + s[WIDTH:])
            agg_ref[q, 4, here, :] = tops[0].astype(BF16)
            agg_ref[q, 5, here, :] = tops[2].astype(BF16)
            lo = factor(h, FIRST[1] + j * 2) * tops[0] + tops[1]
            hi = factor(h, FIRST[1] + j * 2 + 1) * tops[2] + tops[3]
            agg_ref[q, 6, here, :] = lo.astype(BF16)
            p_ref[j, here, :] = factor(h, FIRST[2] + j) * lo + hi
        return carry

    lax.fori_loop(0, HALF, piece, 0, unroll=U_STATE)
    if half == 0:
        return
    for q in range(HALF):
        j = order_ref[q]
        p_ref[j] = p_old[j]
    for h in range(HEADS):
        here = slice(h * WIDTH, (h + 1) * WIDTH)
        tops = [p_ref[j, here, :] for j in range(PIECES)]
        for level in range(4, LOCAL + 1):
            nxt = []
            for i in range(len(tops) // 2):
                slot = FIRST[level - 1] + i
                tree_ref[slot - FIRST[3], here, :] = tops[2 * i].astype(BF16)
                nxt.append(factor(h, slot) * tops[2 * i] + tops[2 * i + 1])
            tops = nxt
        end_ref[here, :] = tops[0]
    end_ref[ROWS : ROWS + 8, :] = jnp.concatenate([row_ref[GRP + 1, :, 31 * 128 :], jnp.zeros((5, 128), F32)], axis=0)


def block_states(half, order, values, rows, b, old=()):
    agg = jax.ShapeDtypeStruct((HALF, 7, ROWS, STATE), BF16)
    tops = jax.ShapeDtypeStruct((PIECES, ROWS, STATE), F32)
    end = [jax.ShapeDtypeStruct((7, ROWS, STATE), BF16), jax.ShapeDtypeStruct((ROWS + 8, STATE), F32)]
    return pl.pallas_call(
        functools.partial(state_kernel, half),
        out_shape=[agg, tops] if half == 0 else [agg] + end,
        in_specs=[SMEM] + [VMEM] * (3 + len(old)),
        out_specs=[VMEM] * (2 if half == 0 else 3),
        scratch_shapes=[] if half == 0 else [pltpu.VMEM(tops.shape, F32)],
        compiler_params=params(),
        name="block_states",
    )(order, values, rows, b, *old)


def local_kernel(half, order_ref, v_ref, sc_ref, agg_ref, tree_ref, b_ref, c_ref, own_ref, *refs):
    out_ref, same_ref = refs[-2:]
    same_ref[...] = own_ref[...]
    s_id = lax.broadcasted_iota(jnp.int32, (128, 128), 0)
    t_id = lax.broadcasted_iota(jnp.int32, (128, 128), 1)
    keep = (s_id <= t_id) & ((s_id >> 6) == (t_id >> 6))

    def piece(q, carry):
        j = order_ref[half * HALF + q]
        base = j * PIECE
        for a in range(4):
            cols = pl.ds(pl.multiple_of(base + a * 128, 128), 128)
            mine = slice(a * 128, (a + 1) * 128)
            c = c_ref[q, :, mine]
            b = b_ref[q, :, mine]
            scores = lax.dot_general(b, c, (((0,), (0,)), ((), ())), preferred_element_type=F32)
            scores = jnp.where(keep, scores, 0.0)
            slots = [(1, a)]
            if a & 1:
                slots.append((2, 4 + a // 2))
            if a & 2:
                slots.append((3, 6))
            reads = [(level, jnp.dot(agg_ref[q, slot], c, preferred_element_type=F32)) for level, slot in slots]
            for h in range(HEADS):
                here = slice(h * WIDTH, (h + 1) * WIDTH)
                col = jnp.transpose(jnp.broadcast_to(sc_ref[BINV, h : h + 1, cols], (128, 128)))
                mix = ((sc_ref[0, h : h + 1, cols] * scores) * col).astype(BF16)
                acc = jnp.dot(v_ref[h, :, cols], mix, preferred_element_type=F32)
                for level, r in reads:
                    acc = acc + sc_ref[level, h : h + 1, cols] * r[here, :]
                out_ref[q, h, :, mine] = acc
        for level in range(4, LOCAL + 1):
            bit = level - 4

            @pl.when(((j >> bit) & 1) == 1)
            def _():
                slot = FIRST[level - 1] - FIRST[3] + (j >> (bit + 1))
                for a in range(2):
                    cols = pl.ds(pl.multiple_of(base + a * 256, 256), 256)
                    mine = slice(a * 256, (a + 1) * 256)
                    r = jnp.dot(tree_ref[slot], c_ref[q, :, mine], preferred_element_type=F32)
                    for h in range(HEADS):
                        here = slice(h * WIDTH, (h + 1) * WIDTH)
                        out_ref[q, h, :, mine] += sc_ref[level, h : h + 1, cols] * r[here, :]

        return carry

    lax.fori_loop(0, HALF, piece, 0, unroll=U_LOCAL)


def local_part(half, order, values, rows, agg, tree, b, c, own):
    return pl.pallas_call(
        functools.partial(local_kernel, half),
        out_shape=[
            jax.ShapeDtypeStruct((HALF, HEADS, WIDTH, PIECE), F32),
            jax.ShapeDtypeStruct(own.shape, own.dtype),
        ],
        in_specs=[SMEM] + [VMEM] * 7,
        out_specs=[VMEM] * 2,
        compiler_params=params(),
        name="local_part",
    )(order, values, rows, agg, tree, b, c, own)


def cross_kernel(rounds, last, order_ref, bits_ref, sc_ref, *refs):
    n = len(rounds)
    s_refs, pre_refs = refs[:n], refs[n : 2 * n]
    c_refs = refs[2 * n : 2 * n + 2]
    loc_refs = refs[2 * n + 2 : 2 * n + 4]
    outs = refs[2 * n + 4 :]
    if not last:
        own_ref, outs, same_ref = outs[0], outs[1:3], outs[3]
        same_ref[...] = own_ref[...]
    facs = []
    for k, r in enumerate(rounds):
        row = jnp.where(bits_ref[r] == 1, jnp.exp(pre_refs[k][:HEADS, :]), 0.0)
        facs.append(jnp.concatenate([row, row], axis=1))
    for g in range(2):

        def piece(q, carry):
            base = order_ref[g * HALF + q] * PIECE
            for a in range(2):
                cols = pl.ds(pl.multiple_of(base + a * 256, 256), 256)
                mine = slice(a * 256, (a + 1) * 256)
                c = c_refs[g][q, :, mine]
                accs = [loc_refs[g][q, h, :, mine] for h in range(HEADS)]
                for k, r in enumerate(rounds):
                    prod = jnp.dot(s_refs[k][...], c, preferred_element_type=F32)
                    for h in range(HEADS):
                        here = slice(h * WIDTH, (h + 1) * WIDTH)
                        row = sc_ref[1 + LOCAL + r, h : h + 1, cols] * facs[k][h : h + 1, :]
                        accs[h] = accs[h] + row * prod[here, :]
                for h in range(HEADS):
                    if last:
                        outs[0][h, :, cols] = accs[h].astype(BF16)
                    else:
                        outs[g][q, h, :, mine] = accs[h]
            return carry

        lax.fori_loop(0, HALF, piece, 0, unroll=U_CROSS)


def cross_part(rounds, order, bits, rows, states, pres, c_stacks, locs, own=None):
    last = own is None
    full = jax.ShapeDtypeStruct((HEADS, WIDTH, TOKENS), BF16)
    same = [jax.ShapeDtypeStruct(x.shape, x.dtype) for x in list(locs) + ([] if last else [own])]
    first_loc = 3 + 2 * len(rounds) + 2
    return pl.pallas_call(
        functools.partial(cross_kernel, rounds, last),
        out_shape=full if last else same,
        in_specs=[SMEM] * 2 + [VMEM] * (1 + 2 * len(rounds) + 4 + (0 if last else 1)),
        out_specs=VMEM if last else [VMEM] * 3,
        input_output_aliases={} if last else {first_loc + i: i for i in range(2)},
        compiler_params=params(),
        name="cross_part",
    )(order, bits, rows, *states, *pres, *c_stacks, *locs, *([] if last else [own]))


def combine(r, bits, own, got, pre):
    right = bits[r] == 1
    own_tot = own[ROWS:]
    got_tot = got[ROWS:]
    scale = jnp.exp(jnp.where(right, own_tot, got_tot))[:HEADS]
    scale = jnp.broadcast_to(scale[:, None], (HEADS, WIDTH, STATE)).reshape(ROWS, STATE)
    scale = jnp.concatenate([scale, jnp.ones((8, STATE), F32)], axis=0)
    new = scale * jnp.where(right, got, own) + jnp.where(right, own, got)
    if r == CROSS - 2:
        new = new[:ROWS].astype(BF16)
    return new, got[:ROWS].astype(BF16), pre + jnp.where(right, got_tot, 0.0)


def y_shift(x, k):
    return lax.ppermute(x, "head", [(i, ((i // 2 + k) % 4) * 2 + i % 2) for i in range(8)])


def other_core(x):
    return lax.ppermute(x, "head", [(i, i ^ 1) for i in range(8)])


def partner(r, i):
    x, z = i // 8, i % 8
    if r == 0:
        z = z ^ 1
    elif r == 1:
        z = z ^ 2
    elif r == 2:
        z = 7 - z
    elif r == 3:
        x = x ^ 1
    else:
        x = 3 - x
    return x * 8 + z


def exchange(r, x):
    return lax.ppermute(x, "seq", [(i, partner(r, i)) for i in range(32)])


def on_device(values, b_rows, c_rows, log_decay, level_weight):
    me = lax.axis_index("head")
    index = lax.axis_index("seq")
    q = lax.iota(jnp.int32, PIECES)
    turn = q & 3
    turn = turn ^ (turn >> 1)
    order = ((((me >> 1) - turn) & 3) << 1) | ((me & 1) ^ (q >> 2))
    bits = (index >> lax.iota(jnp.int32, CROSS)) & 1
    b1, c3 = y_shift(b_rows, 1), y_shift(c_rows, 3)
    b3, c1 = y_shift(b_rows, 3), y_shift(c_rows, 1)
    b2, c2 = y_shift(b1, 1), y_shift(c3, 3)
    rows = decay_rows(log_decay, level_weight, [b1, c3])
    b_near = stack(b_rows, [b1, b3, b2], [rows])
    b_far = other_core(b_near)
    c_near = stack(c_rows, [c1, c3, c2], [b_near])
    c_far = other_core(c_near)
    agg_near, tops = block_states(0, order, values, rows, b_near)
    agg_far, tree, own = block_states(1, order, values, rows, b_far, [tops])
    c_stacks = [c_near, c_far]
    pre = jnp.zeros((8, STATE), F32)
    pres, states, locs = [], [], []
    for r in range(CROSS):
        got = exchange(r, own)
        pres.append(pre)
        if r == 0:
            loc, own = local_part(0, order, values, rows, agg_near, tree, b_near, c_near, own)
            locs.append(loc)
        elif r == 1:
            loc, own = local_part(1, order, values, rows, agg_far, tree, b_far, c_far, own)
            locs.append(loc)
        elif r == 2:
            *locs, own = cross_part((0, 1), order, bits, rows, states, pres[:2], c_stacks, locs, own)
        elif r == 4:
            *locs, own = cross_part((2, 3), order, bits, rows, states[2:], pres[2:4], c_stacks, locs, own)
            return cross_part((4,), order, bits, rows, [got], [pre], c_stacks, locs)
        own, st, pre = combine(r, bits, own, got, pre)
        states.append(st)


def solution(mesh):
    return jax.shard_map(
        on_device,
        mesh=mesh,
        in_specs=(
            P("head", None, "seq"),
            P(None, ("seq", "head")),
            P(None, ("seq", "head")),
            P("head", "seq"),
            P(None, "head", "seq"),
        ),
        out_specs=P("head", None, "seq"),
        check_vma=False,
    )
```

time: 83 us -> 61.3 us (0.74)
  waiting for transfers between devices: 20.2 us -> 11.3 us
  Pallas kernels: 33.6 us -> 24.9 us
  starting transfers between devices: 23.5 us -> 19.2 us
  between operations: 0.22 us -> 2.81 us
  local copies, waits for them, and re-layouts: 5.24 us -> 2.72 us
    pallas_call x4 -> x10, Pallas kernels: 33.6 us -> 24.9 us  [the longest x2 11.1 us: local_part(): pl.pallas_call(functools.partial(local_kernel, half), out_shape=[jax.Shap...]
    ppermute x5, waiting for transfers between devices: 15 us -> 7.52 us  [exchange(): return lax.ppermute(x, 'seq', [(i, partner(r, i)) for i in range(32)])]
    slice x5 -> x9, local copies, waits for them, and re-layouts: 3.12 us -> 0.69 us  [the longest x1 0.65 us: combine(): right = bits[r] == 1]
    ppermute x6, starting transfers between devices: 10.2 us -> 8.66 us  [y_shift(): lax.ppermute(x, 'head', [(i, (i // 2 + k) % 4 * 2 + i % 2) for i in range...]
    ppermute x8 -> x2, starting transfers between devices: 1.61 us -> 0.19 us  [other_core(): return lax.ppermute(x, 'head', [(i, i ^ 1) for i in range(8)])]
    ppermute x5, starting transfers between devices: 11.7 us -> 10.3 us  [exchange(): return lax.ppermute(x, 'seq', [(i, partner(r, i)) for i in range(32)])]
    ppermute x6, waiting for transfers between devices: 5.11 us -> 3.8 us  [y_shift(): lax.ppermute(x, 'head', [(i, (i // 2 + k) % 4 * 2 + i % 2) for i in range...]
    unnamed x33 -> x10, local copies, waits for them, and re-layouts: 1.43 us -> 1.99 us
  transfers between devices with their start and end apart: 19 -> 13, of which waited for: 8 -> 6; matrix products, arithmetic and copies ran while one was open for 4% -> 1% of each run, Pallas kernels for 32% -> 37%
where the time goes in v2:
time: 61.3 us; the launch traced here: 61 us
  Pallas kernels  24.9 us (41%)
  starting transfers between devices  19.2 us (31%)
  waiting for transfers between devices  11.3 us (18%)
  between operations  2.81 us (5%)
  local copies, waits for them, and re-layouts  2.72 us (4%)
    pallas_call x2, Pallas kernels, local_part(): pl.pallas_call(functools.partial(local_kernel, half), out_shape=[jax.Shap...  11.1 us
    ppermute x5, starting transfers between devices, exchange(): return lax.ppermute(x, 'seq', [(i, partner(r, i)) for i in range(32)])  10.3 us
    ppermute x6, starting transfers between devices, y_shift(): lax.ppermute(x, 'head', [(i, (i // 2 + k) % 4 * 2 + i % 2) for i in range...  8.66 us
    ppermute x5, waiting for transfers between devices, exchange(): return lax.ppermute(x, 'seq', [(i, partner(r, i)) for i in range(32)])  7.52 us
    pallas_call x3, Pallas kernels, cross_part(): pl.pallas_call(functools.partial(cross_kernel, rounds, last), out_shape=f...  7.5 us
    pallas_call x2, Pallas kernels, block_states(): pl.pallas_call(functools.partial(state_kernel, half), out_shape=[agg, top...  4.14 us
    ppermute x6, waiting for transfers between devices, y_shift(): lax.ppermute(x, 'head', [(i, (i // 2 + k) % 4 * 2 + i % 2) for i in range...  3.8 us
    unnamed x10, local copies, waits for them, and re-layouts  1.99 us
  transfers between devices with their start and end apart: 13, of which 6 were waited for; matrix products, arithmetic and copies ran while one was open for 1% of the time, Pallas kernels for 37%

profile of v2, /device:TPU:6, one launch (start us, length us, event | category | flops | bytes accessed | tf_op | source)
XLA Modules:
  0.0 61.0 jit_solution(8282809771468717900)
XLA Ops:
  0.0 1.6 %collective-permute-start = (bf16[128,512]{1,0:T(8,128)(2,1)}, bf16[128,512]{1,0:T(8,128)(2,1)S(1)}, u32[]{:S(2)}, u32[]{:S(2)}) collective-permute-start(bf16[128,512]{1,0:T(8,128)(2,1)} %own_hbm.2), channel_id=1, source_target_pairs={{0,2},{1,3},{2,4},{3,5},{4,6},{5,7},{6,0},{7,1},{8,10},{9,11},{10,... | collective-permute-start | bytes 393224 | tf_op jit(solution)/shard_map/ppermute | solution.py:339
  1.6 1.7 %collective-permute-start.1 = (bf16[128,512]{1,0:T(8,128)(2,1)}, bf16[128,512]{1,0:T(8,128)(2,1)S(1)}, u32[]{:S(2)}, u32[]{:S(2)}) collective-permute-start(bf16[128,512]{1,0:T(8,128)(2,1)} %own_hbm.3), channel_id=1, source_target_pairs={{0,6},{1,7},{2,0},{3,1},{4,2},{5,3},{6,4},{7,5},{8,14},{9,15},{10,... | collective-permute-start | bytes 393224 | tf_op jit(solution)/shard_map/ppermute | solution.py:339
  3.2 1.8 %collective-permute-start.2 = (bf16[128,512]{1,0:T(8,128)(2,1)}, bf16[128,512]{1,0:T(8,128)(2,1)S(1)}, u32[]{:S(2)}, u32[]{:S(2)}) collective-permute-start(bf16[128,512]{1,0:T(8,128)(2,1)} %own_hbm.2), channel_id=1, source_target_pairs={{0,6},{1,7},{2,0},{3,1},{4,2},{5,3},{6,4},{7,5},{8,14},{9,15},{10,... | collective-permute-start | bytes 393224 | tf_op jit(solution)/shard_map/ppermute | solution.py:339
  5.0 1.7 %collective-permute-done.refs_0_.p1 = bf16[128,512]{1,0:T(8,128)(2,1)S(1)} collective-permute-done((bf16[128,512]{1,0:T(8,128)(2,1)}, bf16[128,512]{1,0:T(8,128)(2,1)S(1)}, u32[]{:S(2)}, u32[]{:S(2)}) %collective-permute-start) | collective-permute-done | bytes 131104 | tf_op jit(solution)/shard_map/ppermute | solution.py:339
  6.7 0.3 collective-permute-start.3
  7.0 1.1 %collective-permute-done.1.refs_1_.p2 = bf16[128,512]{1,0:T(8,128)(2,1)S(1)} collective-permute-done((bf16[128,512]{1,0:T(8,128)(2,1)}, bf16[128,512]{1,0:T(8,128)(2,1)S(1)}, u32[]{:S(2)}, u32[]{:S(2)}) %collective-permute-start.1) | collective-permute-done | bytes 131104 | tf_op jit(solution)/shard_map/ppermute | solution.py:339
  8.1 1.1 %copy-done.1 = f32[12,3,4096]{2,1,0:T(4,128)S(1)} copy-done((f32[12,3,4096]{2,1,0:T(4,128)S(1)}, f32[12,3,4096]{2,1,0:T(4,128)}, u32[]{:S(2)}) %copy-start.1) | copy-done | bytes 589848
  9.3 0.8 %copy-done.4 = f32[3,4096]{1,0:T(4,128)S(1)} copy-done((f32[3,4096]{1,0:T(4,128)S(1)}, f32[3,4096]{1,0:T(4,128)}, u32[]{:S(2)}) %copy-start.4) | copy-done | bytes 49176
  10.1 1.7 %decay_rows.1.refs_0_.row_ref.sc_ref = f32[16,3,4096]{2,1,0:T(4,128)S(1)} custom-call(f32[3,4096]{1,0:T(4,128)S(1)} %copy-done.4, f32[12,3,4096]{2,1,0:T(4,128)S(1)} %copy-done.1, bf16[128,512]{1,0:T(8,128)(2,1)S(1)} %collective-permute-done.refs_0_.p1, bf16[128,512]{1,0:T(8,128)(2,1)S(1)} %collective-permute-done.1.refs_1_.p2), custom_call_target="tpu_custom_call" | custom-call | tf_op jit(solution)/shard_map/decay_rows/pallas_call | solution.py:98
  11.9 1.0 %collective-permute-done.3.p3 = bf16[128,512]{1,0:T(8,128)(2,1)S(1)} collective-permute-done((bf16[128,512]{1,0:T(8,128)(2,1)S(1)}, bf16[128,512]{1,0:T(8,128)(2,1)S(1)}, u32[]{:S(2)}, u32[]{:S(2)}) %collective-permute-start.3) | collective-permute-done | bytes 131104 | tf_op jit(solution)/shard_map/ppermute | solution.py:339
  12.9 0.2 stack_pieces.2.b_ref.refs_0_
  13.1 0.1 collective-permute-start.4
  13.2 1.1 %collective-permute-start.6 = (bf16[128,512]{1,0:T(8,128)(2,1)S(1)}, bf16[128,512]{1,0:T(8,128)(2,1)S(1)}, u32[]{:S(2)}, u32[]{:S(2)}) collective-permute-start(bf16[128,512]{1,0:T(8,128)(2,1)S(1)} %copy-done.3), channel_id=1, source_target_pairs={{0,2},{1,3},{2,4},{3,5},{4,6},{5,7},{6,0},{7,1},{8,10},{9,11},{10,... | collective-permute-start | bytes 393224 | tf_op jit(solution)/shard_map/ppermute | solution.py:339
  14.4 2.2 %collective-permute-start.7 = (bf16[128,512]{1,0:T(8,128)(2,1)S(1)}, bf16[128,512]{1,0:T(8,128)(2,1)S(1)}, u32[]{:S(2)}, u32[]{:S(2)}) collective-permute-start(bf16[128,512]{1,0:T(8,128)(2,1)S(1)} %collective-permute-done.1.refs_1_.p2), channel_id=1, source_target_pairs={{0,6},{1,7},{2,0},{3,1},{4,2},{5,3},{6,4},{7,5},{8,14},{9,15},{10,... | collective-permute-start | bytes 393224 | tf_op jit(solution)/shard_map/ppermute | solution.py:339
  16.5 1.8 %block_states.2 = (bf16[4,7,192,128]{3,2,1,0:T(8,128)(2,1)S(1)}, f32[8,192,128]{2,1,0:T(8,128)S(1)}) custom-call(s32[8]{0:T(128)S(1)} %fusion.6.order_ref, bf16[3,64,4096]{2,1,0:T(8,128)(2,1)S(1)} %copy-done, f32[16,3,4096]{2,1,0:T(4,128)S(1)} %decay_rows.1.refs_0_.row_ref.sc_ref, bf16[4,128,512]{2,1,0:T(8,128)(2,1)S(1)} %stack_pieces.2.b_ref.refs_0_), custom_call_target="tpu_custom_call" | custom-call | tf_op jit(solution)/shard_map/block_states/pallas_call | solution.py:196
  18.3 2.4 %block_states.3 = (bf16[4,7,192,128]{3,2,1,0:T(8,128)(2,1)S(1)}, bf16[7,192,128]{2,1,0:T(8,128)(2,1)S(1)}, f32[200,128]{1,0:T(8,128)S(1)}) custom-call(s32[8]{0:T(128)S(1)} %fusion.6.order_ref, bf16[3,64,4096]{2,1,0:T(8,128)(2,1)S(1)} %copy-done, f32[16,3,4096]{2,1,0:T(4,128)S(1)} %decay_rows.1.refs_0_.row_ref.sc_ref, ...), custom_call_target="tpu_custom_call" | custom-call | tf_op jit(solution)/shard_map/block_states/pallas_call | solution.py:196
  20.7 2.0 %collective-permute-start.5 = (f32[200,128]{1,0:T(8,128)S(1)}, f32[200,128]{1,0:T(8,128)S(1)}, u32[]{:S(2)}, u32[]{:S(2)}) collective-permute-start(f32[200,128]{1,0:T(8,128)S(1)} %get-tuple-element.20.own_ref), channel_id=1, source_target_pairs={{0,8},{8,0},{16,24},{24,16},{32,40},{40,32},{48,56},{56,48},{64,72... | collective-permute-start | bytes 307208 | tf_op jit(solution)/shard_map/ppermute | solution.py:362
  22.7 0.6 %fusion.7 = (s32[1]{0:T(128)}, s32[1]{0:T(128)}, s32[1]{0:T(128)}, s32[1]{0:T(128)}) fusion(s32[5]{0:T(128)S(1)} %shift-right-arithmetic_and_fusion.bits_ref), kind=kLoop, calls=%fused_computation.25 | loop fusion | bytes 32 | tf_op jit(solution)/shard_map/slice | solution.py:326
  23.9 0.2 stack_pieces.3.c_ref.refs_4_.refs_2_
  24.1 0.1 collective-permute-start.9
  24.2 5.0 %local_part.2 = (f32[4,3,64,512]{3,2,1,0:T(8,128)S(1)}, f32[200,128]{1,0:T(8,128)S(1)}) custom-call(s32[8]{0:T(128)S(1)} %fusion.6.order_ref, bf16[3,64,4096]{2,1,0:T(8,128)(2,1)S(1)} %copy-done, f32[16,3,4096]{2,1,0:T(4,128)S(1)} %decay_rows.1.refs_0_.row_ref.sc_ref, bf16[4,7,192,128]{3,2,1,0:T(8,128)(2,1)S(1)} %get-tuple-element.21.agg_ref, ...), custom_call_target="tpu_custom_call" | custom-call | tf_op jit(solution)/shard_map/local_part/pallas_call | solution.py:258
  29.3 3.4 %collective-permute-start.8 = (f32[200,128]{1,0:T(8,128)S(1)}, f32[200,128]{1,0:T(8,128)S(1)}, u32[]{:S(2)}, u32[]{:S(2)}) collective-permute-start(f32[200,128]{1,0:T(8,128)S(1)} %select_add_fusion.2.own_ref), channel_id=1, source_target_pairs={{0,16},{8,24},{16,0},{24,8},{32,48},{40,56},{48,32},{56,40},{64,80... | collective-permute-start | bytes 307208 | tf_op jit(solution)/shard_map/ppermute | solution.py:362
  33.4 6.1 %local_part.3 = (f32[4,3,64,512]{3,2,1,0:T(8,128)S(1)}, f32[200,128]{1,0:T(8,128)S(1)}) custom-call(s32[8]{0:T(128)S(1)} %fusion.6.order_ref, bf16[3,64,4096]{2,1,0:T(8,128)(2,1)S(1)} %copy-done, f32[16,3,4096]{2,1,0:T(4,128)S(1)} %decay_rows.1.refs_0_.row_ref.sc_ref, bf16[4,7,192,128]{3,2,1,0:T(8,128)(2,1)S(1)} %get-tuple-element.25.agg_ref, ...), custom_call_target="tpu_custom_call" | custom-call | tf_op jit(solution)/shard_map/local_part/pallas_call | solution.py:258
  39.6 3.5 %collective-permute-start.10 = (f32[200,128]{1,0:T(8,128)S(1)}, f32[200,128]{1,0:T(8,128)S(1)}, u32[]{:S(2)}, u32[]{:S(2)}) collective-permute-start(f32[200,128]{1,0:T(8,128)S(1)} %select_add_fusion.1.refs_8_), channel_id=1, source_target_pairs={{0,56},{8,48},{16,40},{24,32},{32,24},{40,16},{48,8},{56,0},{64,12... | collective-permute-start | bytes 307208 | tf_op jit(solution)/shard_map/ppermute | solution.py:362
  43.8 2.3 %cross_part.3 = (f32[4,3,64,512]{3,2,1,0:T(8,128)S(1)}, f32[4,3,64,512]{3,2,1,0:T(8,128)S(1)}, f32[200,128]{1,0:T(8,128)S(1)}) custom-call(s32[8]{0:T(128)S(1)} %fusion.6.order_ref, s32[5]{0:T(128)S(1)} %shift-right-arithmetic_and_fusion.bits_ref, ...), custom_call_target="tpu_custom_call", output_to_operand_aliasing={{0}: (9, {}), {1}: (10, {})} | custom-call | tf_op jit(solution)/shard_map/cross_part/pallas_call | solution.py:314
  46.1 2.3 %collective-permute-done.10 = f32[200,128]{1,0:T(8,128)S(1)} collective-permute-done((f32[200,128]{1,0:T(8,128)S(1)}, f32[200,128]{1,0:T(8,128)S(1)}, u32[]{:S(2)}, u32[]{:S(2)}) %collective-permute-start.10) | collective-permute-done | bytes 102432 | tf_op jit(solution)/shard_map/ppermute | solution.py:362
  48.5 0.9 %collective-permute-start.11 = (f32[200,128]{1,0:T(8,128)S(1)}, f32[200,128]{1,0:T(8,128)S(1)}, u32[]{:S(2)}, u32[]{:S(2)}) collective-permute-start(f32[200,128]{1,0:T(8,128)S(1)} %select_add_fusion), channel_id=1, source_target_pairs={{0,64},{8,72},{16,80},{24,88},{32,96},{40,104},{48,112},{56,120},{... | collective-permute-start | bytes 307208 | tf_op jit(solution)/shard_map/ppermute | solution.py:362
  50.0 3.2 %collective-permute-done.11 = f32[200,128]{1,0:T(8,128)S(1)} collective-permute-done((f32[200,128]{1,0:T(8,128)S(1)}, f32[200,128]{1,0:T(8,128)S(1)}, u32[]{:S(2)}, u32[]{:S(2)}) %collective-permute-start.11) | collective-permute-done | bytes 102432 | tf_op jit(solution)/shard_map/ppermute | solution.py:362
  53.3 0.6 collective-permute-start.12
  53.9 2.8 %cross_part.4 = (f32[4,3,64,512]{3,2,1,0:T(8,128)S(1)}, f32[4,3,64,512]{3,2,1,0:T(8,128)S(1)}, bf16[192,128]{1,0:T(8,128)(2,1)}) custom-call(s32[8]{0:T(128)S(1)} %fusion.6.order_ref, s32[5]{0:T(128)S(1)} %shift-right-arithmetic_and_fusion.bits_ref, ...), custom_call_target="tpu_custom_call", output_to_operand_aliasing={{0}: (9, {}), {1}: (10, {})} | custom-call | tf_op jit(solution)/shard_map/cross_part/pallas_call | solution.py:314
  56.7 2.0 %collective-permute-done.12.refs_0_ = bf16[192,128]{1,0:T(8,128)(2,1)S(1)} collective-permute-done((bf16[192,128]{1,0:T(8,128)(2,1)S(1)}, bf16[192,128]{1,0:T(8,128)(2,1)S(1)}, u32[]{:S(2)}, u32[]{:S(2)}) %collective-permute-start.12) | collective-permute-done | bytes 49184 | tf_op jit(solution)/shard_map/ppermute | solution.py:362
  58.7 2.4 %cross_part.5 = bf16[3,64,4096]{2,1,0:T(8,128)(2,1)} custom-call(s32[8]{0:T(128)S(1)} %fusion.6.order_ref, s32[5]{0:T(128)S(1)} %shift-right-arithmetic_and_fusion.bits_ref, f32[16,3,4096]{2,1,0:T(4,128)S(1)} %decay_rows.1.refs_0_.row_ref.sc_ref, bf16[192,128]{1,0:T(8,128)(2,1)S(1)} %collective-permute-done.12.refs_0_, ...), custom_call_target="tpu_custom_call" | custom-call | tf_op jit(solution)/shard_map/cross_part/pallas_call | solution.py:314
  (38 shorter events, 0.3 us)
Async XLA Ops:
  0.0 6.7 %collective-permute-start = (bf16[128,512]{1,0:T(8,128)(2,1)}, bf16[128,512]{1,0:T(8,128)(2,1)S(1)}, u32[]{:S(2)}, u32[]{:S(2)}) collective-permute-start(bf16[128,512]{1,0:T(8,128)(2,1)} %own_hbm.2), channel_id=1, source_target_pairs={{0,2},{1,3},{2,4},{3,5},{4,6},{5,7},{6,0},{7,1},{8,10},{9,11},{10,... | collective-permute-start | bytes 393224 | tf_op jit(solution)/shard_map/ppermute | solution.py:339
  1.6 6.6 %collective-permute-start.1 = (bf16[128,512]{1,0:T(8,128)(2,1)}, bf16[128,512]{1,0:T(8,128)(2,1)S(1)}, u32[]{:S(2)}, u32[]{:S(2)}) collective-permute-start(bf16[128,512]{1,0:T(8,128)(2,1)} %own_hbm.3), channel_id=1, source_target_pairs={{0,6},{1,7},{2,0},{3,1},{4,2},{5,3},{6,4},{7,5},{8,14},{9,15},{10,... | collective-permute-start | bytes 393224 | tf_op jit(solution)/shard_map/ppermute | solution.py:339
  3.2 8.6 %collective-permute-start.2 = (bf16[128,512]{1,0:T(8,128)(2,1)}, bf16[128,512]{1,0:T(8,128)(2,1)S(1)}, u32[]{:S(2)}, u32[]{:S(2)}) collective-permute-start(bf16[128,512]{1,0:T(8,128)(2,1)} %own_hbm.2), channel_id=1, source_target_pairs={{0,6},{1,7},{2,0},{3,1},{4,2},{5,3},{6,4},{7,5},{8,14},{9,15},{10,... | collective-permute-start | bytes 393224 | tf_op jit(solution)/shard_map/ppermute | solution.py:339
  6.7 6.2 %collective-permute-start.3 = (bf16[128,512]{1,0:T(8,128)(2,1)S(1)}, bf16[128,512]{1,0:T(8,128)(2,1)S(1)}, u32[]{:S(2)}, u32[]{:S(2)}) collective-permute-start(bf16[128,512]{1,0:T(8,128)(2,1)S(1)} %collective-permute-done.refs_0_.p1), channel_id=1, source_target_pairs={{0,2},{1,3},{2,4},{3,5},{4,6},{5,7},{6,0},{7,1},{8,10},{9,11},{10,... | collective-permute-start | bytes 393224 | tf_op jit(solution)/shard_map/ppermute | solution.py:339
  8.1 1.1 %copy-start.1 = (f32[12,3,4096]{2,1,0:T(4,128)S(1)}, f32[12,3,4096]{2,1,0:T(4,128)}, u32[]{:S(2)}) copy-start(f32[12,3,4096]{2,1,0:T(4,128)} %lw_hbm.1) | copy-start | bytes 1769476
  9.3 0.8 %copy-start.4 = (f32[3,4096]{1,0:T(4,128)S(1)}, f32[3,4096]{1,0:T(4,128)}, u32[]{:S(2)}) copy-start(f32[3,4096]{1,0:T(4,128)} %ld_hbm.1) | copy-start | bytes 147460
  10.1 2.8 %copy-start.2 = (bf16[128,512]{1,0:T(8,128)(2,1)S(1)}, bf16[128,512]{1,0:T(8,128)(2,1)}, u32[]{:S(2)}) copy-start(bf16[128,512]{1,0:T(8,128)(2,1)} %own_hbm.2) | copy-start | bytes 393220
  11.9 1.3 %copy-start.3 = (bf16[128,512]{1,0:T(8,128)(2,1)S(1)}, bf16[128,512]{1,0:T(8,128)(2,1)}, u32[]{:S(2)}) copy-start(bf16[128,512]{1,0:T(8,128)(2,1)} %own_hbm.3) | copy-start | bytes 393220
  11.9 4.7 %copy-start = (bf16[3,64,4096]{2,1,0:T(8,128)(2,1)S(1)}, bf16[3,64,4096]{2,1,0:T(8,128)(2,1)}, u32[]{:S(2)}) copy-start(bf16[3,64,4096]{2,1,0:T(8,128)(2,1)} %v_ref.7) | copy-start | bytes 4718596
  13.1 5.2 %collective-permute-start.4 = (bf16[4,128,512]{2,1,0:T(8,128)(2,1)S(1)}, bf16[4,128,512]{2,1,0:T(8,128)(2,1)}, u32[]{:S(2)}, u32[]{:S(2)}) collective-permute-start(bf16[4,128,512]{2,1,0:T(8,128)(2,1)S(1)} %stack_pieces.2.b_ref.refs_0_), channel_id=1, source_target_pairs={{0,1},{1,0},{2,3},{3,2},{4,5},{5,4},{6,7},{7,6},{8,9},{9,8},{10,11... | collective-permute-start | bytes 1572872 | tf_op jit(solution)/shard_map/ppermute | solution.py:343
  13.2 10.7 %collective-permute-start.6 = (bf16[128,512]{1,0:T(8,128)(2,1)S(1)}, bf16[128,512]{1,0:T(8,128)(2,1)S(1)}, u32[]{:S(2)}, u32[]{:S(2)}) collective-permute-start(bf16[128,512]{1,0:T(8,128)(2,1)S(1)} %copy-done.3), channel_id=1, source_target_pairs={{0,2},{1,3},{2,4},{3,5},{4,6},{5,7},{6,0},{7,1},{8,10},{9,11},{10,... | collective-permute-start | bytes 393224 | tf_op jit(solution)/shard_map/ppermute | solution.py:339
  14.4 9.6 %collective-permute-start.7 = (bf16[128,512]{1,0:T(8,128)(2,1)S(1)}, bf16[128,512]{1,0:T(8,128)(2,1)S(1)}, u32[]{:S(2)}, u32[]{:S(2)}) collective-permute-start(bf16[128,512]{1,0:T(8,128)(2,1)S(1)} %collective-permute-done.1.refs_1_.p2), channel_id=1, source_target_pairs={{0,6},{1,7},{2,0},{3,1},{4,2},{5,3},{6,4},{7,5},{8,14},{9,15},{10,... | collective-permute-start | bytes 393224 | tf_op jit(solution)/shard_map/ppermute | solution.py:339
  20.7 8.6 %collective-permute-start.5 = (f32[200,128]{1,0:T(8,128)S(1)}, f32[200,128]{1,0:T(8,128)S(1)}, u32[]{:S(2)}, u32[]{:S(2)}) collective-permute-start(f32[200,128]{1,0:T(8,128)S(1)} %get-tuple-element.20.own_ref), channel_id=1, source_target_pairs={{0,8},{8,0},{16,24},{24,16},{32,40},{40,32},{48,56},{56,48},{64,72... | collective-permute-start | bytes 307208 | tf_op jit(solution)/shard_map/ppermute | solution.py:362
  24.1 9.2 %collective-permute-start.9 = (bf16[4,128,512]{2,1,0:T(8,128)(2,1)S(1)}, bf16[4,128,512]{2,1,0:T(8,128)(2,1)S(1)}, u32[]{:S(2)}, u32[]{:S(2)}) collective-permute-start(bf16[4,128,512]{2,1,0:T(8,128)(2,1)S(1)} %stack_pieces.3.c_ref.refs_4_.refs_2_), channel_id=1, source_target_pairs={{0,1},{1,0},{2,3},{3,2},{4,5},{5,4},{6,7},{7,6},{8,9},{9,8},{10,11... | collective-permute-start | bytes 1572872 | tf_op jit(solution)/shard_map/ppermute | solution.py:343
  29.3 10.2 %collective-permute-start.8 = (f32[200,128]{1,0:T(8,128)S(1)}, f32[200,128]{1,0:T(8,128)S(1)}, u32[]{:S(2)}, u32[]{:S(2)}) collective-permute-start(f32[200,128]{1,0:T(8,128)S(1)} %select_add_fusion.2.own_ref), channel_id=1, source_target_pairs={{0,16},{8,24},{16,0},{24,8},{32,48},{40,56},{48,32},{56,40},{64,80... | collective-permute-start | bytes 307208 | tf_op jit(solution)/shard_map/ppermute | solution.py:362
  39.6 8.8 %collective-permute-start.10 = (f32[200,128]{1,0:T(8,128)S(1)}, f32[200,128]{1,0:T(8,128)S(1)}, u32[]{:S(2)}, u32[]{:S(2)}) collective-permute-start(f32[200,128]{1,0:T(8,128)S(1)} %select_add_fusion.1.refs_8_), channel_id=1, source_target_pairs={{0,56},{8,48},{16,40},{24,32},{32,24},{40,16},{48,8},{56,0},{64,12... | collective-permute-start | bytes 307208 | tf_op jit(solution)/shard_map/ppermute | solution.py:362
  48.5 4.7 %collective-permute-start.11 = (f32[200,128]{1,0:T(8,128)S(1)}, f32[200,128]{1,0:T(8,128)S(1)}, u32[]{:S(2)}, u32[]{:S(2)}) collective-permute-start(f32[200,128]{1,0:T(8,128)S(1)} %select_add_fusion), channel_id=1, source_target_pairs={{0,64},{8,72},{16,80},{24,88},{32,96},{40,104},{48,112},{56,120},{... | collective-permute-start | bytes 307208 | tf_op jit(solution)/shard_map/ppermute | solution.py:362
  53.3 5.4 %collective-permute-start.12 = (bf16[192,128]{1,0:T(8,128)(2,1)S(1)}, bf16[192,128]{1,0:T(8,128)(2,1)S(1)}, u32[]{:S(2)}, u32[]{:S(2)}) collective-permute-start(bf16[192,128]{1,0:T(8,128)(2,1)S(1)} %fusion.1.refs_8_), channel_id=1, source_target_pairs={{0,192},{8,200},{16,208},{24,216},{32,224},{40,232},{48,240},{56,2... | collective-permute-start | bytes 147464 | tf_op jit(solution)/shard_map/ppermute | solution.py:362

commit v3 on v2

v3 whole, which is shorter than its diff:
```python
import functools

import jax
import jax.numpy as jnp
from jax import lax
from jax.experimental import pallas as pl
from jax.experimental.pallas import tpu as pltpu
from jax.sharding import PartitionSpec as P

STRETCH = 64
HEADS = 3
WIDTH = 64
STATE = 128
ROWS = HEADS * WIDTH
PIECE = 512
PIECES = 8
TOKENS = PIECE * PIECES
LOCAL = 6
CROSS = 5
FIRST = (0, 32, 48, 56, 60, 62, 63)
SHARES = ((), (0, 1, 2), (3, 4, 5, 6), (7,))
GROUPS = ((0, 1, 2), (3, 4, 5), (6,), (7,))
STEPS = ((0, 1, 2), (3, 4, 5), (6, 7))
VMEM_LIMIT = 20 * 1024 * 1024
BINV, DEC, GRP = 8, 9, 10
F32 = jnp.float32
BF16 = jnp.bfloat16

VMEM = pl.BlockSpec(memory_space=pltpu.VMEM)
SMEM = pl.BlockSpec(memory_space=pltpu.SMEM)
ANY = pl.BlockSpec(memory_space=pl.ANY)


def params():
    return pltpu.CompilerParams(vmem_limit_bytes=VMEM_LIMIT)


def cost(us):
    return pl.CostEstimate(flops=0, bytes_accessed=int(us * 3_500_000), transcendentals=0)


def decay_kernel(ld_ref, out_ref, run_ref):
    tiles = TOKENS // 128
    batch = 8
    lane = lax.broadcasted_iota(jnp.int32, (HEADS, 128), 1)
    local = lane & 63

    def first(g, carry):
        for i in range(batch):
            cols = pl.ds(pl.multiple_of(g * (batch * 128) + i * 128, 128), 128)
            ld = ld_ref[:, cols]
            cum = ld
            for k in (1, 2, 4, 8, 16, 32):
                cum = cum + jnp.where(local >= k, pltpu.roll(cum, k, 1), 0.0)
            rest = ld
            for k in (1, 2, 4, 8, 16, 32):
                rest = rest + jnp.where(local < 64 - k, pltpu.roll(rest, 128 - k, 1), 0.0)
            grow = jnp.exp(cum)
            out_ref[0, :, cols] = grow
            out_ref[1, :, cols] = jnp.where(lane >= 64, grow, 0.0)
            out_ref[DEC, :, cols] = jnp.exp(rest - ld)
            out_ref[BINV, :, cols] = jnp.exp(-cum)
            out_ref[GRP, :, cols] = jnp.broadcast_to(grow[:, 127:128], (HEADS, 128))
            left = jnp.broadcast_to(cum[:, 63:64], (HEADS, 128))
            run_ref[:, cols] = cum + jnp.where(lane >= 64, left, 0.0)
        return carry

    lax.fori_loop(0, tiles // batch, first, 0)
    runs = [run_ref[:, pl.ds(i * 128, 128)] for i in range(tiles)]
    for level in range(2, LOCAL + 2):
        span = 2 ** (level - 2)
        ends = [jnp.broadcast_to(runs[i][:, 127:128], (HEADS, 128)) for i in range(span - 1, tiles, span)]
        for i in range(tiles):
            cols = pl.ds(i * 128, 128)
            if level > LOCAL or (i // span) % 2:
                out_ref[level, :, cols] = jnp.exp(runs[i])
            else:
                out_ref[level, :, cols] = jnp.zeros((HEADS, 128), F32)
        if level <= LOCAL:
            for i in range(tiles // (2 * span)):
                slot = FIRST[level - 1] - 32 + i
                out_ref[GRP + 1, :, pl.ds(slot * 128, 128)] = jnp.exp(ends[2 * i + 1])
            for i in range(tiles):
                if (i // span) % 2:
                    runs[i] = runs[i] + ends[i // span - 1]
        else:
            out_ref[GRP + 1, :, pl.ds(31 * 128, 128)] = ends[0]


def decay_rows(log_decay):
    return pl.pallas_call(
        decay_kernel,
        out_shape=jax.ShapeDtypeStruct((12, HEADS, TOKENS), F32),
        in_specs=[VMEM],
        out_specs=VMEM,
        scratch_shapes=[pltpu.VMEM(log_decay.shape, F32)],
        compiler_params=params(),
        cost_estimate=cost(2),
        name="decay_rows",
    )(log_decay)


def hold_kernel(n, *refs):
    for x_ref, out_ref in zip(refs[:n], refs[-n:]):
        out_ref[...] = x_ref[...]


def hold(xs, after):
    n = len(xs)
    return pl.pallas_call(
        functools.partial(hold_kernel, n),
        out_shape=[jax.ShapeDtypeStruct(x.shape, x.dtype) for x in xs],
        in_specs=[VMEM] * n + [ANY] * len(after),
        out_specs=[VMEM] * n,
        compiler_params=params(),
        cost_estimate=cost(0.2),
        name="hold",
    )(*xs, *after)


def stack_kernel(p0, p1, p2, *refs):
    out_ref = refs[-1]
    out_ref[0] = p0[...]
    out_ref[1] = p1[...]
    out_ref[2] = p2[...]


def stack(parts, after):
    return pl.pallas_call(
        stack_kernel,
        out_shape=jax.ShapeDtypeStruct((3, STATE, PIECE), BF16),
        in_specs=[VMEM] * 3 + [ANY] * len(after),
        out_specs=VMEM,
        compiler_params=params(),
        cost_estimate=cost(0.2),
        name="stack_pieces",
    )(*parts, *after)


def state_kernel(group, order_ref, v_ref, row_ref, *refs):
    pieces = STEPS[group]
    last = group == len(STEPS) - 1
    b_refs = refs[: len(pieces)]
    if last:
        old_refs = refs[len(pieces) : len(pieces) + group]
        agg_ref, tree_ref, end_ref, p_ref = refs[-4:]
    else:
        agg_ref, top_ref = refs[-2:]
    lane = lax.broadcasted_iota(jnp.int32, (WIDTH, 128), 1)
    first = lane < 64

    def factor(h, slot):
        if isinstance(slot, int):
            return row_ref[GRP + slot // 32, h : h + 1, pl.ds(slot % 32 * 128, 128)]
        return row_ref[GRP + (slot >> 5), h : h + 1, pl.ds(pl.multiple_of((slot & 31) * 128, 128), 128)]

    for q, k in enumerate(pieces):
        j = order_ref[k]
        for h in range(HEADS):
            here = slice(h * WIDTH, (h + 1) * WIDTH)
            tops = []
            for a in range(4):
                cols = pl.ds(pl.multiple_of(j * PIECE + a * 128, 128), 128)
                b = b_refs[q][:, a * 128 : (a + 1) * 128].astype(F32)
                v = v_ref[h, :, cols]
                keys = (row_ref[DEC, h : h + 1, cols] * b).astype(BF16)
                zero = jnp.zeros_like(v)
                both = jnp.concatenate([jnp.where(first, v, zero), jnp.where(first, zero, v)], axis=0)
                s = lax.dot_general(both, keys, (((1,), (1,)), ((), ())), preferred_element_type=F32)
                agg_ref[q, a, here, :] = s[:WIDTH].astype(BF16)
                tops.append(factor(h, j * 4 + a) * s[:WIDTH] + s[WIDTH:])
            agg_ref[q, 4, here, :] = tops[0].astype(BF16)
            agg_ref[q, 5, here, :] = tops[2].astype(BF16)
            lo = factor(h, FIRST[1] + j * 2) * tops[0] + tops[1]
            hi = factor(h, FIRST[1] + j * 2 + 1) * tops[2] + tops[3]
            agg_ref[q, 6, here, :] = lo.astype(BF16)
            top = factor(h, FIRST[2] + j) * lo + hi
            if last:
                p_ref[j, here, :] = top
            else:
                top_ref[q, here, :] = top
    if not last:
        return
    for g, old in enumerate(old_refs):
        for q, k in enumerate(STEPS[g]):
            p_ref[order_ref[k]] = old[q]
    for h in range(HEADS):
        here = slice(h * WIDTH, (h + 1) * WIDTH)
        tops = [p_ref[j, here, :] for j in range(PIECES)]
        for level in range(4, LOCAL + 1):
            nxt = []
            for i in range(len(tops) // 2):
                slot = FIRST[level - 1] + i
                tree_ref[slot - FIRST[3], here, :] = tops[2 * i].astype(BF16)
                nxt.append(factor(h, slot) * tops[2 * i] + tops[2 * i + 1])
            tops = nxt
        end_ref[here, :] = tops[0]
    end_ref[ROWS : ROWS + 8, :] = jnp.concatenate([row_ref[GRP + 1, :, 31 * 128 :], jnp.zeros((5, 128), F32)], axis=0)


def block_states(group, order, values, rows, b_list, old=(), after=()):
    n = len(STEPS[group])
    agg = jax.ShapeDtypeStruct((n, 7, ROWS, STATE), BF16)
    tops = jax.ShapeDtypeStruct((n, ROWS, STATE), F32)
    end = [jax.ShapeDtypeStruct((7, ROWS, STATE), BF16), jax.ShapeDtypeStruct((ROWS + 8, STATE), F32)]
    last = group == len(STEPS) - 1
    return pl.pallas_call(
        functools.partial(state_kernel, group),
        out_shape=[agg] + (end if last else [tops]),
        in_specs=[SMEM] + [VMEM] * (2 + len(b_list) + len(old)) + [ANY] * len(after),
        out_specs=[VMEM] * (3 if last else 2),
        scratch_shapes=[pltpu.VMEM((PIECES, ROWS, STATE), F32)] if last else [],
        compiler_params=params(),
        cost_estimate=cost(1.5),
        name="block_states",
    )(order, values, rows, *b_list, *old, *after)


def home(piece):
    for g, group in enumerate(GROUPS):
        if piece in group:
            return g, group.index(piece)


def local_kernel(pieces, order_ref, v_ref, row_ref, lw_ref, tree_ref, own_ref, *refs):
    out_ref, same_ref = refs[-2:]
    same_ref[...] = own_ref[...]
    used = sorted({home(k)[0] for k in pieces})
    s_id = lax.broadcasted_iota(jnp.int32, (128, 128), 0)
    t_id = lax.broadcasted_iota(jnp.int32, (128, 128), 1)
    keep = (s_id <= t_id) & ((s_id >> 6) == (t_id >> 6))
    for at, k in enumerate(pieces):
        g, q = home(k)
        b_ref = refs[at]
        agg_ref, c_ref = refs[len(pieces) + 2 * used.index(g) :][:2]
        j = order_ref[k]
        for a in range(4):
            cols = pl.ds(pl.multiple_of(j * PIECE + a * 128, 128), 128)
            mine = slice(a * 128, (a + 1) * 128)
            c = c_ref[q, :, mine]
            b = b_ref[:, mine]
            scores = lax.dot_general(b, c, (((0,), (0,)), ((), ())), preferred_element_type=F32)
            scores = jnp.where(keep, scores, 0.0)
            n = 1 if g == 3 else q
            slots = [(1, agg_ref[n, a])]
            if a & 1:
                slots.append((2, agg_ref[n, 4 + a // 2]))
            if a & 2:
                slots.append((3, agg_ref[n, 6]))
            for level in range(4, LOCAL + 1):
                slots.append((level, tree_ref[FIRST[level - 1] - FIRST[3] + (j >> (level - 3))]))
            every = jnp.dot(jnp.concatenate([x for _, x in slots], axis=0), c, preferred_element_type=F32)
            for h in range(HEADS):
                col = jnp.transpose(jnp.broadcast_to(row_ref[BINV, h : h + 1, cols], (128, 128)))
                mix = ((lw_ref[0, h : h + 1, cols] * row_ref[0, h : h + 1, cols] * scores) * col).astype(BF16)
                acc = jnp.dot(v_ref[h, :, cols], mix, preferred_element_type=F32)
                for i, (level, _) in enumerate(slots):
                    read = every[i * ROWS + h * WIDTH : i * ROWS + (h + 1) * WIDTH]
                    acc = acc + lw_ref[level, h : h + 1, cols] * row_ref[level, h : h + 1, cols] * read
                out_ref[at, h, :, mine] = acc


def local_part(pieces, order, values, rows, weights, tree, own, aggs, b_list, c_stacks):
    used = sorted({home(k)[0] for k in pieces})
    parts = [b_list[k] for k in pieces] + [x[i] for i in used for x in (aggs, c_stacks)]
    return pl.pallas_call(
        functools.partial(local_kernel, pieces),
        out_shape=[
            jax.ShapeDtypeStruct((len(pieces), HEADS, WIDTH, PIECE), F32),
            jax.ShapeDtypeStruct(own.shape, own.dtype),
        ],
        in_specs=[SMEM] + [VMEM] * (5 + len(parts)),
        out_specs=[VMEM] * 2,
        compiler_params=params(),
        cost_estimate=cost(len(pieces)),
        name="local_part",
    )(order, values, rows, weights, tree, own, *parts)


def cross_kernel(rounds, sizes, last, order_ref, bits_ref, row_ref, lw_ref, *refs):
    n, m = len(rounds), len(sizes)
    s_refs, pre_refs = refs[:n], refs[n : 2 * n]
    w = len(GROUPS)
    c_refs = refs[2 * n : 2 * n + w]
    loc_refs = refs[2 * n + w : 2 * n + w + m]
    outs = refs[2 * n + w + m :]
    if last:
        full_ref, stage, sems = outs
    else:
        own_ref, outs, same_ref = outs[0], outs[1 : 1 + m], outs[1 + m :]
        if same_ref:
            same_ref[0][...] = own_ref[...]

    def send(k):
        cols = pl.ds(pl.multiple_of(order_ref[k] * PIECE, PIECE), PIECE)
        return pltpu.make_async_copy(stage.at[k], full_ref.at[:, :, cols], sems.at[k])

    facs = []
    for k, r in enumerate(rounds):
        row = jnp.where(bits_ref[r] == 1, jnp.exp(pre_refs[k][:HEADS, :]), 0.0)
        facs.append(jnp.concatenate([row, row], axis=1))
    states = jnp.concatenate([x[...] for x in s_refs], axis=0)
    place = [(g, o) for g in range(m) for o in range(sizes[g])]
    for q, (g, o) in enumerate(place):
        cg, ci = home(q)
        for a in range(2):
            cols = pl.ds(pl.multiple_of(order_ref[q] * PIECE + a * 256, 256), 256)
            mine = slice(a * 256, (a + 1) * 256)
            every = jnp.dot(states, c_refs[cg][ci, :, mine], preferred_element_type=F32)
            for h in range(HEADS):
                acc = loc_refs[g][o, h, :, mine]
                grow = row_ref[1 + LOCAL, h : h + 1, cols]
                for k, r in enumerate(rounds):
                    row = lw_ref[1 + LOCAL + r, h : h + 1, cols] * grow * facs[k][h : h + 1, :]
                    acc = acc + row * every[k * ROWS + h * WIDTH : k * ROWS + (h + 1) * WIDTH]
                if last:
                    stage[q, h, :, mine] = acc.astype(BF16)
                else:
                    outs[g][o, h, :, mine] = acc
        if last:
            send(q).start()
    if last:
        for q in range(PIECES):
            send(q).wait()


def cross_part(rounds, order, bits, rows, weights, states, pres, c_stacks, locs, own=None, back=True):
    last = own is None
    full = jax.ShapeDtypeStruct((HEADS, WIDTH, TOKENS), BF16)
    same = [jax.ShapeDtypeStruct(x.shape, x.dtype) for x in list(locs) + ([own] if back and not last else [])]
    first_loc = 4 + 2 * len(rounds) + len(GROUPS)
    m = len(locs)
    owns = [] if last else [VMEM if back else ANY]
    return pl.pallas_call(
        functools.partial(cross_kernel, rounds, tuple(x.shape[0] for x in locs), last),
        out_shape=full if last else same,
        in_specs=[SMEM] * 2 + [VMEM] * (2 + 2 * len(rounds) + len(GROUPS) + m) + owns,
        out_specs=ANY if last else [VMEM] * len(same),
        scratch_shapes=[
            pltpu.VMEM((PIECES, HEADS, WIDTH, PIECE), BF16),
            pltpu.SemaphoreType.DMA((PIECES,)),
        ]
        if last
        else [],
        input_output_aliases={} if last else {first_loc + i: i for i in range(m)},
        compiler_params=params(),
        cost_estimate=cost(1 + len(rounds)),
        name="cross_part",
    )(order, bits, rows, weights, *states, *pres, *c_stacks, *locs, *([] if last else [own]))


def combine(r, bits, own, got, pre):
    right = bits[r] == 1
    own_tot = own[ROWS:]
    got_tot = got[ROWS:]
    scale = jnp.exp(jnp.where(right, own_tot, got_tot))[:HEADS]
    scale = jnp.broadcast_to(scale[:, None], (HEADS, WIDTH, STATE)).reshape(ROWS, STATE)
    scale = jnp.concatenate([scale, jnp.ones((8, STATE), F32)], axis=0)
    new = scale * jnp.where(right, got, own) + jnp.where(right, own, got)
    return new, got[:ROWS].astype(BF16), pre + jnp.where(right, got_tot, 0.0)


def y_shift(x, k):
    return lax.ppermute(x, "head", [(i, ((i // 2 + k) % 4) * 2 + i % 2) for i in range(8)])


def other_core(x):
    return lax.ppermute(x, "head", [(i, i ^ 1) for i in range(8)])


def partner(r, i):
    x, z = i // 8, i % 8
    if r == 0:
        z = z ^ 1
    elif r == 1:
        z = z ^ 2
    elif r == 2:
        z = 7 - z
    elif r == 3:
        x = x ^ 1
    else:
        x = 3 - x
    return x * 8 + z


def exchange(r, x):
    return lax.ppermute(x, "seq", [(i, partner(r, i)) for i in range(32)])


def on_device(values, b_rows, c_rows, log_decay, level_weight):
    me = lax.axis_index("head")
    index = lax.axis_index("seq")
    q = lax.iota(jnp.int32, PIECES)
    far = jnp.where(q < 6, (q >= 3).astype(jnp.int32), q & 1)
    near = q - 3 * far
    turn = jnp.where(q < 6, near + (near >> 1), 2)
    order = ((((me >> 1) - turn) & 3) << 1) | ((me & 1) ^ far)
    bits = (index >> lax.iota(jnp.int32, CROSS)) & 1
    b1, b3, b2 = (y_shift(b_rows, k) for k in (1, 3, 2))
    rows = decay_rows(log_decay)
    near = [*hold([b_rows, b1, b3], [rows]), b2]
    near_far = [other_core(x) for x in near]
    b_list = near[:3] + near_far[:3] + [near[3], near_far[3]]
    agg_a, top_a = block_states(0, order, values, rows, b_list[:3])
    agg_b, top_b = block_states(1, order, values, rows, b_list[3:6], (), [top_a])
    agg_c, tree, own = block_states(2, order, values, rows, b_list[6:], [top_a, top_b])
    (c_own,) = hold([c_rows], [rows])
    c1, c3 = y_shift(c_own, 1), y_shift(c_own, 3)
    c2 = y_shift(c3, 3)
    c_a = stack([c_own, c1, c3], [])
    c_b = other_core(c_a)
    c_d = other_core(c2)
    c_stacks = [c_a, c_b, c2[None], c_d[None]]
    stacks = ([agg_a, agg_b, agg_c, agg_c], b_list, c_stacks)
    local_args = (order, values, rows, level_weight, tree)
    cross_args = (order, bits, rows, level_weight)
    pre = jnp.zeros((8, STATE), F32)
    pres, states, locs = [], [], []
    for r in range(CROSS):
        sent = own if r < CROSS - 1 else own[:ROWS].astype(BF16)
        got = exchange(r, sent)
        pres.append(pre)
        if r < CROSS - 1 and SHARES[r]:
            loc, own = local_part(SHARES[r], *local_args, own, *stacks)
            locs.append(loc)
        elif r == CROSS - 1:
            locs = cross_part((0, 1, 2, 3), *cross_args, states, pres[:4], c_stacks, locs, sent, False)
            return cross_part((4,), *cross_args, [got], [pre], c_stacks, locs)
        own, st, pre = combine(r, bits, own, got, pre)
        states.append(st)


def solution(mesh):
    return jax.shard_map(
        on_device,
        mesh=mesh,
        in_specs=(
            P("head", None, "seq"),
            P(None, ("seq", "head")),
            P(None, ("seq", "head")),
            P("head", "seq"),
            P(None, "head", "seq"),
        ),
        out_specs=P("head", None, "seq"),
        check_vma=False,
    )
```

time: 61.3 us -> 54.4 us (0.89)
  waiting for transfers between devices: 11.3 us -> 6.38 us
  Pallas kernels: 24.9 us -> 20.3 us
  starting transfers between devices: 19.2 us -> 22.1 us
    pallas_call x10 -> x12, Pallas kernels: 24.9 us -> 20.3 us  [the longest x3 8.12 us: local_part(): pl.pallas_call(functools.partial(local_kernel, pieces), out_shape=[jax.Sh...]
    ppermute x6, waiting for transfers between devices: 3.8 us -> 0.02 us  [y_shift(): lax.ppermute(x, 'head', [(i, (i // 2 + k) % 4 * 2 + i % 2) for i in range...]
    ppermute x6, starting transfers between devices: 8.66 us -> 9.92 us  [y_shift(): lax.ppermute(x, 'head', [(i, (i // 2 + k) % 4 * 2 + i % 2) for i in range...]
    ppermute x5, waiting for transfers between devices: 7.52 us -> 6.35 us  [exchange(): return lax.ppermute(x, 'seq', [(i, partner(r, i)) for i in range(32)])]
    ppermute x2 -> x6, starting transfers between devices: 0.19 us -> 1.29 us  [other_core(): return lax.ppermute(x, 'head', [(i, i ^ 1) for i in range(8)])]
  transfers between devices with their start and end apart: 13 -> 17, of which waited for: 6 -> 4; matrix products, arithmetic and copies ran while one was open for 1% -> 1% of each run, Pallas kernels for 37% -> 34%
where the time goes in v3:
time: 54.4 us; the launch traced here: 54.2 us
  starting transfers between devices  22.1 us (41%)
  Pallas kernels  20.3 us (37%)
  waiting for transfers between devices  6.38 us (12%)
  between operations  2.93 us (5%)
  local copies, waits for them, and re-layouts  2.47 us (5%)
    ppermute x5, starting transfers between devices, exchange(): return lax.ppermute(x, 'seq', [(i, partner(r, i)) for i in range(32)])  10.8 us
    ppermute x6, starting transfers between devices, y_shift(): lax.ppermute(x, 'head', [(i, (i // 2 + k) % 4 * 2 + i % 2) for i in range...  9.92 us
    pallas_call x3, Pallas kernels, local_part(): pl.pallas_call(functools.partial(local_kernel, pieces), out_shape=[jax.Sh...  8.12 us
    ppermute x5, waiting for transfers between devices, exchange(): return lax.ppermute(x, 'seq', [(i, partner(r, i)) for i in range(32)])  6.35 us
    pallas_call x2, Pallas kernels, cross_part(): pl.pallas_call(functools.partial(cross_kernel, rounds, tuple((x.shape[0]...  4.39 us
    pallas_call x3, Pallas kernels, block_states(): pl.pallas_call(functools.partial(state_kernel, group), out_shape=[agg] +...  4.32 us
    pallas_call x1, Pallas kernels, decay_rows(): pl.pallas_call(decay_kernel, out_shape=jax.ShapeDtypeStruct((12, HEADS, T...  2.46 us
    unnamed x10, local copies, waits for them, and re-layouts  1.76 us
  transfers between devices with their start and end apart: 17, of which 4 were waited for; matrix products, arithmetic and copies ran while one was open for 1% of the time, Pallas kernels for 34%

profile of v3, /device:TPU:6, one launch (start us, length us, event | category | flops | bytes accessed | tf_op | source)
XLA Modules:
  0.0 54.2 jit_solution(12075089190203854818)
XLA Ops:
  0.0 1.6 %collective-permute-start.2 = (bf16[128,512]{1,0:T(8,128)(2,1)}, bf16[128,512]{1,0:T(8,128)(2,1)S(1)}, u32[]{:S(2)}, u32[]{:S(2)}) collective-permute-start(bf16[128,512]{1,0:T(8,128)(2,1)} %refs_0_.2), channel_id=1, source_target_pairs={{0,2},{1,3},{2,4},{3,5},{4,6},{5,7},{6,0},{7,1},{8,10},{9,11},{10,... | collective-permute-start | bytes 393224 | tf_op jit(solution)/shard_map/ppermute | solution.py:364
  1.6 1.7 %collective-permute-start.3 = (bf16[128,512]{1,0:T(8,128)(2,1)}, bf16[128,512]{1,0:T(8,128)(2,1)S(1)}, u32[]{:S(2)}, u32[]{:S(2)}) collective-permute-start(bf16[128,512]{1,0:T(8,128)(2,1)} %refs_0_.2), channel_id=1, source_target_pairs={{0,6},{1,7},{2,0},{3,1},{4,2},{5,3},{6,4},{7,5},{8,14},{9,15},{10,... | collective-permute-start | bytes 393224 | tf_op jit(solution)/shard_map/ppermute | solution.py:364
  3.2 2.0 %collective-permute-start = (bf16[128,512]{1,0:T(8,128)(2,1)}, bf16[128,512]{1,0:T(8,128)(2,1)S(1)}, u32[]{:S(2)}, u32[]{:S(2)}) collective-permute-start(bf16[128,512]{1,0:T(8,128)(2,1)} %refs_0_.2), channel_id=1, source_target_pairs={{0,4},{1,5},{2,6},{3,7},{4,0},{5,1},{6,2},{7,3},{8,12},{9,13},{10,... | collective-permute-start | bytes 393224 | tf_op jit(solution)/shard_map/ppermute | solution.py:364
  5.2 0.8 %copy-done.4 = f32[3,4096]{1,0:T(4,128)S(1)} copy-done((f32[3,4096]{1,0:T(4,128)S(1)}, f32[3,4096]{1,0:T(4,128)}, u32[]{:S(2)}) %copy-start.4) | copy-done | bytes 49176
  6.1 2.5 %decay_rows.1.refs_3_.row_ref.refs_1_ = f32[12,3,4096]{2,1,0:T(4,128)S(1)} custom-call(f32[3,4096]{1,0:T(4,128)S(1)} %copy-done.4), custom_call_target="tpu_custom_call" | custom-call | bytes 7000000 | tf_op jit(solution)/shard_map/decay_rows/pallas_call | solution.py:91
  8.5 0.9 %copy-done.3 = bf16[128,512]{1,0:T(8,128)(2,1)S(1)} copy-done((bf16[128,512]{1,0:T(8,128)(2,1)S(1)}, bf16[128,512]{1,0:T(8,128)(2,1)}, u32[]{:S(2)}) %copy-start.3) | copy-done | bytes 131096
  9.5 1.1 %collective-permute-start.9 = (bf16[128,512]{1,0:T(8,128)(2,1)S(1)}, bf16[128,512]{1,0:T(8,128)(2,1)}, u32[]{:S(2)}, u32[]{:S(2)}) collective-permute-start(bf16[128,512]{1,0:T(8,128)(2,1)S(1)} %hold.3.p0), channel_id=1, source_target_pairs={{0,6},{1,7},{2,0},{3,1},{4,2},{5,3},{6,4},{7,5},{8,14},{9,15},{10,... | collective-permute-start | bytes 393224 | tf_op jit(solution)/shard_map/ppermute | solution.py:364
  10.6 0.1 collective-permute-start.4
  10.7 0.5 collective-permute-start.5
  11.2 0.1 collective-permute-start.6
  11.3 0.4 collective-permute-start.1
  11.8 1.5 %block_states.3 = (bf16[3,7,192,128]{3,2,1,0:T(8,128)(2,1)S(1)}, f32[3,192,128]{2,1,0:T(8,128)S(1)}) custom-call(s32[8]{0:T(128)S(1)} %fusion.7.order_ref, bf16[3,64,4096]{2,1,0:T(8,128)(2,1)S(1)} %copy-done, f32[12,3,4096]{2,1,0:T(4,128)S(1)} %decay_rows.1.refs_3_.row_ref.refs_1_, bf16[128,512]{1,0:T(8,128)(2,1)S(1)} %get-tuple-element.24.refs_0_, ...), custom_call_target="tpu_custom_call" | custom-call | bytes 5250000 | tf_op jit(solution)/shard_map/block_states/pallas_call | solution.py:207
  13.3 1.0 %collective-permute-start.8 = (bf16[128,512]{1,0:T(8,128)(2,1)S(1)}, bf16[128,512]{1,0:T(8,128)(2,1)S(1)}, u32[]{:S(2)}, u32[]{:S(2)}) collective-permute-start(bf16[128,512]{1,0:T(8,128)(2,1)S(1)} %hold.3.p0), channel_id=1, source_target_pairs={{0,2},{1,3},{2,4},{3,5},{4,6},{5,7},{6,0},{7,1},{8,10},{9,11},{10,... | collective-permute-start | bytes 393224 | tf_op jit(solution)/shard_map/ppermute | solution.py:364
  14.3 1.5 %block_states.4 = (bf16[3,7,192,128]{3,2,1,0:T(8,128)(2,1)S(1)}, f32[3,192,128]{2,1,0:T(8,128)S(1)}) custom-call(s32[8]{0:T(128)S(1)} %fusion.7.order_ref, bf16[3,64,4096]{2,1,0:T(8,128)(2,1)S(1)} %copy-done, f32[12,3,4096]{2,1,0:T(4,128)S(1)} %decay_rows.1.refs_3_.row_ref.refs_1_, bf16[128,512]{1,0:T(8,128)(2,1)S(1)} %collective-permute-done.4.refs_0_, ...), custom_call_target="tpu_custom_call" | custom-call | bytes 5250000 | tf_op jit(solution)/shard_map/block_states/pallas_call | solution.py:207
  15.9 1.3 %block_states.5 = (bf16[2,7,192,128]{3,2,1,0:T(8,128)(2,1)S(1)}, bf16[7,192,128]{2,1,0:T(8,128)(2,1)S(1)}, f32[200,128]{1,0:T(8,128)S(1)}) custom-call(s32[8]{0:T(128)S(1)} %fusion.7.order_ref, bf16[3,64,4096]{2,1,0:T(8,128)(2,1)S(1)} %copy-done, f32[12,3,4096]{2,1,0:T(4,128)S(1)} %decay_rows.1.refs_3_.row_ref.refs_1_, ...), custom_call_target="tpu_custom_call" | custom-call | bytes 5250000 | tf_op jit(solution)/shard_map/block_states/pallas_call | solution.py:207
  17.2 2.0 %collective-permute-start.7 = (f32[200,128]{1,0:T(8,128)S(1)}, f32[200,128]{1,0:T(8,128)S(1)}, u32[]{:S(2)}, u32[]{:S(2)}) collective-permute-start(f32[200,128]{1,0:T(8,128)S(1)} %get-tuple-element.30), channel_id=1, source_target_pairs={{0,8},{8,0},{16,24},{24,16},{32,40},{40,32},{48,56},{56,48},{64,72... | collective-permute-start | bytes 307208 | tf_op jit(solution)/shard_map/ppermute | solution.py:387
  19.2 0.6 %fusion.8 = (s32[1]{0:T(128)}, s32[1]{0:T(128)}, s32[1]{0:T(128)}, s32[1]{0:T(128)}) fusion(s32[5]{0:T(128)S(1)} %shift-right-arithmetic_and_fusion.bits_ref), kind=kLoop, calls=%fused_computation.30 | loop fusion | bytes 32 | tf_op jit(solution)/shard_map/slice | solution.py:353
  20.5 1.6 %collective-permute-done.7 = f32[200,128]{1,0:T(8,128)S(1)} collective-permute-done((f32[200,128]{1,0:T(8,128)S(1)}, f32[200,128]{1,0:T(8,128)S(1)}, u32[]{:S(2)}, u32[]{:S(2)}) %collective-permute-start.7) | collective-permute-done | bytes 102432 | tf_op jit(solution)/shard_map/ppermute | solution.py:387
  22.1 3.4 %collective-permute-start.10 = (f32[200,128]{1,0:T(8,128)S(1)}, f32[200,128]{1,0:T(8,128)S(1)}, u32[]{:S(2)}, u32[]{:S(2)}) collective-permute-start(f32[200,128]{1,0:T(8,128)S(1)} %select_add_fusion.2.own_ref), channel_id=1, source_target_pairs={{0,16},{8,24},{16,0},{24,8},{32,48},{40,56},{48,32},{56,40},{64,80... | collective-permute-start | bytes 307208 | tf_op jit(solution)/shard_map/ppermute | solution.py:387
  26.1 0.9 %stack_pieces.1.refs_4_.refs_8_.refs_2_ = bf16[3,128,512]{2,1,0:T(8,128)(2,1)S(1)} custom-call(bf16[128,512]{1,0:T(8,128)(2,1)S(1)} %hold.3.p0, bf16[128,512]{1,0:T(8,128)(2,1)S(1)} %collective-permute-done.8.p1, bf16[128,512]{1,0:T(8,128)(2,1)} %collective-permute-done.9.p2), custom_call_target="tpu_custom_call" | custom-call | bytes 700000 | tf_op jit(solution)/shard_map/stack_pieces/pallas_call | solution.py:129
  27.1 2.5 %collective-permute-start.12 = (bf16[128,512]{1,0:T(8,128)(2,1)}, bf16[128,512]{1,0:T(8,128)(2,1)S(1)}, u32[]{:S(2)}, u32[]{:S(2)}) collective-permute-start(bf16[128,512]{1,0:T(8,128)(2,1)} %collective-permute-done.9.p2), channel_id=1, source_target_pairs={{0,6},{1,7},{2,0},{3,1},{4,2},{5,3},{6,4},{7,5},{8,14},{9,15},{10,... | collective-permute-start | bytes 393224 | tf_op jit(solution)/shard_map/ppermute | solution.py:364
  29.7 2.9 %local_part.3 = (f32[3,3,64,512]{3,2,1,0:T(8,128)S(1)}, f32[200,128]{1,0:T(8,128)S(1)}) custom-call(s32[8]{0:T(128)S(1)} %fusion.7.order_ref, bf16[3,64,4096]{2,1,0:T(8,128)(2,1)S(1)} %copy-done, f32[12,3,4096]{2,1,0:T(4,128)S(1)} %decay_rows.1.refs_3_.row_ref.refs_1_, f32[12,3,4096]{2,1,0:T(4,128)S(1)} %copy-done.1, ...), custom_call_target="tpu_custom_call" | custom-call | bytes 10500000 | tf_op jit(solution)/shard_map/local_part/pallas_call | solution.py:266
  32.7 4.0 %collective-permute-start.13 = (f32[200,128]{1,0:T(8,128)S(1)}, f32[200,128]{1,0:T(8,128)S(1)}, u32[]{:S(2)}, u32[]{:S(2)}) collective-permute-start(f32[200,128]{1,0:T(8,128)S(1)} %select_add_fusion.1.own_ref), channel_id=1, source_target_pairs={{0,56},{8,48},{16,40},{24,32},{32,24},{40,16},{48,8},{56,0},{64,12... | collective-permute-start | bytes 307208 | tf_op jit(solution)/shard_map/ppermute | solution.py:387
  37.4 3.7 %local_part.4 = (f32[4,3,64,512]{3,2,1,0:T(8,128)S(1)}, f32[200,128]{1,0:T(8,128)S(1)}) custom-call(s32[8]{0:T(128)S(1)} %fusion.7.order_ref, bf16[3,64,4096]{2,1,0:T(8,128)(2,1)S(1)} %copy-done, f32[12,3,4096]{2,1,0:T(4,128)S(1)} %decay_rows.1.refs_3_.row_ref.refs_1_, f32[12,3,4096]{2,1,0:T(4,128)S(1)} %copy-done.1, ...), custom_call_target="tpu_custom_call" | custom-call | bytes 14000000 | tf_op jit(solution)/shard_map/local_part/pallas_call | solution.py:266
  41.1 0.7 %collective-permute-done.13 = f32[200,128]{1,0:T(8,128)S(1)} collective-permute-done((f32[200,128]{1,0:T(8,128)S(1)}, f32[200,128]{1,0:T(8,128)S(1)}, u32[]{:S(2)}, u32[]{:S(2)}) %collective-permute-start.13) | collective-permute-done | bytes 102432 | tf_op jit(solution)/shard_map/ppermute | solution.py:387
  41.9 0.9 %collective-permute-start.15 = (f32[200,128]{1,0:T(8,128)S(1)}, f32[200,128]{1,0:T(8,128)S(1)}, u32[]{:S(2)}, u32[]{:S(2)}) collective-permute-start(f32[200,128]{1,0:T(8,128)S(1)} %select_add_fusion.own_ref), channel_id=1, source_target_pairs={{0,64},{8,72},{16,80},{24,88},{32,96},{40,104},{48,112},{56,120},{... | collective-permute-start | bytes 307208 | tf_op jit(solution)/shard_map/ppermute | solution.py:387
  43.5 1.5 %local_part.5 = (f32[1,3,64,512]{3,2,1,0:T(8,128)S(1)}, f32[200,128]{1,0:T(8,128)S(1)}) custom-call(s32[8]{0:T(128)S(1)} %fusion.7.order_ref, bf16[3,64,4096]{2,1,0:T(8,128)(2,1)S(1)} %copy-done, f32[12,3,4096]{2,1,0:T(4,128)S(1)} %decay_rows.1.refs_3_.row_ref.refs_1_, f32[12,3,4096]{2,1,0:T(4,128)S(1)} %copy-done.1, ...), custom_call_target="tpu_custom_call" | custom-call | bytes 3500000 | tf_op jit(solution)/shard_map/local_part/pallas_call | solution.py:266
  45.0 1.7 %collective-permute-done.15 = f32[200,128]{1,0:T(8,128)S(1)} collective-permute-done((f32[200,128]{1,0:T(8,128)S(1)}, f32[200,128]{1,0:T(8,128)S(1)}, u32[]{:S(2)}, u32[]{:S(2)}) %collective-permute-start.15) | collective-permute-done | bytes 102432 | tf_op jit(solution)/shard_map/ppermute | solution.py:387
  46.7 0.6 %collective-permute-start.16 = (bf16[192,128]{1,0:T(8,128)(2,1)S(1)}, bf16[192,128]{1,0:T(8,128)(2,1)S(1)}, u32[]{:S(2)}, u32[]{:S(2)}) collective-permute-start(bf16[192,128]{1,0:T(8,128)(2,1)S(1)} %fusion.1.refs_15_), channel_id=1, source_target_pairs={{0,192},{8,200},{16,208},{24,216},{32,224},{40,232},{48,240},{56,2... | collective-permute-start | bytes 147464 | tf_op jit(solution)/shard_map/ppermute | solution.py:387
  47.4 2.4 %cross_part.2 = (f32[3,3,64,512]{3,2,1,0:T(8,128)S(1)}, f32[4,3,64,512]{3,2,1,0:T(8,128)S(1)}, f32[1,3,64,512]{3,2,1,0:T(8,128)S(1)}) custom-call(s32[8]{0:T(128)S(1)} %fusion.7.order_ref, s32[5]{0:T(128)S(1)} %shift-right-arithmetic_and_fusion.bits_ref, ...), custom_call_target="tpu_custom_call", output_to_operand_aliasing={{0}: (16, {}), {1}: (17, {}), {2}: (18, {})} | custom-call | bytes 17500000 | tf_op jit(solution)/shard_map/cross_part/pallas_call | solution.py:334
  49.8 2.3 %collective-permute-done.16.refs_0_ = bf16[192,128]{1,0:T(8,128)(2,1)S(1)} collective-permute-done((bf16[192,128]{1,0:T(8,128)(2,1)S(1)}, bf16[192,128]{1,0:T(8,128)(2,1)S(1)}, u32[]{:S(2)}, u32[]{:S(2)}) %collective-permute-start.16) | collective-permute-done | bytes 49184 | tf_op jit(solution)/shard_map/ppermute | solution.py:387
  52.1 1.9 %cross_part.3 = bf16[3,64,4096]{2,1,0:T(8,128)(2,1)} custom-call(s32[8]{0:T(128)S(1)} %fusion.7.order_ref, s32[5]{0:T(128)S(1)} %shift-right-arithmetic_and_fusion.bits_ref, f32[12,3,4096]{2,1,0:T(4,128)S(1)} %decay_rows.1.refs_3_.row_ref.refs_1_, f32[12,3,4096]{2,1,0:T(4,128)S(1)} %copy-done.1, bf16[192,128]{1,0:T(8,128)(2,1)S(1)} %collective-permute-done.16.refs_0_, ...), custom_call_target="tpu_custom_call" | custom-call | bytes 7000000 | tf_op jit(solution)/shard_map/cross_part/pallas_call | solution.py:334
  (48 shorter events, 0.5 us)
Async XLA Ops:
  0.0 10.6 %copy-start.2 = (bf16[128,512]{1,0:T(8,128)(2,1)S(1)}, bf16[128,512]{1,0:T(8,128)(2,1)}, u32[]{:S(2)}) copy-start(bf16[128,512]{1,0:T(8,128)(2,1)} %refs_0_.2) | copy-start | bytes 393220
  0.0 11.8 %copy-start = (bf16[3,64,4096]{2,1,0:T(8,128)(2,1)S(1)}, bf16[3,64,4096]{2,1,0:T(8,128)(2,1)}, u32[]{:S(2)}) copy-start(bf16[3,64,4096]{2,1,0:T(8,128)(2,1)} %v_ref.11) | copy-start | bytes 4718596
  0.0 10.6 %collective-permute-start.2 = (bf16[128,512]{1,0:T(8,128)(2,1)}, bf16[128,512]{1,0:T(8,128)(2,1)S(1)}, u32[]{:S(2)}, u32[]{:S(2)}) collective-permute-start(bf16[128,512]{1,0:T(8,128)(2,1)} %refs_0_.2), channel_id=1, source_target_pairs={{0,2},{1,3},{2,4},{3,5},{4,6},{5,7},{6,0},{7,1},{8,10},{9,11},{10,... | collective-permute-start | bytes 393224 | tf_op jit(solution)/shard_map/ppermute | solution.py:364
  1.6 9.0 %collective-permute-start.3 = (bf16[128,512]{1,0:T(8,128)(2,1)}, bf16[128,512]{1,0:T(8,128)(2,1)S(1)}, u32[]{:S(2)}, u32[]{:S(2)}) collective-permute-start(bf16[128,512]{1,0:T(8,128)(2,1)} %refs_0_.2), channel_id=1, source_target_pairs={{0,6},{1,7},{2,0},{3,1},{4,2},{5,3},{6,4},{7,5},{8,14},{9,15},{10,... | collective-permute-start | bytes 393224 | tf_op jit(solution)/shard_map/ppermute | solution.py:364
  3.2 8.1 %collective-permute-start = (bf16[128,512]{1,0:T(8,128)(2,1)}, bf16[128,512]{1,0:T(8,128)(2,1)S(1)}, u32[]{:S(2)}, u32[]{:S(2)}) collective-permute-start(bf16[128,512]{1,0:T(8,128)(2,1)} %refs_0_.2), channel_id=1, source_target_pairs={{0,4},{1,5},{2,6},{3,7},{4,0},{5,1},{6,2},{7,3},{8,12},{9,13},{10,... | collective-permute-start | bytes 393224 | tf_op jit(solution)/shard_map/ppermute | solution.py:364
  5.2 0.8 %copy-start.4 = (f32[3,4096]{1,0:T(4,128)S(1)}, f32[3,4096]{1,0:T(4,128)}, u32[]{:S(2)}) copy-start(f32[3,4096]{1,0:T(4,128)} %ld_ref.1) | copy-start | bytes 147460
  8.5 0.9 %copy-start.3 = (bf16[128,512]{1,0:T(8,128)(2,1)S(1)}, bf16[128,512]{1,0:T(8,128)(2,1)}, u32[]{:S(2)}) copy-start(bf16[128,512]{1,0:T(8,128)(2,1)} %refs_0_.3) | copy-start | bytes 393220
  9.5 16.6 %collective-permute-start.9 = (bf16[128,512]{1,0:T(8,128)(2,1)S(1)}, bf16[128,512]{1,0:T(8,128)(2,1)}, u32[]{:S(2)}, u32[]{:S(2)}) collective-permute-start(bf16[128,512]{1,0:T(8,128)(2,1)S(1)} %hold.3.p0), channel_id=1, source_target_pairs={{0,6},{1,7},{2,0},{3,1},{4,2},{5,3},{6,4},{7,5},{8,14},{9,15},{10,... | collective-permute-start | bytes 393224 | tf_op jit(solution)/shard_map/ppermute | solution.py:364
  10.6 2.6 %collective-permute-start.4 = (bf16[128,512]{1,0:T(8,128)(2,1)S(1)}, bf16[128,512]{1,0:T(8,128)(2,1)S(1)}, u32[]{:S(2)}, u32[]{:S(2)}) collective-permute-start(bf16[128,512]{1,0:T(8,128)(2,1)S(1)} %get-tuple-element.24.refs_0_), channel_id=1, source_target_pairs={{0,1},{1,0},{2,3},{3,2},{4,5},{5,4},{6,7},{7,6},{8,9},{9,8},{10,11... | collective-permute-start | bytes 393224 | tf_op jit(solution)/shard_map/ppermute | solution.py:368
  10.7 3.6 %collective-permute-start.5 = (bf16[128,512]{1,0:T(8,128)(2,1)S(1)}, bf16[128,512]{1,0:T(8,128)(2,1)S(1)}, u32[]{:S(2)}, u32[]{:S(2)}) collective-permute-start(bf16[128,512]{1,0:T(8,128)(2,1)S(1)} %get-tuple-element.25.refs_1_), channel_id=1, source_target_pairs={{0,1},{1,0},{2,3},{3,2},{4,5},{5,4},{6,7},{7,6},{8,9},{9,8},{10,11... | collective-permute-start | bytes 393224 | tf_op jit(solution)/shard_map/ppermute | solution.py:368
  11.2 3.1 %collective-permute-start.6 = (bf16[128,512]{1,0:T(8,128)(2,1)S(1)}, bf16[128,512]{1,0:T(8,128)(2,1)S(1)}, u32[]{:S(2)}, u32[]{:S(2)}) collective-permute-start(bf16[128,512]{1,0:T(8,128)(2,1)S(1)} %get-tuple-element.26.refs_2_), channel_id=1, source_target_pairs={{0,1},{1,0},{2,3},{3,2},{4,5},{5,4},{6,7},{7,6},{8,9},{9,8},{10,11... | collective-permute-start | bytes 393224 | tf_op jit(solution)/shard_map/ppermute | solution.py:368
  11.3 4.5 %collective-permute-start.1 = (bf16[128,512]{1,0:T(8,128)(2,1)S(1)}, bf16[128,512]{1,0:T(8,128)(2,1)S(1)}, u32[]{:S(2)}, u32[]{:S(2)}) collective-permute-start(bf16[128,512]{1,0:T(8,128)(2,1)S(1)} %collective-permute-done.refs_0_.refs_3_), channel_id=1, source_target_pairs={{0,1},{1,0},{2,3},{3,2},{4,5},{5,4},{6,7},{7,6},{8,9},{9,8},{10,11... | collective-permute-start | bytes 393224 | tf_op jit(solution)/shard_map/ppermute | solution.py:368
  13.3 12.8 %collective-permute-start.8 = (bf16[128,512]{1,0:T(8,128)(2,1)S(1)}, bf16[128,512]{1,0:T(8,128)(2,1)S(1)}, u32[]{:S(2)}, u32[]{:S(2)}) collective-permute-start(bf16[128,512]{1,0:T(8,128)(2,1)S(1)} %hold.3.p0), channel_id=1, source_target_pairs={{0,2},{1,3},{2,4},{3,5},{4,6},{5,7},{6,0},{7,1},{8,10},{9,11},{10,... | collective-permute-start | bytes 393224 | tf_op jit(solution)/shard_map/ppermute | solution.py:364
  15.8 13.8 %copy-start.1 = (f32[12,3,4096]{2,1,0:T(4,128)S(1)}, f32[12,3,4096]{2,1,0:T(4,128)}, u32[]{:S(2)}) copy-start(f32[12,3,4096]{2,1,0:T(4,128)} %lw_ref.9) | copy-start | bytes 1769476
  17.2 4.9 %collective-permute-start.7 = (f32[200,128]{1,0:T(8,128)S(1)}, f32[200,128]{1,0:T(8,128)S(1)}, u32[]{:S(2)}, u32[]{:S(2)}) collective-permute-start(f32[200,128]{1,0:T(8,128)S(1)} %get-tuple-element.30), channel_id=1, source_target_pairs={{0,8},{8,0},{16,24},{24,16},{32,40},{40,32},{48,56},{56,48},{64,72... | collective-permute-start | bytes 307208 | tf_op jit(solution)/shard_map/ppermute | solution.py:387
  22.1 10.5 %collective-permute-start.10 = (f32[200,128]{1,0:T(8,128)S(1)}, f32[200,128]{1,0:T(8,128)S(1)}, u32[]{:S(2)}, u32[]{:S(2)}) collective-permute-start(f32[200,128]{1,0:T(8,128)S(1)} %select_add_fusion.2.own_ref), channel_id=1, source_target_pairs={{0,16},{8,24},{16,0},{24,8},{32,48},{40,56},{48,32},{56,40},{64,80... | collective-permute-start | bytes 307208 | tf_op jit(solution)/shard_map/ppermute | solution.py:387
  27.0 10.4 %collective-permute-start.11 = (bf16[3,128,512]{2,1,0:T(8,128)(2,1)S(1)}, bf16[3,128,512]{2,1,0:T(8,128)(2,1)S(1)}, u32[]{:S(2)}, u32[]{:S(2)}) collective-permute-start(bf16[3,128,512]{2,1,0:T(8,128)(2,1)S(1)} %stack_pieces.1.refs_4_.refs_8_.refs_2_), channel_id=1, source_target_pairs={{0,1},{1,0},{2,3},{3,2},{4,5},{5,4},{6,7},{7,6},{8,9},{9,8},{10,11... | collective-permute-start | bytes 1179656 | tf_op jit(solution)/shard_map/ppermute | solution.py:368
  27.1 10.2 %collective-permute-start.12 = (bf16[128,512]{1,0:T(8,128)(2,1)}, bf16[128,512]{1,0:T(8,128)(2,1)S(1)}, u32[]{:S(2)}, u32[]{:S(2)}) collective-permute-start(bf16[128,512]{1,0:T(8,128)(2,1)} %collective-permute-done.9.p2), channel_id=1, source_target_pairs={{0,6},{1,7},{2,0},{3,1},{4,2},{5,3},{6,4},{7,5},{8,14},{9,15},{10,... | collective-permute-start | bytes 393224 | tf_op jit(solution)/shard_map/ppermute | solution.py:364
  32.7 9.2 %collective-permute-start.13 = (f32[200,128]{1,0:T(8,128)S(1)}, f32[200,128]{1,0:T(8,128)S(1)}, u32[]{:S(2)}, u32[]{:S(2)}) collective-permute-start(f32[200,128]{1,0:T(8,128)S(1)} %select_add_fusion.1.own_ref), channel_id=1, source_target_pairs={{0,56},{8,48},{16,40},{24,32},{32,24},{40,16},{48,8},{56,0},{64,12... | collective-permute-start | bytes 307208 | tf_op jit(solution)/shard_map/ppermute | solution.py:387
  37.3 6.2 %collective-permute-start.14 = (bf16[128,512]{1,0:T(8,128)(2,1)S(1)}, bf16[128,512]{1,0:T(8,128)(2,1)S(1)}, u32[]{:S(2)}, u32[]{:S(2)}) collective-permute-start(bf16[128,512]{1,0:T(8,128)(2,1)S(1)} %collective-permute-done.12), channel_id=1, source_target_pairs={{0,1},{1,0},{2,3},{3,2},{4,5},{5,4},{6,7},{7,6},{8,9},{9,8},{10,11... | collective-permute-start | bytes 393224 | tf_op jit(solution)/shard_map/ppermute | solution.py:368
  41.9 4.7 %collective-permute-start.15 = (f32[200,128]{1,0:T(8,128)S(1)}, f32[200,128]{1,0:T(8,128)S(1)}, u32[]{:S(2)}, u32[]{:S(2)}) collective-permute-start(f32[200,128]{1,0:T(8,128)S(1)} %select_add_fusion.own_ref), channel_id=1, source_target_pairs={{0,64},{8,72},{16,80},{24,88},{32,96},{40,104},{48,112},{56,120},{... | collective-permute-start | bytes 307208 | tf_op jit(solution)/shard_map/ppermute | solution.py:387
  46.7 5.4 %collective-permute-start.16 = (bf16[192,128]{1,0:T(8,128)(2,1)S(1)}, bf16[192,128]{1,0:T(8,128)(2,1)S(1)}, u32[]{:S(2)}, u32[]{:S(2)}) collective-permute-start(bf16[192,128]{1,0:T(8,128)(2,1)S(1)} %fusion.1.refs_15_), channel_id=1, source_target_pairs={{0,192},{8,200},{16,208},{24,216},{32,224},{40,232},{48,240},{56,2... | collective-permute-start | bytes 147464 | tf_op jit(solution)/shard_map/ppermute | solution.py:387

commit v4 on v3

--- a/solution.py
+++ b/solution.py
@@ -18,9 +18,9 @@
 LOCAL = 6
 CROSS = 5
 FIRST = (0, 32, 48, 56, 60, 62, 63)
-SHARES = ((), (0, 1, 2), (3, 4, 5, 6), (7,))
+SHARES = ((), (0, 1, 2), (3, 4, 5), (6, 7))
 GROUPS = ((0, 1, 2), (3, 4, 5), (6,), (7,))
-STEPS = ((0, 1, 2), (3, 4, 5), (6, 7))
+STEPS = ((0, 1, 2), (3, 4, 5, 6, 7))
 VMEM_LIMIT = 20 * 1024 * 1024
 BINV, DEC, GRP = 8, 9, 10
 F32 = jnp.float32
@@ -241,7 +241,7 @@
             b = b_ref[:, mine]
             scores = lax.dot_general(b, c, (((0,), (0,)), ((), ())), preferred_element_type=F32)
             scores = jnp.where(keep, scores, 0.0)
-            n = 1 if g == 3 else q
+            n = k - GROUPS[min(g, 1)][0]
             slots = [(1, agg_ref[n, a])]
             if a & 1:
                 slots.append((2, agg_ref[n, 4 + a // 2]))
@@ -393,25 +393,26 @@
     q = lax.iota(jnp.int32, PIECES)
     far = jnp.where(q < 6, (q >= 3).astype(jnp.int32), q & 1)
     near = q - 3 * far
-    turn = jnp.where(q < 6, near + (near >> 1), 2)
+    turn = jnp.where(q < 6, (4 - near - (near >> 1)) & 3, 2)
     order = ((((me >> 1) - turn) & 3) << 1) | ((me & 1) ^ far)
     bits = (index >> lax.iota(jnp.int32, CROSS)) & 1
     b1, b3, b2 = (y_shift(b_rows, k) for k in (1, 3, 2))
     rows = decay_rows(log_decay)
-    near = [*hold([b_rows, b1, b3], [rows]), b2]
+    (c_own,) = hold([c_rows], [rows])
+    near = [*hold([b_rows, b3, b1], [rows, c_own]), b2]
     near_far = [other_core(x) for x in near]
     b_list = near[:3] + near_far[:3] + [near[3], near_far[3]]
     agg_a, top_a = block_states(0, order, values, rows, b_list[:3])
-    agg_b, top_b = block_states(1, order, values, rows, b_list[3:6], (), [top_a])
-    agg_c, tree, own = block_states(2, order, values, rows, b_list[6:], [top_a, top_b])
-    (c_own,) = hold([c_rows], [rows])
-    c1, c3 = y_shift(c_own, 1), y_shift(c_own, 3)
+    agg_b, tree, own = block_states(1, order, values, rows, b_list[3:], [top_a])
+    c3 = y_shift(c_own, 3)
+    (c_late,) = hold([c_own], [own])
+    c1 = y_shift(c_late, 1)
     c2 = y_shift(c3, 3)
-    c_a = stack([c_own, c1, c3], [])
+    c_a = stack([c_own, c3, c1], [])
     c_b = other_core(c_a)
     c_d = other_core(c2)
     c_stacks = [c_a, c_b, c2[None], c_d[None]]
-    stacks = ([agg_a, agg_b, agg_c, agg_c], b_list, c_stacks)
+    stacks = ([agg_a, agg_b, agg_b, agg_b], b_list, c_stacks)
     local_args = (order, values, rows, level_weight, tree)
     cross_args = (order, bits, rows, level_weight)
     pre = jnp.zeros((8, STATE), F32)

time: 54.4 us -> 53.3 us (0.980)
  Pallas kernels: 20.3 us -> 19.6 us
    pallas_call x3 -> x2, Pallas kernels: 4.32 us -> 3.63 us  [block_states(): pl.pallas_call(functools.partial(state_kernel, group), out_shape=[agg] +...]
  transfers between devices with their start and end apart: 17 -> 17, of which waited for: 4 -> 4; matrix products, arithmetic and copies ran while one was open for 1% -> 2% of each run, Pallas kernels for 34% -> 33%
where the time goes in v4:
time: 53.3 us; the launch traced here: 53.1 us
  starting transfers between devices  21.9 us (41%)
  Pallas kernels  19.6 us (37%)
  waiting for transfers between devices  6.01 us (11%)
  between operations  2.97 us (6%)
  local copies, waits for them, and re-layouts  2.5 us (5%)
    ppermute x5, starting transfers between devices, exchange(): return lax.ppermute(x, 'seq', [(i, partner(r, i)) for i in range(32)])  10.8 us
    ppermute x6, starting transfers between devices, y_shift(): lax.ppermute(x, 'head', [(i, (i // 2 + k) % 4 * 2 + i % 2) for i in range...  9.44 us
    pallas_call x3, Pallas kernels, local_part(): pl.pallas_call(functools.partial(local_kernel, pieces), out_shape=[jax.Sh...  8.07 us
    ppermute x5, waiting for transfers between devices, exchange(): return lax.ppermute(x, 'seq', [(i, partner(r, i)) for i in range(32)])  5.98 us
    pallas_call x2, Pallas kernels, cross_part(): pl.pallas_call(functools.partial(cross_kernel, rounds, tuple((x.shape[0]...  4.4 us
    pallas_call x2, Pallas kernels, block_states(): pl.pallas_call(functools.partial(state_kernel, group), out_shape=[agg] +...  3.63 us
    pallas_call x1, Pallas kernels, decay_rows(): pl.pallas_call(decay_kernel, out_shape=jax.ShapeDtypeStruct((12, HEADS, T...  2.46 us
    unnamed x10, local copies, waits for them, and re-layouts  1.76 us
  transfers between devices with their start and end apart: 17, of which 4 were waited for; matrix products, arithmetic and copies ran while one was open for 2% of the time, Pallas kernels for 33%

profile of v4, /device:TPU:6, one launch (start us, length us, event | category | flops | bytes accessed | tf_op | source)
XLA Modules:
  0.0 53.1 jit_solution(16176697548265461373)
XLA Ops:
  0.0 1.6 %collective-permute-start.1 = (bf16[128,512]{1,0:T(8,128)(2,1)}, bf16[128,512]{1,0:T(8,128)(2,1)S(1)}, u32[]{:S(2)}, u32[]{:S(2)}) collective-permute-start(bf16[128,512]{1,0:T(8,128)(2,1)} %refs_0_.3), channel_id=1, source_target_pairs={{0,2},{1,3},{2,4},{3,5},{4,6},{5,7},{6,0},{7,1},{8,10},{9,11},{10,... | collective-permute-start | bytes 393224 | tf_op jit(solution)/shard_map/ppermute | solution.py:364
  1.6 1.7 %collective-permute-start = (bf16[128,512]{1,0:T(8,128)(2,1)}, bf16[128,512]{1,0:T(8,128)(2,1)S(1)}, u32[]{:S(2)}, u32[]{:S(2)}) collective-permute-start(bf16[128,512]{1,0:T(8,128)(2,1)} %refs_0_.3), channel_id=1, source_target_pairs={{0,6},{1,7},{2,0},{3,1},{4,2},{5,3},{6,4},{7,5},{8,14},{9,15},{10,... | collective-permute-start | bytes 393224 | tf_op jit(solution)/shard_map/ppermute | solution.py:364
  3.2 2.0 %collective-permute-start.5 = (bf16[128,512]{1,0:T(8,128)(2,1)}, bf16[128,512]{1,0:T(8,128)(2,1)S(1)}, u32[]{:S(2)}, u32[]{:S(2)}) collective-permute-start(bf16[128,512]{1,0:T(8,128)(2,1)} %refs_0_.3), channel_id=1, source_target_pairs={{0,4},{1,5},{2,6},{3,7},{4,0},{5,1},{6,2},{7,3},{8,12},{9,13},{10,... | collective-permute-start | bytes 393224 | tf_op jit(solution)/shard_map/ppermute | solution.py:364
  5.2 0.8 %copy-done.4 = f32[3,4096]{1,0:T(4,128)S(1)} copy-done((f32[3,4096]{1,0:T(4,128)S(1)}, f32[3,4096]{1,0:T(4,128)}, u32[]{:S(2)}) %copy-start.4) | copy-done | bytes 49176
  6.1 2.5 %decay_rows.1.refs_1_.refs_3_.row_ref = f32[12,3,4096]{2,1,0:T(4,128)S(1)} custom-call(f32[3,4096]{1,0:T(4,128)S(1)} %copy-done.4), custom_call_target="tpu_custom_call" | custom-call | bytes 7000000 | tf_op jit(solution)/shard_map/decay_rows/pallas_call | solution.py:91
  8.5 0.9 %copy-done.3 = bf16[128,512]{1,0:T(8,128)(2,1)S(1)} copy-done((bf16[128,512]{1,0:T(8,128)(2,1)S(1)}, bf16[128,512]{1,0:T(8,128)(2,1)}, u32[]{:S(2)}) %copy-start.3) | copy-done | bytes 131096
  9.5 1.1 %collective-permute-start.8 = (bf16[128,512]{1,0:T(8,128)(2,1)S(1)}, bf16[128,512]{1,0:T(8,128)(2,1)}, u32[]{:S(2)}, u32[]{:S(2)}) collective-permute-start(bf16[128,512]{1,0:T(8,128)(2,1)S(1)} %hold.3.refs_4_.refs_0_.p0), channel_id=1, source_target_pairs={{0,6},{1,7},{2,0},{3,1},{4,2},{5,3},{6,4},{7,5},{8,14},{9,15},{10,... | collective-permute-start | bytes 393224 | tf_op jit(solution)/shard_map/ppermute | solution.py:364
  10.7 0.5 collective-permute-start.3
  11.2 0.1 collective-permute-start.4
  11.3 0.4 collective-permute-start.6
  11.8 1.5 %block_states.2 = (bf16[3,7,192,128]{3,2,1,0:T(8,128)(2,1)S(1)}, f32[3,192,128]{2,1,0:T(8,128)S(1)}) custom-call(s32[8]{0:T(128)S(1)} %fusion.7.order_ref, bf16[3,64,4096]{2,1,0:T(8,128)(2,1)S(1)} %copy-done, f32[12,3,4096]{2,1,0:T(4,128)S(1)} %decay_rows.1.refs_1_.refs_3_.row_ref, bf16[128,512]{1,0:T(8,128)(2,1)S(1)} %get-tuple-element.22.refs_0_, ...), custom_call_target="tpu_custom_call" | custom-call | bytes 5250000 | tf_op jit(solution)/shard_map/block_states/pallas_call | solution.py:207
  13.3 2.1 %block_states.3 = (bf16[5,7,192,128]{3,2,1,0:T(8,128)(2,1)S(1)}, bf16[7,192,128]{2,1,0:T(8,128)(2,1)S(1)}, f32[200,128]{1,0:T(8,128)S(1)}) custom-call(s32[8]{0:T(128)S(1)} %fusion.7.order_ref, bf16[3,64,4096]{2,1,0:T(8,128)(2,1)S(1)} %copy-done, f32[12,3,4096]{2,1,0:T(4,128)S(1)} %decay_rows.1.refs_1_.refs_3_.row_ref, ...), custom_call_target="tpu_custom_call" | custom-call | bytes 5250000 | tf_op jit(solution)/shard_map/block_states/pallas_call | solution.py:207
  15.5 2.0 %collective-permute-start.7 = (f32[200,128]{1,0:T(8,128)S(1)}, f32[200,128]{1,0:T(8,128)S(1)}, u32[]{:S(2)}, u32[]{:S(2)}) collective-permute-start(f32[200,128]{1,0:T(8,128)S(1)} %get-tuple-element.27.refs_1_), channel_id=1, source_target_pairs={{0,8},{8,0},{16,24},{24,16},{32,40},{40,32},{48,56},{56,48},{64,72... | collective-permute-start | bytes 307208 | tf_op jit(solution)/shard_map/ppermute | solution.py:387
  17.5 0.6 %fusion.8 = (s32[1]{0:T(128)}, s32[1]{0:T(128)}, s32[1]{0:T(128)}, s32[1]{0:T(128)}) fusion(s32[5]{0:T(128)S(1)} %shift-right-arithmetic_and_fusion.bits_ref), kind=kLoop, calls=%fused_computation.29 | loop fusion | bytes 32 | tf_op jit(solution)/shard_map/slice | solution.py:353
  18.8 1.0 %collective-permute-start.9 = (bf16[128,512]{1,0:T(8,128)(2,1)S(1)}, bf16[128,512]{1,0:T(8,128)(2,1)S(1)}, u32[]{:S(2)}, u32[]{:S(2)}) collective-permute-start(bf16[128,512]{1,0:T(8,128)(2,1)S(1)} %hold.5), channel_id=1, source_target_pairs={{0,2},{1,3},{2,4},{3,5},{4,6},{5,7},{6,0},{7,1},{8,10},{9,11},{10,... | collective-permute-start | bytes 393224 | tf_op jit(solution)/shard_map/ppermute | solution.py:364
  19.8 0.8 %collective-permute-done.7 = f32[200,128]{1,0:T(8,128)S(1)} collective-permute-done((f32[200,128]{1,0:T(8,128)S(1)}, f32[200,128]{1,0:T(8,128)S(1)}, u32[]{:S(2)}, u32[]{:S(2)}) %collective-permute-start.7) | collective-permute-done | bytes 102432 | tf_op jit(solution)/shard_map/ppermute | solution.py:387
  20.7 3.4 %collective-permute-start.10 = (f32[200,128]{1,0:T(8,128)S(1)}, f32[200,128]{1,0:T(8,128)S(1)}, u32[]{:S(2)}, u32[]{:S(2)}) collective-permute-start(f32[200,128]{1,0:T(8,128)S(1)} %select_add_fusion.2.own_ref), channel_id=1, source_target_pairs={{0,16},{8,24},{16,0},{24,8},{32,48},{40,56},{48,32},{56,40},{64,80... | collective-permute-start | bytes 307208 | tf_op jit(solution)/shard_map/ppermute | solution.py:387
  24.7 2.0 %collective-permute-start.13 = (bf16[128,512]{1,0:T(8,128)(2,1)}, bf16[128,512]{1,0:T(8,128)(2,1)S(1)}, u32[]{:S(2)}, u32[]{:S(2)}) collective-permute-start(bf16[128,512]{1,0:T(8,128)(2,1)} %collective-permute-done.8.p1), channel_id=1, source_target_pairs={{0,6},{1,7},{2,0},{3,1},{4,2},{5,3},{6,4},{7,5},{8,14},{9,15},{10,... | collective-permute-start | bytes 393224 | tf_op jit(solution)/shard_map/ppermute | solution.py:364
  26.7 1.0 %stack_pieces.1.refs_4_.refs_8_.refs_2_ = bf16[3,128,512]{2,1,0:T(8,128)(2,1)S(1)} custom-call(bf16[128,512]{1,0:T(8,128)(2,1)S(1)} %hold.3.refs_4_.refs_0_.p0, bf16[128,512]{1,0:T(8,128)(2,1)} %collective-permute-done.8.p1, bf16[128,512]{1,0:T(8,128)(2,1)S(1)} %collective-permute-done.9.p2), custom_call_target="tpu_custom_call" | custom-call | bytes 700000 | tf_op jit(solution)/shard_map/stack_pieces/pallas_call | solution.py:129
  27.7 0.3 collective-permute-start.11
  28.0 2.9 %local_part.3 = (f32[3,3,64,512]{3,2,1,0:T(8,128)S(1)}, f32[200,128]{1,0:T(8,128)S(1)}) custom-call(s32[8]{0:T(128)S(1)} %fusion.7.order_ref, bf16[3,64,4096]{2,1,0:T(8,128)(2,1)S(1)} %copy-done, f32[12,3,4096]{2,1,0:T(4,128)S(1)} %decay_rows.1.refs_1_.refs_3_.row_ref, f32[12,3,4096]{2,1,0:T(4,128)S(1)} %copy-done.1, ...), custom_call_target="tpu_custom_call" | custom-call | bytes 10500000 | tf_op jit(solution)/shard_map/local_part/pallas_call | solution.py:266
  31.0 3.9 %collective-permute-start.12 = (f32[200,128]{1,0:T(8,128)S(1)}, f32[200,128]{1,0:T(8,128)S(1)}, u32[]{:S(2)}, u32[]{:S(2)}) collective-permute-start(f32[200,128]{1,0:T(8,128)S(1)} %select_add_fusion.1.own_ref), channel_id=1, source_target_pairs={{0,56},{8,48},{16,40},{24,32},{32,24},{40,16},{48,8},{56,0},{64,12... | collective-permute-start | bytes 307208 | tf_op jit(solution)/shard_map/ppermute | solution.py:387
  35.6 0.3 collective-permute-start.14
  35.9 3.0 %local_part.4 = (f32[3,3,64,512]{3,2,1,0:T(8,128)S(1)}, f32[200,128]{1,0:T(8,128)S(1)}) custom-call(s32[8]{0:T(128)S(1)} %fusion.7.order_ref, bf16[3,64,4096]{2,1,0:T(8,128)(2,1)S(1)} %copy-done, f32[12,3,4096]{2,1,0:T(4,128)S(1)} %decay_rows.1.refs_1_.refs_3_.row_ref, f32[12,3,4096]{2,1,0:T(4,128)S(1)} %copy-done.1, ...), custom_call_target="tpu_custom_call" | custom-call | bytes 10500000 | tf_op jit(solution)/shard_map/local_part/pallas_call | solution.py:266
  38.9 1.8 %collective-permute-done.12 = f32[200,128]{1,0:T(8,128)S(1)} collective-permute-done((f32[200,128]{1,0:T(8,128)S(1)}, f32[200,128]{1,0:T(8,128)S(1)}, u32[]{:S(2)}, u32[]{:S(2)}) %collective-permute-start.12) | collective-permute-done | bytes 102432 | tf_op jit(solution)/shard_map/ppermute | solution.py:387
  40.7 0.9 %collective-permute-start.15 = (f32[200,128]{1,0:T(8,128)S(1)}, f32[200,128]{1,0:T(8,128)S(1)}, u32[]{:S(2)}, u32[]{:S(2)}) collective-permute-start(f32[200,128]{1,0:T(8,128)S(1)} %select_add_fusion.own_ref), channel_id=1, source_target_pairs={{0,64},{8,72},{16,80},{24,88},{32,96},{40,104},{48,112},{56,120},{... | collective-permute-start | bytes 307208 | tf_op jit(solution)/shard_map/ppermute | solution.py:387
  42.3 2.2 %local_part.5 = (f32[2,3,64,512]{3,2,1,0:T(8,128)S(1)}, f32[200,128]{1,0:T(8,128)S(1)}) custom-call(s32[8]{0:T(128)S(1)} %fusion.7.order_ref, bf16[3,64,4096]{2,1,0:T(8,128)(2,1)S(1)} %copy-done, f32[12,3,4096]{2,1,0:T(4,128)S(1)} %decay_rows.1.refs_1_.refs_3_.row_ref, f32[12,3,4096]{2,1,0:T(4,128)S(1)} %copy-done.1, ...), custom_call_target="tpu_custom_call" | custom-call | bytes 7000000 | tf_op jit(solution)/shard_map/local_part/pallas_call | solution.py:266
  44.5 1.0 %collective-permute-done.15 = f32[200,128]{1,0:T(8,128)S(1)} collective-permute-done((f32[200,128]{1,0:T(8,128)S(1)}, f32[200,128]{1,0:T(8,128)S(1)}, u32[]{:S(2)}, u32[]{:S(2)}) %collective-permute-start.15) | collective-permute-done | bytes 102432 | tf_op jit(solution)/shard_map/ppermute | solution.py:387
  45.6 0.6 %collective-permute-start.16 = (bf16[192,128]{1,0:T(8,128)(2,1)S(1)}, bf16[192,128]{1,0:T(8,128)(2,1)S(1)}, u32[]{:S(2)}, u32[]{:S(2)}) collective-permute-start(bf16[192,128]{1,0:T(8,128)(2,1)S(1)} %fusion.1.refs_15_), channel_id=1, source_target_pairs={{0,192},{8,200},{16,208},{24,216},{32,224},{40,232},{48,240},{56,2... | collective-permute-start | bytes 147464 | tf_op jit(solution)/shard_map/ppermute | solution.py:387
  46.2 2.5 %cross_part.2 = (f32[3,3,64,512]{3,2,1,0:T(8,128)S(1)}, f32[3,3,64,512]{3,2,1,0:T(8,128)S(1)}, f32[2,3,64,512]{3,2,1,0:T(8,128)S(1)}) custom-call(s32[8]{0:T(128)S(1)} %fusion.7.order_ref, s32[5]{0:T(128)S(1)} %shift-right-arithmetic_and_fusion.bits_ref, ...), custom_call_target="tpu_custom_call", output_to_operand_aliasing={{0}: (16, {}), {1}: (17, {}), {2}: (18, {})} | custom-call | bytes 17500000 | tf_op jit(solution)/shard_map/cross_part/pallas_call | solution.py:334
  48.7 2.3 %collective-permute-done.16.refs_0_ = bf16[192,128]{1,0:T(8,128)(2,1)S(1)} collective-permute-done((bf16[192,128]{1,0:T(8,128)(2,1)S(1)}, bf16[192,128]{1,0:T(8,128)(2,1)S(1)}, u32[]{:S(2)}, u32[]{:S(2)}) %collective-permute-start.16) | collective-permute-done | bytes 49184 | tf_op jit(solution)/shard_map/ppermute | solution.py:387
  51.0 1.9 %cross_part.3 = bf16[3,64,4096]{2,1,0:T(8,128)(2,1)} custom-call(s32[8]{0:T(128)S(1)} %fusion.7.order_ref, s32[5]{0:T(128)S(1)} %shift-right-arithmetic_and_fusion.bits_ref, f32[12,3,4096]{2,1,0:T(4,128)S(1)} %decay_rows.1.refs_1_.refs_3_.row_ref, f32[12,3,4096]{2,1,0:T(4,128)S(1)} %copy-done.1, bf16[192,128]{1,0:T(8,128)(2,1)S(1)} %collective-permute-done.16.refs_0_, ...), custom_call_target="tpu_custom_call" | custom-call | bytes 7000000 | tf_op jit(solution)/shard_map/cross_part/pallas_call | solution.py:334
  (48 shorter events, 0.4 us)
Async XLA Ops:
  0.0 10.6 %copy-start.2 = (bf16[128,512]{1,0:T(8,128)(2,1)S(1)}, bf16[128,512]{1,0:T(8,128)(2,1)}, u32[]{:S(2)}) copy-start(bf16[128,512]{1,0:T(8,128)(2,1)} %refs_0_.3) | copy-start | bytes 393220
  0.0 10.6 %collective-permute-start.1 = (bf16[128,512]{1,0:T(8,128)(2,1)}, bf16[128,512]{1,0:T(8,128)(2,1)S(1)}, u32[]{:S(2)}, u32[]{:S(2)}) collective-permute-start(bf16[128,512]{1,0:T(8,128)(2,1)} %refs_0_.3), channel_id=1, source_target_pairs={{0,2},{1,3},{2,4},{3,5},{4,6},{5,7},{6,0},{7,1},{8,10},{9,11},{10,... | collective-permute-start | bytes 393224 | tf_op jit(solution)/shard_map/ppermute | solution.py:364
  1.6 9.0 %collective-permute-start = (bf16[128,512]{1,0:T(8,128)(2,1)}, bf16[128,512]{1,0:T(8,128)(2,1)S(1)}, u32[]{:S(2)}, u32[]{:S(2)}) collective-permute-start(bf16[128,512]{1,0:T(8,128)(2,1)} %refs_0_.3), channel_id=1, source_target_pairs={{0,6},{1,7},{2,0},{3,1},{4,2},{5,3},{6,4},{7,5},{8,14},{9,15},{10,... | collective-permute-start | bytes 393224 | tf_op jit(solution)/shard_map/ppermute | solution.py:364
  3.2 8.1 %collective-permute-start.5 = (bf16[128,512]{1,0:T(8,128)(2,1)}, bf16[128,512]{1,0:T(8,128)(2,1)S(1)}, u32[]{:S(2)}, u32[]{:S(2)}) collective-permute-start(bf16[128,512]{1,0:T(8,128)(2,1)} %refs_0_.3), channel_id=1, source_target_pairs={{0,4},{1,5},{2,6},{3,7},{4,0},{5,1},{6,2},{7,3},{8,12},{9,13},{10,... | collective-permute-start | bytes 393224 | tf_op jit(solution)/shard_map/ppermute | solution.py:364
  5.2 0.8 %copy-start.4 = (f32[3,4096]{1,0:T(4,128)S(1)}, f32[3,4096]{1,0:T(4,128)}, u32[]{:S(2)}) copy-start(f32[3,4096]{1,0:T(4,128)} %ld_ref.1) | copy-start | bytes 147460
  8.5 0.9 %copy-start.3 = (bf16[128,512]{1,0:T(8,128)(2,1)S(1)}, bf16[128,512]{1,0:T(8,128)(2,1)}, u32[]{:S(2)}) copy-start(bf16[128,512]{1,0:T(8,128)(2,1)} %refs_0_.2) | copy-start | bytes 393220
  9.4 2.3 %copy-start = (bf16[3,64,4096]{2,1,0:T(8,128)(2,1)S(1)}, bf16[3,64,4096]{2,1,0:T(8,128)(2,1)}, u32[]{:S(2)}) copy-start(bf16[3,64,4096]{2,1,0:T(8,128)(2,1)} %v_ref.9) | copy-start | bytes 4718596
  9.5 15.2 %collective-permute-start.8 = (bf16[128,512]{1,0:T(8,128)(2,1)S(1)}, bf16[128,512]{1,0:T(8,128)(2,1)}, u32[]{:S(2)}, u32[]{:S(2)}) collective-permute-start(bf16[128,512]{1,0:T(8,128)(2,1)S(1)} %hold.3.refs_4_.refs_0_.p0), channel_id=1, source_target_pairs={{0,6},{1,7},{2,0},{3,1},{4,2},{5,3},{6,4},{7,5},{8,14},{9,15},{10,... | collective-permute-start | bytes 393224 | tf_op jit(solution)/shard_map/ppermute | solution.py:364
  10.6 2.7 %collective-permute-start.2 = (bf16[128,512]{1,0:T(8,128)(2,1)S(1)}, bf16[128,512]{1,0:T(8,128)(2,1)S(1)}, u32[]{:S(2)}, u32[]{:S(2)}) collective-permute-start(bf16[128,512]{1,0:T(8,128)(2,1)S(1)} %get-tuple-element.22.refs_0_), channel_id=1, source_target_pairs={{0,1},{1,0},{2,3},{3,2},{4,5},{5,4},{6,7},{7,6},{8,9},{9,8},{10,11... | collective-permute-start | bytes 393224 | tf_op jit(solution)/shard_map/ppermute | solution.py:368
  10.7 2.6 %collective-permute-start.3 = (bf16[128,512]{1,0:T(8,128)(2,1)S(1)}, bf16[128,512]{1,0:T(8,128)(2,1)S(1)}, u32[]{:S(2)}, u32[]{:S(2)}) collective-permute-start(bf16[128,512]{1,0:T(8,128)(2,1)S(1)} %get-tuple-element.23.refs_1_), channel_id=1, source_target_pairs={{0,1},{1,0},{2,3},{3,2},{4,5},{5,4},{6,7},{7,6},{8,9},{9,8},{10,11... | collective-permute-start | bytes 393224 | tf_op jit(solution)/shard_map/ppermute | solution.py:368
  11.2 2.1 %collective-permute-start.4 = (bf16[128,512]{1,0:T(8,128)(2,1)S(1)}, bf16[128,512]{1,0:T(8,128)(2,1)S(1)}, u32[]{:S(2)}, u32[]{:S(2)}) collective-permute-start(bf16[128,512]{1,0:T(8,128)(2,1)S(1)} %get-tuple-element.24.refs_2_), channel_id=1, source_target_pairs={{0,1},{1,0},{2,3},{3,2},{4,5},{5,4},{6,7},{7,6},{8,9},{9,8},{10,11... | collective-permute-start | bytes 393224 | tf_op jit(solution)/shard_map/ppermute | solution.py:368
  11.3 1.9 %collective-permute-start.6 = (bf16[128,512]{1,0:T(8,128)(2,1)S(1)}, bf16[128,512]{1,0:T(8,128)(2,1)S(1)}, u32[]{:S(2)}, u32[]{:S(2)}) collective-permute-start(bf16[128,512]{1,0:T(8,128)(2,1)S(1)} %collective-permute-done.5.refs_3_.refs_0_), channel_id=1, source_target_pairs={{0,1},{1,0},{2,3},{3,2},{4,5},{5,4},{6,7},{7,6},{8,9},{9,8},{10,11... | collective-permute-start | bytes 393224 | tf_op jit(solution)/shard_map/ppermute | solution.py:368
  15.5 12.5 %copy-start.1 = (f32[12,3,4096]{2,1,0:T(4,128)S(1)}, f32[12,3,4096]{2,1,0:T(4,128)}, u32[]{:S(2)}) copy-start(f32[12,3,4096]{2,1,0:T(4,128)} %lw_ref.9) | copy-start | bytes 1769476
  15.5 5.2 %collective-permute-start.7 = (f32[200,128]{1,0:T(8,128)S(1)}, f32[200,128]{1,0:T(8,128)S(1)}, u32[]{:S(2)}, u32[]{:S(2)}) collective-permute-start(f32[200,128]{1,0:T(8,128)S(1)} %get-tuple-element.27.refs_1_), channel_id=1, source_target_pairs={{0,8},{8,0},{16,24},{24,16},{32,40},{40,32},{48,56},{56,48},{64,72... | collective-permute-start | bytes 307208 | tf_op jit(solution)/shard_map/ppermute | solution.py:387
  18.8 8.0 %collective-permute-start.9 = (bf16[128,512]{1,0:T(8,128)(2,1)S(1)}, bf16[128,512]{1,0:T(8,128)(2,1)S(1)}, u32[]{:S(2)}, u32[]{:S(2)}) collective-permute-start(bf16[128,512]{1,0:T(8,128)(2,1)S(1)} %hold.5), channel_id=1, source_target_pairs={{0,2},{1,3},{2,4},{3,5},{4,6},{5,7},{6,0},{7,1},{8,10},{9,11},{10,... | collective-permute-start | bytes 393224 | tf_op jit(solution)/shard_map/ppermute | solution.py:364
  20.7 10.2 %collective-permute-start.10 = (f32[200,128]{1,0:T(8,128)S(1)}, f32[200,128]{1,0:T(8,128)S(1)}, u32[]{:S(2)}, u32[]{:S(2)}) collective-permute-start(f32[200,128]{1,0:T(8,128)S(1)} %select_add_fusion.2.own_ref), channel_id=1, source_target_pairs={{0,16},{8,24},{16,0},{24,8},{32,48},{40,56},{48,32},{56,40},{64,80... | collective-permute-start | bytes 307208 | tf_op jit(solution)/shard_map/ppermute | solution.py:387
  24.7 10.9 %collective-permute-start.13 = (bf16[128,512]{1,0:T(8,128)(2,1)}, bf16[128,512]{1,0:T(8,128)(2,1)S(1)}, u32[]{:S(2)}, u32[]{:S(2)}) collective-permute-start(bf16[128,512]{1,0:T(8,128)(2,1)} %collective-permute-done.8.p1), channel_id=1, source_target_pairs={{0,6},{1,7},{2,0},{3,1},{4,2},{5,3},{6,4},{7,5},{8,14},{9,15},{10,... | collective-permute-start | bytes 393224 | tf_op jit(solution)/shard_map/ppermute | solution.py:364
  27.7 8.2 %collective-permute-start.11 = (bf16[3,128,512]{2,1,0:T(8,128)(2,1)S(1)}, bf16[3,128,512]{2,1,0:T(8,128)(2,1)S(1)}, u32[]{:S(2)}, u32[]{:S(2)}) collective-permute-start(bf16[3,128,512]{2,1,0:T(8,128)(2,1)S(1)} %stack_pieces.1.refs_4_.refs_8_.refs_2_), channel_id=1, source_target_pairs={{0,1},{1,0},{2,3},{3,2},{4,5},{5,4},{6,7},{7,6},{8,9},{9,8},{10,11... | collective-permute-start | bytes 1179656 | tf_op jit(solution)/shard_map/ppermute | solution.py:368
  31.0 9.7 %collective-permute-start.12 = (f32[200,128]{1,0:T(8,128)S(1)}, f32[200,128]{1,0:T(8,128)S(1)}, u32[]{:S(2)}, u32[]{:S(2)}) collective-permute-start(f32[200,128]{1,0:T(8,128)S(1)} %select_add_fusion.1.own_ref), channel_id=1, source_target_pairs={{0,56},{8,48},{16,40},{24,32},{32,24},{40,16},{48,8},{56,0},{64,12... | collective-permute-start | bytes 307208 | tf_op jit(solution)/shard_map/ppermute | solution.py:387
  35.6 6.7 %collective-permute-start.14 = (bf16[128,512]{1,0:T(8,128)(2,1)S(1)}, bf16[128,512]{1,0:T(8,128)(2,1)S(1)}, u32[]{:S(2)}, u32[]{:S(2)}) collective-permute-start(bf16[128,512]{1,0:T(8,128)(2,1)S(1)} %collective-permute-done.13), channel_id=1, source_target_pairs={{0,1},{1,0},{2,3},{3,2},{4,5},{5,4},{6,7},{7,6},{8,9},{9,8},{10,11... | collective-permute-start | bytes 393224 | tf_op jit(solution)/shard_map/ppermute | solution.py:368
  40.7 4.8 %collective-permute-start.15 = (f32[200,128]{1,0:T(8,128)S(1)}, f32[200,128]{1,0:T(8,128)S(1)}, u32[]{:S(2)}, u32[]{:S(2)}) collective-permute-start(f32[200,128]{1,0:T(8,128)S(1)} %select_add_fusion.own_ref), channel_id=1, source_target_pairs={{0,64},{8,72},{16,80},{24,88},{32,96},{40,104},{48,112},{56,120},{... | collective-permute-start | bytes 307208 | tf_op jit(solution)/shard_map/ppermute | solution.py:387
  45.6 5.4 %collective-permute-start.16 = (bf16[192,128]{1,0:T(8,128)(2,1)S(1)}, bf16[192,128]{1,0:T(8,128)(2,1)S(1)}, u32[]{:S(2)}, u32[]{:S(2)}) collective-permute-start(bf16[192,128]{1,0:T(8,128)(2,1)S(1)} %fusion.1.refs_15_), channel_id=1, source_target_pairs={{0,192},{8,200},{16,208},{24,216},{32,224},{40,232},{48,240},{56,2... | collective-permute-start | bytes 147464 | tf_op jit(solution)/shard_map/ppermute | solution.py:387

commit v5 on v4

--- a/solution.py
+++ b/solution.py
@@ -375,7 +375,7 @@
     elif r == 1:
         z = z ^ 2
     elif r == 2:
-        z = 7 - z
+        z = z ^ 6
     elif r == 3:
         x = x ^ 1
     else:

time: 53.3 us -> 53.1 us (level)
  waiting for transfers between devices: 6.01 us -> 5.21 us
    ppermute x5, waiting for transfers between devices: 5.98 us -> 5.18 us  [exchange(): return lax.ppermute(x, 'seq', [(i, partner(r, i)) for i in range(32)])]
where the time goes in v5:
time: 53.1 us; the launch traced here: 52.8 us
  starting transfers between devices  22.4 us (42%)
  Pallas kernels  19.6 us (37%)
  waiting for transfers between devices  5.21 us (10%)
  between operations  2.97 us (6%)
  local copies, waits for them, and re-layouts  2.5 us (5%)
    ppermute x5, starting transfers between devices, exchange(): return lax.ppermute(x, 'seq', [(i, partner(r, i)) for i in range(32)])  11.2 us
    ppermute x6, starting transfers between devices, y_shift(): lax.ppermute(x, 'head', [(i, (i // 2 + k) % 4 * 2 + i % 2) for i in range...  9.44 us
    pallas_call x3, Pallas kernels, local_part(): pl.pallas_call(functools.partial(local_kernel, pieces), out_shape=[jax.Sh...  8.07 us
    ppermute x5, waiting for transfers between devices, exchange(): return lax.ppermute(x, 'seq', [(i, partner(r, i)) for i in range(32)])  5.18 us
    pallas_call x2, Pallas kernels, cross_part(): pl.pallas_call(functools.partial(cross_kernel, rounds, tuple((x.shape[0]...  4.41 us
    pallas_call x2, Pallas kernels, block_states(): pl.pallas_call(functools.partial(state_kernel, group), out_shape=[agg] +...  3.63 us
    pallas_call x1, Pallas kernels, decay_rows(): pl.pallas_call(decay_kernel, out_shape=jax.ShapeDtypeStruct((12, HEADS, T...  2.46 us
    unnamed x10, local copies, waits for them, and re-layouts  1.76 us
  transfers between devices with their start and end apart: 17, of which 4 were waited for; matrix products, arithmetic and copies ran while one was open for 2% of the time, Pallas kernels for 33%

profile of v5, /device:TPU:6, one launch (start us, length us, event | category | flops | bytes accessed | tf_op | source)
XLA Modules:
  0.0 52.8 jit_solution(8800942977269755167)
XLA Ops:
  0.0 1.6 %collective-permute-start.1 = (bf16[128,512]{1,0:T(8,128)(2,1)}, bf16[128,512]{1,0:T(8,128)(2,1)S(1)}, u32[]{:S(2)}, u32[]{:S(2)}) collective-permute-start(bf16[128,512]{1,0:T(8,128)(2,1)} %refs_0_.3), channel_id=1, source_target_pairs={{0,2},{1,3},{2,4},{3,5},{4,6},{5,7},{6,0},{7,1},{8,10},{9,11},{10,... | collective-permute-start | bytes 393224 | tf_op jit(solution)/shard_map/ppermute | solution.py:364
  1.6 1.7 %collective-permute-start = (bf16[128,512]{1,0:T(8,128)(2,1)}, bf16[128,512]{1,0:T(8,128)(2,1)S(1)}, u32[]{:S(2)}, u32[]{:S(2)}) collective-permute-start(bf16[128,512]{1,0:T(8,128)(2,1)} %refs_0_.3), channel_id=1, source_target_pairs={{0,6},{1,7},{2,0},{3,1},{4,2},{5,3},{6,4},{7,5},{8,14},{9,15},{10,... | collective-permute-start | bytes 393224 | tf_op jit(solution)/shard_map/ppermute | solution.py:364
  3.2 2.0 %collective-permute-start.5 = (bf16[128,512]{1,0:T(8,128)(2,1)}, bf16[128,512]{1,0:T(8,128)(2,1)S(1)}, u32[]{:S(2)}, u32[]{:S(2)}) collective-permute-start(bf16[128,512]{1,0:T(8,128)(2,1)} %refs_0_.3), channel_id=1, source_target_pairs={{0,4},{1,5},{2,6},{3,7},{4,0},{5,1},{6,2},{7,3},{8,12},{9,13},{10,... | collective-permute-start | bytes 393224 | tf_op jit(solution)/shard_map/ppermute | solution.py:364
  5.2 0.8 %copy-done.4 = f32[3,4096]{1,0:T(4,128)S(1)} copy-done((f32[3,4096]{1,0:T(4,128)S(1)}, f32[3,4096]{1,0:T(4,128)}, u32[]{:S(2)}) %copy-start.4) | copy-done | bytes 49176
  6.1 2.5 %decay_rows.1.refs_1_.refs_3_.row_ref = f32[12,3,4096]{2,1,0:T(4,128)S(1)} custom-call(f32[3,4096]{1,0:T(4,128)S(1)} %copy-done.4), custom_call_target="tpu_custom_call" | custom-call | bytes 7000000 | tf_op jit(solution)/shard_map/decay_rows/pallas_call | solution.py:91
  8.5 0.9 %copy-done.3 = bf16[128,512]{1,0:T(8,128)(2,1)S(1)} copy-done((bf16[128,512]{1,0:T(8,128)(2,1)S(1)}, bf16[128,512]{1,0:T(8,128)(2,1)}, u32[]{:S(2)}) %copy-start.3) | copy-done | bytes 131096
  9.5 1.1 %collective-permute-start.8 = (bf16[128,512]{1,0:T(8,128)(2,1)S(1)}, bf16[128,512]{1,0:T(8,128)(2,1)}, u32[]{:S(2)}, u32[]{:S(2)}) collective-permute-start(bf16[128,512]{1,0:T(8,128)(2,1)S(1)} %hold.3.refs_4_.refs_0_.p0), channel_id=1, source_target_pairs={{0,6},{1,7},{2,0},{3,1},{4,2},{5,3},{6,4},{7,5},{8,14},{9,15},{10,... | collective-permute-start | bytes 393224 | tf_op jit(solution)/shard_map/ppermute | solution.py:364
  10.7 0.5 collective-permute-start.3
  11.2 0.1 collective-permute-start.4
  11.3 0.4 collective-permute-start.6
  11.8 1.5 %block_states.2 = (bf16[3,7,192,128]{3,2,1,0:T(8,128)(2,1)S(1)}, f32[3,192,128]{2,1,0:T(8,128)S(1)}) custom-call(s32[8]{0:T(128)S(1)} %fusion.7.order_ref, bf16[3,64,4096]{2,1,0:T(8,128)(2,1)S(1)} %copy-done, f32[12,3,4096]{2,1,0:T(4,128)S(1)} %decay_rows.1.refs_1_.refs_3_.row_ref, bf16[128,512]{1,0:T(8,128)(2,1)S(1)} %get-tuple-element.22.refs_0_, ...), custom_call_target="tpu_custom_call" | custom-call | bytes 5250000 | tf_op jit(solution)/shard_map/block_states/pallas_call | solution.py:207
  13.3 2.1 %block_states.3 = (bf16[5,7,192,128]{3,2,1,0:T(8,128)(2,1)S(1)}, bf16[7,192,128]{2,1,0:T(8,128)(2,1)S(1)}, f32[200,128]{1,0:T(8,128)S(1)}) custom-call(s32[8]{0:T(128)S(1)} %fusion.7.order_ref, bf16[3,64,4096]{2,1,0:T(8,128)(2,1)S(1)} %copy-done, f32[12,3,4096]{2,1,0:T(4,128)S(1)} %decay_rows.1.refs_1_.refs_3_.row_ref, ...), custom_call_target="tpu_custom_call" | custom-call | bytes 5250000 | tf_op jit(solution)/shard_map/block_states/pallas_call | solution.py:207
  15.5 2.0 %collective-permute-start.7 = (f32[200,128]{1,0:T(8,128)S(1)}, f32[200,128]{1,0:T(8,128)S(1)}, u32[]{:S(2)}, u32[]{:S(2)}) collective-permute-start(f32[200,128]{1,0:T(8,128)S(1)} %get-tuple-element.27.refs_1_), channel_id=1, source_target_pairs={{0,8},{8,0},{16,24},{24,16},{32,40},{40,32},{48,56},{56,48},{64,72... | collective-permute-start | bytes 307208 | tf_op jit(solution)/shard_map/ppermute | solution.py:387
  17.5 0.6 %fusion.8 = (s32[1]{0:T(128)}, s32[1]{0:T(128)}, s32[1]{0:T(128)}, s32[1]{0:T(128)}) fusion(s32[5]{0:T(128)S(1)} %shift-right-arithmetic_and_fusion.bits_ref), kind=kLoop, calls=%fused_computation.29 | loop fusion | bytes 32 | tf_op jit(solution)/shard_map/slice | solution.py:353
  18.8 1.0 %collective-permute-start.9 = (bf16[128,512]{1,0:T(8,128)(2,1)S(1)}, bf16[128,512]{1,0:T(8,128)(2,1)S(1)}, u32[]{:S(2)}, u32[]{:S(2)}) collective-permute-start(bf16[128,512]{1,0:T(8,128)(2,1)S(1)} %hold.5), channel_id=1, source_target_pairs={{0,2},{1,3},{2,4},{3,5},{4,6},{5,7},{6,0},{7,1},{8,10},{9,11},{10,... | collective-permute-start | bytes 393224 | tf_op jit(solution)/shard_map/ppermute | solution.py:364
  19.8 0.8 %collective-permute-done.7 = f32[200,128]{1,0:T(8,128)S(1)} collective-permute-done((f32[200,128]{1,0:T(8,128)S(1)}, f32[200,128]{1,0:T(8,128)S(1)}, u32[]{:S(2)}, u32[]{:S(2)}) %collective-permute-start.7) | collective-permute-done | bytes 102432 | tf_op jit(solution)/shard_map/ppermute | solution.py:387
  20.7 3.4 %collective-permute-start.10 = (f32[200,128]{1,0:T(8,128)S(1)}, f32[200,128]{1,0:T(8,128)S(1)}, u32[]{:S(2)}, u32[]{:S(2)}) collective-permute-start(f32[200,128]{1,0:T(8,128)S(1)} %select_add_fusion.2.own_ref), channel_id=1, source_target_pairs={{0,16},{8,24},{16,0},{24,8},{32,48},{40,56},{48,32},{56,40},{64,80... | collective-permute-start | bytes 307208 | tf_op jit(solution)/shard_map/ppermute | solution.py:387
  24.7 2.0 %collective-permute-start.13 = (bf16[128,512]{1,0:T(8,128)(2,1)}, bf16[128,512]{1,0:T(8,128)(2,1)S(1)}, u32[]{:S(2)}, u32[]{:S(2)}) collective-permute-start(bf16[128,512]{1,0:T(8,128)(2,1)} %collective-permute-done.8.p1), channel_id=1, source_target_pairs={{0,6},{1,7},{2,0},{3,1},{4,2},{5,3},{6,4},{7,5},{8,14},{9,15},{10,... | collective-permute-start | bytes 393224 | tf_op jit(solution)/shard_map/ppermute | solution.py:364
  26.7 1.0 %stack_pieces.1.refs_4_.refs_8_.refs_2_ = bf16[3,128,512]{2,1,0:T(8,128)(2,1)S(1)} custom-call(bf16[128,512]{1,0:T(8,128)(2,1)S(1)} %hold.3.refs_4_.refs_0_.p0, bf16[128,512]{1,0:T(8,128)(2,1)} %collective-permute-done.8.p1, bf16[128,512]{1,0:T(8,128)(2,1)S(1)} %collective-permute-done.9.p2), custom_call_target="tpu_custom_call" | custom-call | bytes 700000 | tf_op jit(solution)/shard_map/stack_pieces/pallas_call | solution.py:129
  27.7 0.3 collective-permute-start.11
  28.0 2.9 %local_part.3 = (f32[3,3,64,512]{3,2,1,0:T(8,128)S(1)}, f32[200,128]{1,0:T(8,128)S(1)}) custom-call(s32[8]{0:T(128)S(1)} %fusion.7.order_ref, bf16[3,64,4096]{2,1,0:T(8,128)(2,1)S(1)} %copy-done, f32[12,3,4096]{2,1,0:T(4,128)S(1)} %decay_rows.1.refs_1_.refs_3_.row_ref, f32[12,3,4096]{2,1,0:T(4,128)S(1)} %copy-done.1, ...), custom_call_target="tpu_custom_call" | custom-call | bytes 10500000 | tf_op jit(solution)/shard_map/local_part/pallas_call | solution.py:266
  31.0 4.4 %collective-permute-start.12 = (f32[200,128]{1,0:T(8,128)S(1)}, f32[200,128]{1,0:T(8,128)S(1)}, u32[]{:S(2)}, u32[]{:S(2)}) collective-permute-start(f32[200,128]{1,0:T(8,128)S(1)} %select_add_fusion.1.own_ref), channel_id=1, source_target_pairs={{0,48},{8,56},{16,32},{24,40},{32,16},{40,24},{48,0},{56,8},{64,11... | collective-permute-start | bytes 307208 | tf_op jit(solution)/shard_map/ppermute | solution.py:387
  36.0 0.3 collective-permute-start.14
  36.3 2.9 %local_part.4 = (f32[3,3,64,512]{3,2,1,0:T(8,128)S(1)}, f32[200,128]{1,0:T(8,128)S(1)}) custom-call(s32[8]{0:T(128)S(1)} %fusion.7.order_ref, bf16[3,64,4096]{2,1,0:T(8,128)(2,1)S(1)} %copy-done, f32[12,3,4096]{2,1,0:T(4,128)S(1)} %decay_rows.1.refs_1_.refs_3_.row_ref, f32[12,3,4096]{2,1,0:T(4,128)S(1)} %copy-done.1, ...), custom_call_target="tpu_custom_call" | custom-call | bytes 10500000 | tf_op jit(solution)/shard_map/local_part/pallas_call | solution.py:266
  39.3 1.1 %collective-permute-done.12 = f32[200,128]{1,0:T(8,128)S(1)} collective-permute-done((f32[200,128]{1,0:T(8,128)S(1)}, f32[200,128]{1,0:T(8,128)S(1)}, u32[]{:S(2)}, u32[]{:S(2)}) %collective-permute-start.12) | collective-permute-done | bytes 102432 | tf_op jit(solution)/shard_map/ppermute | solution.py:387
  40.4 0.9 %collective-permute-start.15 = (f32[200,128]{1,0:T(8,128)S(1)}, f32[200,128]{1,0:T(8,128)S(1)}, u32[]{:S(2)}, u32[]{:S(2)}) collective-permute-start(f32[200,128]{1,0:T(8,128)S(1)} %select_add_fusion.own_ref), channel_id=1, source_target_pairs={{0,64},{8,72},{16,80},{24,88},{32,96},{40,104},{48,112},{56,120},{... | collective-permute-start | bytes 307208 | tf_op jit(solution)/shard_map/ppermute | solution.py:387
  42.0 2.2 %local_part.5 = (f32[2,3,64,512]{3,2,1,0:T(8,128)S(1)}, f32[200,128]{1,0:T(8,128)S(1)}) custom-call(s32[8]{0:T(128)S(1)} %fusion.7.order_ref, bf16[3,64,4096]{2,1,0:T(8,128)(2,1)S(1)} %copy-done, f32[12,3,4096]{2,1,0:T(4,128)S(1)} %decay_rows.1.refs_1_.refs_3_.row_ref, f32[12,3,4096]{2,1,0:T(4,128)S(1)} %copy-done.1, ...), custom_call_target="tpu_custom_call" | custom-call | bytes 7000000 | tf_op jit(solution)/shard_map/local_part/pallas_call | solution.py:266
  44.2 1.0 %collective-permute-done.15 = f32[200,128]{1,0:T(8,128)S(1)} collective-permute-done((f32[200,128]{1,0:T(8,128)S(1)}, f32[200,128]{1,0:T(8,128)S(1)}, u32[]{:S(2)}, u32[]{:S(2)}) %collective-permute-start.15) | collective-permute-done | bytes 102432 | tf_op jit(solution)/shard_map/ppermute | solution.py:387
  45.3 0.6 %collective-permute-start.16 = (bf16[192,128]{1,0:T(8,128)(2,1)S(1)}, bf16[192,128]{1,0:T(8,128)(2,1)S(1)}, u32[]{:S(2)}, u32[]{:S(2)}) collective-permute-start(bf16[192,128]{1,0:T(8,128)(2,1)S(1)} %fusion.1.refs_15_), channel_id=1, source_target_pairs={{0,192},{8,200},{16,208},{24,216},{32,224},{40,232},{48,240},{56,2... | collective-permute-start | bytes 147464 | tf_op jit(solution)/shard_map/ppermute | solution.py:387
  45.9 2.5 %cross_part.2 = (f32[3,3,64,512]{3,2,1,0:T(8,128)S(1)}, f32[3,3,64,512]{3,2,1,0:T(8,128)S(1)}, f32[2,3,64,512]{3,2,1,0:T(8,128)S(1)}) custom-call(s32[8]{0:T(128)S(1)} %fusion.7.order_ref, s32[5]{0:T(128)S(1)} %shift-right-arithmetic_and_fusion.bits_ref, ...), custom_call_target="tpu_custom_call", output_to_operand_aliasing={{0}: (16, {}), {1}: (17, {}), {2}: (18, {})} | custom-call | bytes 17500000 | tf_op jit(solution)/shard_map/cross_part/pallas_call | solution.py:334
  48.3 2.3 %collective-permute-done.16.refs_0_ = bf16[192,128]{1,0:T(8,128)(2,1)S(1)} collective-permute-done((bf16[192,128]{1,0:T(8,128)(2,1)S(1)}, bf16[192,128]{1,0:T(8,128)(2,1)S(1)}, u32[]{:S(2)}, u32[]{:S(2)}) %collective-permute-start.16) | collective-permute-done | bytes 49184 | tf_op jit(solution)/shard_map/ppermute | solution.py:387
  50.6 1.9 %cross_part.3 = bf16[3,64,4096]{2,1,0:T(8,128)(2,1)} custom-call(s32[8]{0:T(128)S(1)} %fusion.7.order_ref, s32[5]{0:T(128)S(1)} %shift-right-arithmetic_and_fusion.bits_ref, f32[12,3,4096]{2,1,0:T(4,128)S(1)} %decay_rows.1.refs_1_.refs_3_.row_ref, f32[12,3,4096]{2,1,0:T(4,128)S(1)} %copy-done.1, bf16[192,128]{1,0:T(8,128)(2,1)S(1)} %collective-permute-done.16.refs_0_, ...), custom_call_target="tpu_custom_call" | custom-call | bytes 7000000 | tf_op jit(solution)/shard_map/cross_part/pallas_call | solution.py:334
  (48 shorter events, 0.4 us)
Async XLA Ops:
  0.0 10.6 %copy-start.2 = (bf16[128,512]{1,0:T(8,128)(2,1)S(1)}, bf16[128,512]{1,0:T(8,128)(2,1)}, u32[]{:S(2)}) copy-start(bf16[128,512]{1,0:T(8,128)(2,1)} %refs_0_.3) | copy-start | bytes 393220
  0.0 10.6 %collective-permute-start.1 = (bf16[128,512]{1,0:T(8,128)(2,1)}, bf16[128,512]{1,0:T(8,128)(2,1)S(1)}, u32[]{:S(2)}, u32[]{:S(2)}) collective-permute-start(bf16[128,512]{1,0:T(8,128)(2,1)} %refs_0_.3), channel_id=1, source_target_pairs={{0,2},{1,3},{2,4},{3,5},{4,6},{5,7},{6,0},{7,1},{8,10},{9,11},{10,... | collective-permute-start | bytes 393224 | tf_op jit(solution)/shard_map/ppermute | solution.py:364
  1.6 9.0 %collective-permute-start = (bf16[128,512]{1,0:T(8,128)(2,1)}, bf16[128,512]{1,0:T(8,128)(2,1)S(1)}, u32[]{:S(2)}, u32[]{:S(2)}) collective-permute-start(bf16[128,512]{1,0:T(8,128)(2,1)} %refs_0_.3), channel_id=1, source_target_pairs={{0,6},{1,7},{2,0},{3,1},{4,2},{5,3},{6,4},{7,5},{8,14},{9,15},{10,... | collective-permute-start | bytes 393224 | tf_op jit(solution)/shard_map/ppermute | solution.py:364
  3.2 8.1 %collective-permute-start.5 = (bf16[128,512]{1,0:T(8,128)(2,1)}, bf16[128,512]{1,0:T(8,128)(2,1)S(1)}, u32[]{:S(2)}, u32[]{:S(2)}) collective-permute-start(bf16[128,512]{1,0:T(8,128)(2,1)} %refs_0_.3), channel_id=1, source_target_pairs={{0,4},{1,5},{2,6},{3,7},{4,0},{5,1},{6,2},{7,3},{8,12},{9,13},{10,... | collective-permute-start | bytes 393224 | tf_op jit(solution)/shard_map/ppermute | solution.py:364
  5.2 0.8 %copy-start.4 = (f32[3,4096]{1,0:T(4,128)S(1)}, f32[3,4096]{1,0:T(4,128)}, u32[]{:S(2)}) copy-start(f32[3,4096]{1,0:T(4,128)} %ld_ref.1) | copy-start | bytes 147460
  8.5 0.9 %copy-start.3 = (bf16[128,512]{1,0:T(8,128)(2,1)S(1)}, bf16[128,512]{1,0:T(8,128)(2,1)}, u32[]{:S(2)}) copy-start(bf16[128,512]{1,0:T(8,128)(2,1)} %refs_0_.2) | copy-start | bytes 393220
  9.4 2.3 %copy-start = (bf16[3,64,4096]{2,1,0:T(8,128)(2,1)S(1)}, bf16[3,64,4096]{2,1,0:T(8,128)(2,1)}, u32[]{:S(2)}) copy-start(bf16[3,64,4096]{2,1,0:T(8,128)(2,1)} %v_ref.9) | copy-start | bytes 4718596
  9.5 15.2 %collective-permute-start.8 = (bf16[128,512]{1,0:T(8,128)(2,1)S(1)}, bf16[128,512]{1,0:T(8,128)(2,1)}, u32[]{:S(2)}, u32[]{:S(2)}) collective-permute-start(bf16[128,512]{1,0:T(8,128)(2,1)S(1)} %hold.3.refs_4_.refs_0_.p0), channel_id=1, source_target_pairs={{0,6},{1,7},{2,0},{3,1},{4,2},{5,3},{6,4},{7,5},{8,14},{9,15},{10,... | collective-permute-start | bytes 393224 | tf_op jit(solution)/shard_map/ppermute | solution.py:364
  10.6 2.7 %collective-permute-start.2 = (bf16[128,512]{1,0:T(8,128)(2,1)S(1)}, bf16[128,512]{1,0:T(8,128)(2,1)S(1)}, u32[]{:S(2)}, u32[]{:S(2)}) collective-permute-start(bf16[128,512]{1,0:T(8,128)(2,1)S(1)} %get-tuple-element.22.refs_0_), channel_id=1, source_target_pairs={{0,1},{1,0},{2,3},{3,2},{4,5},{5,4},{6,7},{7,6},{8,9},{9,8},{10,11... | collective-permute-start | bytes 393224 | tf_op jit(solution)/shard_map/ppermute | solution.py:368
  10.7 2.6 %collective-permute-start.3 = (bf16[128,512]{1,0:T(8,128)(2,1)S(1)}, bf16[128,512]{1,0:T(8,128)(2,1)S(1)}, u32[]{:S(2)}, u32[]{:S(2)}) collective-permute-start(bf16[128,512]{1,0:T(8,128)(2,1)S(1)} %get-tuple-element.23.refs_1_), channel_id=1, source_target_pairs={{0,1},{1,0},{2,3},{3,2},{4,5},{5,4},{6,7},{7,6},{8,9},{9,8},{10,11... | collective-permute-start | bytes 393224 | tf_op jit(solution)/shard_map/ppermute | solution.py:368
  11.2 2.1 %collective-permute-start.4 = (bf16[128,512]{1,0:T(8,128)(2,1)S(1)}, bf16[128,512]{1,0:T(8,128)(2,1)S(1)}, u32[]{:S(2)}, u32[]{:S(2)}) collective-permute-start(bf16[128,512]{1,0:T(8,128)(2,1)S(1)} %get-tuple-element.24.refs_2_), channel_id=1, source_target_pairs={{0,1},{1,0},{2,3},{3,2},{4,5},{5,4},{6,7},{7,6},{8,9},{9,8},{10,11... | collective-permute-start | bytes 393224 | tf_op jit(solution)/shard_map/ppermute | solution.py:368
  11.3 1.9 %collective-permute-start.6 = (bf16[128,512]{1,0:T(8,128)(2,1)S(1)}, bf16[128,512]{1,0:T(8,128)(2,1)S(1)}, u32[]{:S(2)}, u32[]{:S(2)}) collective-permute-start(bf16[128,512]{1,0:T(8,128)(2,1)S(1)} %collective-permute-done.5.refs_3_.refs_0_), channel_id=1, source_target_pairs={{0,1},{1,0},{2,3},{3,2},{4,5},{5,4},{6,7},{7,6},{8,9},{9,8},{10,11... | collective-permute-start | bytes 393224 | tf_op jit(solution)/shard_map/ppermute | solution.py:368
  15.5 12.5 %copy-start.1 = (f32[12,3,4096]{2,1,0:T(4,128)S(1)}, f32[12,3,4096]{2,1,0:T(4,128)}, u32[]{:S(2)}) copy-start(f32[12,3,4096]{2,1,0:T(4,128)} %lw_ref.9) | copy-start | bytes 1769476
  15.5 5.2 %collective-permute-start.7 = (f32[200,128]{1,0:T(8,128)S(1)}, f32[200,128]{1,0:T(8,128)S(1)}, u32[]{:S(2)}, u32[]{:S(2)}) collective-permute-start(f32[200,128]{1,0:T(8,128)S(1)} %get-tuple-element.27.refs_1_), channel_id=1, source_target_pairs={{0,8},{8,0},{16,24},{24,16},{32,40},{40,32},{48,56},{56,48},{64,72... | collective-permute-start | bytes 307208 | tf_op jit(solution)/shard_map/ppermute | solution.py:387
  18.8 8.0 %collective-permute-start.9 = (bf16[128,512]{1,0:T(8,128)(2,1)S(1)}, bf16[128,512]{1,0:T(8,128)(2,1)S(1)}, u32[]{:S(2)}, u32[]{:S(2)}) collective-permute-start(bf16[128,512]{1,0:T(8,128)(2,1)S(1)} %hold.5), channel_id=1, source_target_pairs={{0,2},{1,3},{2,4},{3,5},{4,6},{5,7},{6,0},{7,1},{8,10},{9,11},{10,... | collective-permute-start | bytes 393224 | tf_op jit(solution)/shard_map/ppermute | solution.py:364
  20.7 10.2 %collective-permute-start.10 = (f32[200,128]{1,0:T(8,128)S(1)}, f32[200,128]{1,0:T(8,128)S(1)}, u32[]{:S(2)}, u32[]{:S(2)}) collective-permute-start(f32[200,128]{1,0:T(8,128)S(1)} %select_add_fusion.2.own_ref), channel_id=1, source_target_pairs={{0,16},{8,24},{16,0},{24,8},{32,48},{40,56},{48,32},{56,40},{64,80... | collective-permute-start | bytes 307208 | tf_op jit(solution)/shard_map/ppermute | solution.py:387
  24.7 11.3 %collective-permute-start.13 = (bf16[128,512]{1,0:T(8,128)(2,1)}, bf16[128,512]{1,0:T(8,128)(2,1)S(1)}, u32[]{:S(2)}, u32[]{:S(2)}) collective-permute-start(bf16[128,512]{1,0:T(8,128)(2,1)} %collective-permute-done.8.p1), channel_id=1, source_target_pairs={{0,6},{1,7},{2,0},{3,1},{4,2},{5,3},{6,4},{7,5},{8,14},{9,15},{10,... | collective-permute-start | bytes 393224 | tf_op jit(solution)/shard_map/ppermute | solution.py:364
  27.7 8.7 %collective-permute-start.11 = (bf16[3,128,512]{2,1,0:T(8,128)(2,1)S(1)}, bf16[3,128,512]{2,1,0:T(8,128)(2,1)S(1)}, u32[]{:S(2)}, u32[]{:S(2)}) collective-permute-start(bf16[3,128,512]{2,1,0:T(8,128)(2,1)S(1)} %stack_pieces.1.refs_4_.refs_8_.refs_2_), channel_id=1, source_target_pairs={{0,1},{1,0},{2,3},{3,2},{4,5},{5,4},{6,7},{7,6},{8,9},{9,8},{10,11... | collective-permute-start | bytes 1179656 | tf_op jit(solution)/shard_map/ppermute | solution.py:368
  31.0 9.4 %collective-permute-start.12 = (f32[200,128]{1,0:T(8,128)S(1)}, f32[200,128]{1,0:T(8,128)S(1)}, u32[]{:S(2)}, u32[]{:S(2)}) collective-permute-start(f32[200,128]{1,0:T(8,128)S(1)} %select_add_fusion.1.own_ref), channel_id=1, source_target_pairs={{0,48},{8,56},{16,32},{24,40},{32,16},{40,24},{48,0},{56,8},{64,11... | collective-permute-start | bytes 307208 | tf_op jit(solution)/shard_map/ppermute | solution.py:387
  36.0 6.0 %collective-permute-start.14 = (bf16[128,512]{1,0:T(8,128)(2,1)S(1)}, bf16[128,512]{1,0:T(8,128)(2,1)S(1)}, u32[]{:S(2)}, u32[]{:S(2)}) collective-permute-start(bf16[128,512]{1,0:T(8,128)(2,1)S(1)} %collective-permute-done.13), channel_id=1, source_target_pairs={{0,1},{1,0},{2,3},{3,2},{4,5},{5,4},{6,7},{7,6},{8,9},{9,8},{10,11... | collective-permute-start | bytes 393224 | tf_op jit(solution)/shard_map/ppermute | solution.py:368
  40.4 4.7 %collective-permute-start.15 = (f32[200,128]{1,0:T(8,128)S(1)}, f32[200,128]{1,0:T(8,128)S(1)}, u32[]{:S(2)}, u32[]{:S(2)}) collective-permute-start(f32[200,128]{1,0:T(8,128)S(1)} %select_add_fusion.own_ref), channel_id=1, source_target_pairs={{0,64},{8,72},{16,80},{24,88},{32,96},{40,104},{48,112},{56,120},{... | collective-permute-start | bytes 307208 | tf_op jit(solution)/shard_map/ppermute | solution.py:387
  45.3 5.4 %collective-permute-start.16 = (bf16[192,128]{1,0:T(8,128)(2,1)S(1)}, bf16[192,128]{1,0:T(8,128)(2,1)S(1)}, u32[]{:S(2)}, u32[]{:S(2)}) collective-permute-start(bf16[192,128]{1,0:T(8,128)(2,1)S(1)} %fusion.1.refs_15_), channel_id=1, source_target_pairs={{0,192},{8,200},{16,208},{24,216},{32,224},{40,232},{48,240},{56,2... | collective-permute-start | bytes 147464 | tf_op jit(solution)/shard_map/ppermute | solution.py:387
